TPU v7x, 512 devices: a whole 4x8x8 slice. The times are simulated.
512 devices in a mesh: row: 32 (over x, y_hi, core), col: 16 (over y_lo, z).
Axes of the slice: x: 4, y: 8 (y_hi: 4, y_lo: 2; y = y_hi * 2 + y_lo), z: 8, core: 2. Of those that a mesh axis runs over, the one named last changes fastest.
Arguments:
- activation: bfloat16 [1024, 12288], P('row', 'col'), may hold values from -6 to 6
- upstream: bfloat16 [1024, 49152], P('col', 'row'), may hold values from -0.75 to 0.75
- up_weight: bfloat16 [12288, 49152], P('col', 'row'), may hold values from -0.0546875 to 0.0546875
Outputs:
- act_gradient: bfloat16 [1024, 12288], P('row', 'col')
- weight_gradient: bfloat16 [12288, 49152], P('col', 'row')
All inputs are finite; a program needn't handle non-finite values.
Results may differ from a plain program's by a relative error of at most 0.001.
Values may be sent and summed in bfloat16 or wider, within the bound.
No kernel may reach another device: no remote copies, remote signals or barrier semaphores. Data moves between devices by JAX's collectives and lax.ppermute only.
A program may use at most 64 MiB of HBM per device.

v0:
```python
import jax
import jax.numpy as jnp
from jax import lax
from jax.sharding import PartitionSpec as P


def outer_tokens(left, right):
    return lax.dot_general(
        left, right, (((0,), (0,)), ((), ())), preferred_element_type=jnp.float32
    )


def inner_hidden(rows, weight):
    return lax.dot_general(
        rows, weight, (((1,), (1,)), ((), ())), preferred_element_type=jnp.float32
    )


def on_device(activation, upstream, up_weight):
    grad_rows = lax.all_gather(upstream, "col", axis=0, tiled=True)
    weight_total = outer_tokens(lax.all_gather(activation, "row", axis=0, tiled=True), grad_rows)
    input_total = lax.psum_scatter(
        inner_hidden(grad_rows, up_weight), "row", scatter_dimension=0, tiled=True
    )
    return (input_total.astype(jnp.bfloat16), weight_total.astype(jnp.bfloat16))


def solution(mesh):
    return jax.shard_map(
        on_device,
        mesh=mesh,
        in_specs=(P("row", "col"), P("col", "row"), P("col", "row")),
        out_specs=(P("row", "col"), P("col", "row")),
        check_vma=False,
    )
```

profile of v0, /device:TPU:6, one launch (start us, length us, event | category | flops | bytes accessed | tf_op | source)
XLA Modules:
  0.0 264.5 jit_solution(4822475955505154650)
XLA Ops:
  7.2 0.0 copy-start
  7.2 0.0 all-gather.3.cloned.1.call-start
  7.2 0.7 all-gather.3.cloned.1.call-update
  7.9 0.0 all-gather.5.cloned.1.call-start
  8.0 0.7 all-gather.5.cloned.1.call-update
  8.7 0.0 reduce-scatter.2.cloned.1.call-start
  8.7 83.9 %all-gather.3.cloned.1.call-done = bf16[1024,1536]{1,0:T(8,128)(2,1)} async-done(((bf16[64,1536]{1,0:T(8,128)(2,1)}), bf16[1024,1536]{1,0:T(8,128)(2,1)}) %all-gather.3.cloned.1.call-update) | async-done | bytes 3145744 | tf_op jit(solution)/shard_map/all_gather | solution.py:20
  92.6 0.0 copy-done
  92.6 6.2 %fusion = f32[1024,768]{1,0:T(8,128)} fusion(bf16[1024,1536]{1,0:T(8,128)(2,1)} %all-gather.3.cloned.1.call-done, bf16[768,1536]{1,0:T(8,128)(2,1)S(1)} %copy-done), kind=kOutput, calls=%fused_computation.1 | convolution fusion | flops 2415919104 | bytes 8650752 | tf_op jit(solution)/shard_map/dot_general | solution.py:14
  98.8 0.0 reduce-scatter.2.cloned.1.call-update
  98.9 50.9 %all-gather.5.cloned.1.call-done = bf16[1024,768]{1,0:T(8,128)(2,1)} async-done(((bf16[32,768]{1,0:T(8,128)(2,1)}), bf16[1024,768]{1,0:T(8,128)(2,1)}) %all-gather.5.cloned.1.call-update) | async-done | bytes 1572880 | tf_op jit(solution)/shard_map/all_gather | solution.py:21
  149.8 6.4 %convolution_convert_fusion = bf16[768,1536]{1,0:T(8,128)(2,1)} fusion(bf16[1024,768]{1,0:T(8,128)(2,1)} %all-gather.5.cloned.1.call-done, bf16[1024,1536]{1,0:T(8,128)(2,1)} %all-gather.3.cloned.1.call-done), kind=kOutput, calls=%fused_computation | convolution fusion | flops 2417098752 | bytes 7077888 | tf_op jit(solution)/shard_map/dot_general | solution.py:8
  156.2 100.3 %reduce-scatter.2.cloned.1.call-done = f32[32,768]{1,0:T(8,128)} async-done(((f32[1024,768]{1,0:T(8,128)}), f32[32,768]{1,0:T(8,128)}) %reduce-scatter.2.cloned.1.call-update) | async-done | bytes 98320 | tf_op jit(solution)/shard_map/reduce_scatter | solution.py:22
  256.5 1.5 convert_element_type.6
Async XLA Ops:
  7.2 85.5 %copy-start = (bf16[768,1536]{1,0:T(8,128)(2,1)S(1)}, bf16[768,1536]{1,0:T(8,128)(2,1)}, u32[]{:S(2)}) copy-start(bf16[768,1536]{1,0:T(8,128)(2,1)} %param.5) | copy-start | bytes 7077892
  7.2 85.4 %all-gather.3.cloned.1.call-start = ((), (), s32[]{:S(2)}) async-start(), calls=%async_computation.1 | async-start | bytes 3342336 | tf_op jit(solution)/shard_map/all_gather | solution.py:20
  7.9 141.9 %all-gather.5.cloned.1.call-start = ((), (), s32[]{:S(2)}) async-start(), calls=%async_computation.3 | async-start | bytes 1622016 | tf_op jit(solution)/shard_map/all_gather | solution.py:21
  8.7 247.8 %reduce-scatter.2.cloned.1.call-start = ((), (), s32[]{:S(2)}) async-start(), calls=%async_computation.2 | async-start | bytes 3244032 | tf_op jit(solution)/shard_map/reduce_scatter | solution.py:22
Sparse Core Ops, SparseCore 0:
  10.1 82.4 all-gather.2
  95.8 53.9 all-gather.4
  154.3 102.1 reduce-scatter.1
where the time goes:
time: 265 us
  waiting for transfers between devices  237 us (89%)
  between operations  13.8 us (5%)
  matrix products  12.6 us (5%)
    reduce_scatter x1, waiting for transfers between devices, on_device(): lax.psum_scatter(inner_hidden(grad_rows, up_weight), 'row', scatter_dimen...  100 us
    all_gather x1, waiting for transfers between devices, on_device(): grad_rows = lax.all_gather(upstream, 'col', axis=0, tiled=True)  83.9 us
    all_gather x1, waiting for transfers between devices, on_device(): lax.all_gather(activation, 'row', axis=0, tiled=True)  50.9 us
    dot_general x1, matrix products, outer_tokens(): lax.dot_general(left, right, (((0,), (0,)), ((), ())), preferred_element_...  6.41 us
    dot_general x1, matrix products, inner_hidden(): lax.dot_general(rows, weight, (((1,), (1,)), ((), ())), preferred_element...  6.2 us
  transfers between devices with their start and end apart: 3, of which 3 were waited for; matrix products, arithmetic and copies ran while one was open for 5% of the time, Pallas kernels for 0%

commit v1 on v0

v1 whole, which is shorter than its diff:
```python
import jax
import jax.numpy as jnp
from jax import lax
from jax.experimental import pallas as pl
from jax.experimental.pallas import tpu as pltpu
from jax.sharding import Mesh, PartitionSpec as P

AXES = ("x", "yh", "core", "yl", "z")
ROW = ("x", "yh", "core")
COL = ("yl", "z")


def swap(value, axis):
    return lax.ppermute(value, axis, [(0, 1), (1, 0)])


def partial_kernel(which, grads, weight, out):
    rows = grads[...].reshape(128, 1536)
    out[0] = lax.dot_general(
        rows, weight[...], (((1,), (1,)), ((), ())), preferred_element_type=jnp.float32
    )


def partial_add_kernel(which, grads, weight, other, out):
    rows = grads[...].reshape(128, 1536)
    out[0] = other[0] + lax.dot_general(
        rows, weight[...], (((1,), (1,)), ((), ())), preferred_element_type=jnp.float32
    )


def partial(which, grads, weight, other=None):
    specs = [
        pl.BlockSpec((1, 4, 1, 1, 32, 1536), lambda x, w: (x % 2, 0, x // 2, w[0], 0, 0)),
        pl.BlockSpec((768, 1536), lambda x, w: (0, 0)),
    ]
    block = pl.BlockSpec((1, 128, 768), lambda x, w: (x, 0, 0))
    args = (which, grads, weight)
    if other is not None:
        specs.append(block)
        args += (other,)
    return pl.pallas_call(
        partial_kernel if other is None else partial_add_kernel,
        grid_spec=pltpu.PrefetchScalarGridSpec(
            num_scalar_prefetch=1, grid=(4,), in_specs=specs, out_specs=block
        ),
        out_shape=jax.ShapeDtypeStruct((4, 128, 768), jnp.float32),
        compiler_params=pltpu.CompilerParams(vmem_limit_bytes=32 * 2**20),
        cost_estimate=pl.CostEstimate(
            flops=2 * 512 * 768 * 1536, bytes_accessed=8 * 2**20, transcendentals=0
        ),
    )(*args)


def weight_kernel(act, grads, out, turned):
    @pl.when(pl.program_id(0) == 0)
    def _():
        for core in range(2):
            for yl in range(2):
                turned[core, yl] = act[core, yl].T

    total = jnp.zeros(out.shape, jnp.float32)
    for core in range(2):
        for yl in range(2):
            rows = grads[:, yl, core].reshape(256, out.shape[1])
            total += jnp.dot(turned[core, yl], rows, preferred_element_type=jnp.float32)
    out[...] = total.astype(out.dtype)


def weight_gradient(act, grads):
    wide = 256
    return pl.pallas_call(
        weight_kernel,
        grid=(1536 // wide,),
        in_specs=[
            pl.BlockSpec((2, 2, 256, 768), lambda n: (0, 0, 0, 0)),
            pl.BlockSpec((8, 2, 2, 32, wide), lambda n: (0, 0, 0, 0, n)),
        ],
        out_specs=pl.BlockSpec((768, wide), lambda n: (0, n)),
        out_shape=jax.ShapeDtypeStruct((768, 1536), jnp.bfloat16),
        scratch_shapes=[pltpu.VMEM((2, 2, 768, 256), jnp.bfloat16)],
        compiler_params=pltpu.CompilerParams(vmem_limit_bytes=32 * 2**20),
        cost_estimate=pl.CostEstimate(
            flops=2 * 1024 * 768 * 1536, bytes_accessed=7 * 2**20, transcendentals=0
        ),
    )(act, grads)


def on_device(activation, upstream, up_weight):
    core = lax.axis_index("core").astype(jnp.int32).reshape(1)

    pair = lax.all_gather(upstream, "yl", axis=0, tiled=True)
    grads = lax.all_gather(pair, "z", axis=0, tiled=True)

    act = lax.all_to_all(jnp.tile(activation, (4, 1)), "yh", 0, 0, tiled=True)
    act = lax.all_to_all(jnp.tile(act, (4, 1)), "x", 0, 0, tiled=True)
    sibling = swap(act, "core")
    act = jnp.where(core[0] == 0, jnp.stack([act, sibling]), jnp.stack([sibling, act]))

    blocks = grads.reshape(2, 4, 2, 2, 32, 1536)
    other = swap(partial(1 - core, blocks, up_weight), "core")
    weight_grad = weight_gradient(
        act.reshape(2, 2, 256, 768), grads.reshape(8, 2, 2, 32, 1536)
    )
    total = partial(core, blocks, up_weight, other)
    total = lax.all_to_all(total, "x", 0, 0, tiled=False).sum(0)
    total = lax.all_to_all(total.reshape(4, 32, 768), "yh", 0, 0, tiled=False).sum(0)
    return total.astype(jnp.bfloat16), weight_grad


def solution(mesh):
    fine = Mesh(mesh.devices.reshape(4, 4, 2, 2, 8), AXES)
    return jax.shard_map(
        on_device,
        mesh=fine,
        in_specs=(P(ROW, COL), P(COL, ROW), P(COL, ROW)),
        out_specs=(P(ROW, COL), P(COL, ROW)),
        check_vma=False,
    )
```

time: 265 us -> 161 us (0.61)
  waiting for transfers between devices: 237 us -> 72.6 us
  blocking collectives: 0 us -> 25.6 us
  starting transfers between devices: 0.11 us -> 19.9 us
  Pallas kernels: 0 us -> 14.4 us
  matrix products: 12.6 us -> 0 us
  local copies, waits for them, and re-layouts: 0.01 us -> 7.32 us
  other arithmetic: 1.52 us -> 5.03 us
    reduce_scatter x1 -> x0, waiting for transfers between devices: 100 us -> none  [on_device(): lax.psum_scatter(inner_hidden(grad_rows, up_weight), 'row', scatter_dimen...]
    all_gather x2 -> x1, waiting for transfers between devices: 135 us -> 52.3 us  [on_device(): grads = lax.all_gather(pair, 'z', axis=0, tiled=True)]
    all_to_all x0 -> x3, waiting for transfers between devices: none -> 20.3 us  [the longest x1 14.9 us: on_device(): total = lax.all_to_all(total, 'x', 0, 0, tiled=False).sum(0)]
    all_to_all x0 -> x1, blocking collectives: none -> 16.6 us  [on_device(): act = lax.all_to_all(jnp.tile(activation, (4, 1)), 'yh', 0, 0, tiled=True)]
    all_to_all x0 -> x3, starting transfers between devices: none -> 15.8 us  [the longest x1 6.37 us: on_device(): total = lax.all_to_all(total, 'x', 0, 0, tiled=False).sum(0)]
    pallas_call x0 -> x3, Pallas kernels: none -> 14.4 us  [the longest x2 9.24 us: partial(): pl.pallas_call(partial_kernel if other is None else partial_add_kernel, g...]
    dot_general x2 -> x0, matrix products: 12.6 us -> none  [the longest x1 6.41 us: outer_tokens(): lax.dot_general(left, right, (((0,), (0,)), ((), ())), preferred_element_...]
    all_gather x0 -> x1, blocking collectives: none -> 9.04 us  [on_device(): pair = lax.all_gather(upstream, 'yl', axis=0, tiled=True)]
  transfers between devices with their start and end apart: 3 -> 6, of which waited for: 3 -> 4; matrix products, arithmetic and copies ran while one was open for 5% -> 3% of each run, Pallas kernels for 0% -> 6%
where the time goes in v1:
time: 161 us; the launch traced here: 159 us
  waiting for transfers between devices  72.6 us (45%)
  blocking collectives  25.6 us (16%)
  starting transfers between devices  19.9 us (12%)
  Pallas kernels  14.4 us (9%)
  between operations  14.1 us (9%)
  local copies, waits for them, and re-layouts  7.32 us (5%)
  other arithmetic  5.03 us (3%)
    all_gather x1, waiting for transfers between devices, on_device(): grads = lax.all_gather(pair, 'z', axis=0, tiled=True)  52.3 us
    all_to_all x1, blocking collectives, on_device(): act = lax.all_to_all(jnp.tile(activation, (4, 1)), 'yh', 0, 0, tiled=True)  16.6 us
    all_to_all x1, waiting for transfers between devices, on_device(): total = lax.all_to_all(total, 'x', 0, 0, tiled=False).sum(0)  14.9 us
    pallas_call x2, Pallas kernels, partial(): pl.pallas_call(partial_kernel if other is None else partial_add_kernel, g...  9.24 us
    all_gather x1, blocking collectives, on_device(): pair = lax.all_gather(upstream, 'yl', axis=0, tiled=True)  9.04 us
    all_to_all x1, starting transfers between devices, on_device(): total = lax.all_to_all(total, 'x', 0, 0, tiled=False).sum(0)  6.37 us
    unnamed x12, local copies, waits for them, and re-layouts  6.36 us
    pallas_call x1, Pallas kernels, weight_gradient(): pl.pallas_call(weight_kernel, grid=(1536 // wide,), in_specs=[pl.BlockSpe...  5.19 us
  transfers between devices with their start and end apart: 6, of which 4 were waited for; matrix products, arithmetic and copies ran while one was open for 3% of the time, Pallas kernels for 6%

profile of v1, /device:TPU:6, one launch (start us, length us, event | category | flops | bytes accessed | tf_op | source)
XLA Modules:
  0.0 159.0 jit_solution(13905153251374416261)
XLA Ops:
  7.2 0.0 all-gather.2.cloned.1.call-start
  7.2 9.0 %all_gather.6 = bf16[128,1536]{1,0:T(8,128)(2,1)} all-gather(bf16[64,1536]{1,0:T(8,128)(2,1)} %param.4), channel_id=1, replica_groups=mesh['x'=4,'yh'=4,'core'=2,'yl'=2,'z'=8] {'yl'}, dimensions={0}, use_global_device_ids=true | all-gather | bytes 589824 | tf_op jit(solution)/shard_map/all_gather | solution.py:91
  16.3 0.0 all-gather.2.cloned.1.call-update
  16.3 52.3 %all-gather.2.cloned.1.call-done = bf16[1024,1536]{1,0:T(8,128)(2,1)} async-done(((bf16[128,1536]{1,0:T(8,128)(2,1)}), bf16[1024,1536]{1,0:T(8,128)(2,1)}) %all-gather.2.cloned.1.call-update) | async-done | bytes 3145744 | tf_op jit(solution)/shard_map/all_gather | solution.py:92
  68.5 0.0 copy-start
  68.5 1.9 %copy-done = bf16[1024,1536]{1,0:T(8,128)(2,1)S(1)} copy-done((bf16[1024,1536]{1,0:T(8,128)(2,1)S(1)}, bf16[1024,1536]{1,0:T(8,128)(2,1)}, u32[]{:S(2)}) %copy-start) | copy-done | bytes 3145752
  70.4 0.0 copy-start.2
  70.4 1.7 %copy-done.2 = bf16[768,1536]{1,0:T(8,128)(2,1)S(1)} copy-done((bf16[768,1536]{1,0:T(8,128)(2,1)S(1)}, bf16[768,1536]{1,0:T(8,128)(2,1)}, u32[]{:S(2)}) %copy-start.2) | copy-done | bytes 2359320
  72.1 0.0 copy-start.5
  72.1 4.4 %shard_map.50 = f32[4,128,768]{2,1,0:T(8,128)} custom-call(s32[1]{0:T(128)S(6)} %sub.3.which, bf16[2,4,2,2,32,1536]{5,4,3,2,1,0:T(8,128)(2,1)S(1)} %bitcast.8, bf16[768,1536]{1,0:T(8,128)(2,1)S(1)} %copy-done.2), custom_call_target="tpu_custom_call" | custom-call | flops 1207959552 | bytes 8388608 | tf_op jit(solution)/shard_map/pallas_call | solution.py:41
  76.6 0.0 copy-start.1
  76.6 2.2 %collective-permute-start = (f32[4,128,768]{2,1,0:T(8,128)}, f32[4,128,768]{2,1,0:T(8,128)}, u32[]{:S(2)}, u32[]{:S(2)}) collective-permute-start(f32[4,128,768]{2,1,0:T(8,128)} %shard_map.50), channel_id=1, source_target_pairs={{0,16},{16,0},{1,17},{17,1},{2,18},{18,2},{3,19},{19,3},{4,20},{20... | collective-permute-start | bytes 4718600 | tf_op jit(solution)/shard_map/ppermute | solution.py:14
  78.7 0.0 copy-done.5
  78.8 16.6 %all_to_all.25 = bf16[4,32,768]{2,1,0:T(8,128)(2,1)S(1)} all-to-all(bf16[4,32,768]{2,1,0:T(8,128)(2,1)S(1)} %tile.6), channel_id=1, replica_groups=mesh['x'=4,'yh'=4,'core'=2,'yl'=2,'z'=8] {'yh'}, dimensions={0} | all-to-all | bytes 393216 | tf_op jit(solution)/shard_map/all_to_all | solution.py:94
  95.3 0.9 tile.8
  96.3 4.8 %all-to-all-start.3 = ((bf16[4,128,768]{2,1,0:T(8,128)(2,1)}), bf16[4,128,768]{2,1,0:T(8,128)(2,1)}, u32[]{:S(2)}, u32[]{:S(2)}) async-start(bf16[4,128,768]{2,1,0:T(8,128)(2,1)} %tile.8), calls=%async_computation.3 | async-start | bytes 1572864 | tf_op jit(solution)/shard_map/all_to_all | solution.py:95
  101.1 0.0 collective-permute-done.other
  101.1 0.0 copy-done.1
  101.1 0.0 copy-start.3
  101.1 1.7 %copy-done.3 = bf16[768,1536]{1,0:T(8,128)(2,1)S(1)} copy-done((bf16[768,1536]{1,0:T(8,128)(2,1)S(1)}, bf16[768,1536]{1,0:T(8,128)(2,1)}, u32[]{:S(2)}) %copy-start.3) | copy-done | bytes 2359320
  102.7 4.8 %shard_map.51 = f32[4,128,768]{2,1,0:T(8,128)S(1)} custom-call(s32[1]{0:T(128)} %bitcast.which, bf16[2,4,2,2,32,1536]{5,4,3,2,1,0:T(8,128)(2,1)S(1)} %bitcast.9, bf16[768,1536]{1,0:T(8,128)(2,1)S(1)} %copy-done.3, f32[4,128,768]{2,1,0:T(8,128)} %collective-permute-done.other), custom_call_target="tpu_custom_call" | custom-call | flops 1207959552 | bytes 8388608 | tf_op jit(solution)/shard_map/pallas_call | solution.py:41
  107.5 0.0 copy-start.4
  107.6 1.1 copy-done.4
  108.7 2.0 %all-to-all-done.3 = bf16[4,128,768]{2,1,0:T(8,128)(2,1)} async-done(((bf16[4,128,768]{2,1,0:T(8,128)(2,1)}), bf16[4,128,768]{2,1,0:T(8,128)(2,1)}, u32[]{:S(2)}, u32[]{:S(2)}) %all-to-all-start.3) | async-done | bytes 786464 | tf_op jit(solution)/shard_map/all_to_all | solution.py:95
  110.7 6.4 %all-to-all-start = ((f32[4,128,768]{2,1,0:T(8,128)}), f32[4,128,768]{2,1,0:T(8,128)}, u32[]{:S(2)}, u32[]{:S(2)}) async-start(f32[4,128,768]{2,1,0:T(8,128)} %copy-done.4), calls=%async_computation | async-start | bytes 3145728 | tf_op jit(solution)/shard_map/all_to_all | solution.py:105
  117.0 1.9 %collective-permute-start.1 = (bf16[512,768]{1,0:T(8,128)(2,1)}, bf16[512,768]{1,0:T(8,128)(2,1)}, u32[]{:S(2)}, u32[]{:S(2)}) collective-permute-start(bf16[512,768]{1,0:T(8,128)(2,1)} %bitcast.5), channel_id=1, source_target_pairs={{0,16},{16,0},{1,17},{17,1},{2,18},{18,2},{3,19},{19,3},{4,20},{20... | collective-permute-start | bytes 2359304 | tf_op jit(solution)/shard_map/ppermute | solution.py:14
  118.9 14.9 %all-to-all-done = f32[4,128,768]{2,1,0:T(8,128)} async-done(((f32[4,128,768]{2,1,0:T(8,128)}), f32[4,128,768]{2,1,0:T(8,128)}, u32[]{:S(2)}, u32[]{:S(2)}) %all-to-all-start) | async-done | bytes 1572896 | tf_op jit(solution)/shard_map/all_to_all | solution.py:105
  133.8 2.3 %reduce_sum.18 = f32[128,768]{1,0:T(8,128)} reduce(f32[4,128,768]{2,1,0:T(8,128)} %all-to-all-done, f32[]{:T(128)} %constant.10.clone.1), dimensions={0}, to_apply=%region_0.1 | reduce | flops 294912 | bytes 1966084 | tf_op jit(solution)/shard_map/reduce_sum | solution.py:105
  136.1 4.6 %all-to-all-start.1 = ((f32[4,32,768]{2,1,0:T(8,128)}), f32[4,32,768]{2,1,0:T(8,128)S(1)}, u32[]{:S(2)}, u32[]{:S(2)}) async-start(f32[4,32,768]{2,1,0:T(8,128)} %bitcast.11), calls=%async_computation.1 | async-start | bytes 786432 | tf_op jit(solution)/shard_map/all_to_all | solution.py:106
  140.7 0.0 collective-permute-done.1
  140.7 2.1 %maximum_select_fusion.act = bf16[2,2,256,768]{3,2,1,0:T(8,128)(2,1)S(1)} fusion(bf16[1,2,256,768]{3,2,1,0:T(8,128)(2,1)} %bitcast.6, bf16[1,2,256,768]{3,2,1,0:T(8,128)(2,1)} %bitcast.4, pred[]{:T(512)S(6)} %eq.3), kind=kLoop, calls=%fused_computation | loop fusion | flops 2359296 | bytes 3145729 | tf_op jit(solution)/shard_map/jit(_where)/select_n | solution.py:97
  142.8 5.2 %shard_map.52 = bf16[768,1536]{1,0:T(8,128)(2,1)} custom-call(bf16[2,2,256,768]{3,2,1,0:T(8,128)(2,1)S(1)} %maximum_select_fusion.act, bf16[8,2,2,32,1536]{4,3,2,1,0:T(8,128)(2,1)S(1)} %bitcast.10), custom_call_target="tpu_custom_call" | custom-call | flops 2415919104 | bytes 7340032 | tf_op jit(solution)/shard_map/pallas_call | solution.py:71
  148.0 3.5 %all-to-all-done.1 = f32[4,32,768]{2,1,0:T(8,128)S(1)} async-done(((f32[4,32,768]{2,1,0:T(8,128)}), f32[4,32,768]{2,1,0:T(8,128)S(1)}, u32[]{:S(2)}, u32[]{:S(2)}) %all-to-all-start.1) | async-done | bytes 393248 | tf_op jit(solution)/shard_map/all_to_all | solution.py:106
  151.5 0.6 reduce_sum.19
  (1 shorter events, 0.0 us)
Async XLA Ops:
  7.2 61.4 %all-gather.2.cloned.1.call-start = ((), (), s32[]{:S(2)}) async-start(), calls=%async_computation.4 | async-start | bytes 3538944 | tf_op jit(solution)/shard_map/all_gather | solution.py:92
  68.5 1.9 %copy-start = (bf16[1024,1536]{1,0:T(8,128)(2,1)S(1)}, bf16[1024,1536]{1,0:T(8,128)(2,1)}, u32[]{:S(2)}) copy-start(bf16[1024,1536]{1,0:T(8,128)(2,1)} %all-gather.2.cloned.1.call-done) | copy-start | bytes 9437188
  70.4 1.7 %copy-start.2 = (bf16[768,1536]{1,0:T(8,128)(2,1)S(1)}, bf16[768,1536]{1,0:T(8,128)(2,1)}, u32[]{:S(2)}) copy-start(bf16[768,1536]{1,0:T(8,128)(2,1)} %weight.3) | copy-start | bytes 7077892
  72.1 6.6 %copy-start.5 = (bf16[32,768]{1,0:T(8,128)(2,1)S(1)}, bf16[32,768]{1,0:T(8,128)(2,1)}, u32[]{:S(2)}) copy-start(bf16[32,768]{1,0:T(8,128)(2,1)} %param.3) | copy-start | bytes 147460
  76.6 24.5 %copy-start.1 = (bf16[1024,1536]{1,0:T(8,128)(2,1)S(1)}, bf16[1024,1536]{1,0:T(8,128)(2,1)}, u32[]{:S(2)}) copy-start(bf16[1024,1536]{1,0:T(8,128)(2,1)} %all-gather.2.cloned.1.call-done) | copy-start | bytes 9437188
  76.6 24.5 %collective-permute-start = (f32[4,128,768]{2,1,0:T(8,128)}, f32[4,128,768]{2,1,0:T(8,128)}, u32[]{:S(2)}, u32[]{:S(2)}) collective-permute-start(f32[4,128,768]{2,1,0:T(8,128)} %shard_map.50), channel_id=1, source_target_pairs={{0,16},{16,0},{1,17},{17,1},{2,18},{18,2},{3,19},{19,3},{4,20},{20... | collective-permute-start | bytes 4718600 | tf_op jit(solution)/shard_map/ppermute | solution.py:14
  96.3 14.4 %all-to-all-start.3 = ((bf16[4,128,768]{2,1,0:T(8,128)(2,1)}), bf16[4,128,768]{2,1,0:T(8,128)(2,1)}, u32[]{:S(2)}, u32[]{:S(2)}) async-start(bf16[4,128,768]{2,1,0:T(8,128)(2,1)} %tile.8), calls=%async_computation.3 | async-start | bytes 1572864 | tf_op jit(solution)/shard_map/all_to_all | solution.py:95
  101.1 1.7 %copy-start.3 = (bf16[768,1536]{1,0:T(8,128)(2,1)S(1)}, bf16[768,1536]{1,0:T(8,128)(2,1)}, u32[]{:S(2)}) copy-start(bf16[768,1536]{1,0:T(8,128)(2,1)} %weight.3) | copy-start | bytes 7077892
  107.5 1.1 copy-start.4
  110.7 23.2 %all-to-all-start = ((f32[4,128,768]{2,1,0:T(8,128)}), f32[4,128,768]{2,1,0:T(8,128)}, u32[]{:S(2)}, u32[]{:S(2)}) async-start(f32[4,128,768]{2,1,0:T(8,128)} %copy-done.4), calls=%async_computation | async-start | bytes 3145728 | tf_op jit(solution)/shard_map/all_to_all | solution.py:105
  117.0 23.7 %collective-permute-start.1 = (bf16[512,768]{1,0:T(8,128)(2,1)}, bf16[512,768]{1,0:T(8,128)(2,1)}, u32[]{:S(2)}, u32[]{:S(2)}) collective-permute-start(bf16[512,768]{1,0:T(8,128)(2,1)} %bitcast.5), channel_id=1, source_target_pairs={{0,16},{16,0},{1,17},{17,1},{2,18},{18,2},{3,19},{19,3},{4,20},{20... | collective-permute-start | bytes 2359304 | tf_op jit(solution)/shard_map/ppermute | solution.py:14
  136.1 15.4 %all-to-all-start.1 = ((f32[4,32,768]{2,1,0:T(8,128)}), f32[4,32,768]{2,1,0:T(8,128)S(1)}, u32[]{:S(2)}, u32[]{:S(2)}) async-start(f32[4,32,768]{2,1,0:T(8,128)} %bitcast.11), calls=%async_computation.1 | async-start | bytes 786432 | tf_op jit(solution)/shard_map/all_to_all | solution.py:106
Sparse Core Ops, SparseCore 0:
  16.4 52.1 all-gather.1

commit v2 on v0

v2 whole, which is shorter than its diff:
```python
import jax
import jax.numpy as jnp
from jax import lax
from jax.experimental import pallas as pl
from jax.experimental.pallas import tpu as pltpu
from jax.sharding import Mesh, PartitionSpec as P

AXES = ("x", "yh", "core", "yl", "z")
ROW = ("x", "yh", "core")
COL = ("yl", "z")
SMEM = pl.BlockSpec(memory_space=pltpu.SMEM)
VMEM = pl.BlockSpec(memory_space=pltpu.VMEM)
MIB = 2**20


def swap(value, axis):
    return lax.ppermute(value, axis, [(0, 1), (1, 0)])


def around(value, axis, sign=1):
    pairs = [
        (2 * i + c, 2 * ((i + sign * (1 - 2 * c)) % 4) + c) for i in range(4) for c in range(2)
    ]
    return lax.ppermute(value, (axis, "core"), pairs)


def sums_kernel(place, weight, grads, *outs):
    rows = []
    for i in range(4):
        x = place[1 + i]
        first = 4 * lax.rem(x, 2)
        rows.append(grads[pl.ds(first, 4), x // 2, place[0]].reshape(128, -1))
    product = jnp.dot(
        jnp.concatenate(rows), weight[...], preferred_element_type=jnp.float32
    ).reshape(4, 4, 32, -1)
    if len(outs) == 1:
        outs[0][...] = product
    else:
        for i, out in enumerate(outs):
            out[...] = product[i]


def sums(place, weight, grads, apart):
    part = jax.ShapeDtypeStruct((4, 32, 768), jnp.float32)
    whole = jax.ShapeDtypeStruct((4, 4, 32, 768), jnp.float32)
    return pl.pallas_call(
        sums_kernel,
        in_specs=[SMEM, VMEM, VMEM],
        out_specs=[VMEM] * 4 if apart else VMEM,
        out_shape=[part] * 4 if apart else whole,
        compiler_params=pltpu.CompilerParams(vmem_limit_bytes=12 * MIB),
        cost_estimate=pl.CostEstimate(
            flops=2 * 512 * 768 * 1536, bytes_accessed=6 * MIB, transcendentals=0
        ),
    )(place, weight, grads)


def turn_kernel(place, act, sibling, out):
    for yl in range(2):
        out[place[0], yl] = act[yl].T
        out[1 - place[0], yl] = sibling[yl].T


def turn(place, act, sibling):
    return pl.pallas_call(
        turn_kernel,
        in_specs=[SMEM, VMEM, VMEM],
        out_specs=VMEM,
        out_shape=jax.ShapeDtypeStruct((2, 2, 768, 256), jnp.bfloat16),
        compiler_params=pltpu.CompilerParams(vmem_limit_bytes=12 * MIB),
    )(place, act, sibling)


def weight_kernel(turned, grads, out):
    total = jnp.zeros(out.shape, jnp.float32)
    for core in range(2):
        for yl in range(2):
            rows = grads[:, yl, core].reshape(256, out.shape[1])
            total += jnp.dot(turned[core, yl], rows, preferred_element_type=jnp.float32)
    out[...] = total.astype(out.dtype)


def weight_gradient(turned, grads):
    wide = 512
    return pl.pallas_call(
        weight_kernel,
        grid=(1536 // wide,),
        in_specs=[
            pl.BlockSpec((2, 2, 768, 256), lambda n: (0, 0, 0, 0)),
            pl.BlockSpec((8, 2, 2, 32, wide), lambda n: (0, 0, 0, 0, n)),
        ],
        out_specs=pl.BlockSpec((768, wide), lambda n: (0, n)),
        out_shape=jax.ShapeDtypeStruct((768, 1536), jnp.bfloat16),
        compiler_params=pltpu.CompilerParams(vmem_limit_bytes=20 * MIB),
        cost_estimate=pl.CostEstimate(
            flops=2 * 1024 * 768 * 1536, bytes_accessed=7 * MIB, transcendentals=0
        ),
    )(turned, grads)


def on_device(activation, upstream, up_weight):
    core, x = lax.axis_index("core"), lax.axis_index("x")
    way = 1 - 2 * core

    pair = lax.all_gather(upstream, "yl", axis=0, tiled=True)
    grads = lax.all_gather(pair, "z", axis=0, tiled=True).reshape(8, 2, 2, 32, 1536)

    weight = up_weight.T
    act = lax.all_to_all(jnp.tile(activation, (4, 1)), "yh", 0, 0, tiled=True)
    act = lax.all_to_all(jnp.tile(act, (4, 1)), "x", 0, 0, tiled=True)
    turned = turn(
        core.astype(jnp.int32).reshape(1),
        act.reshape(2, 256, 768),
        swap(act, "core").reshape(2, 256, 768),
    )
    grads, weight, turned = lax.optimization_barrier((grads, weight, turned))

    def work(half, sign):
        steps = [lax.rem(x + sign * step + 4, 4) for step in range(4)]
        return jnp.stack([half, *steps]).astype(jnp.int32)

    other = swap(sums(work(1 - core, -way), weight, grads, False), "core")
    parts = sums(work(core, way), weight, grads, True)
    own, one, two, three = (part + other[i] for i, part in enumerate(parts))
    passed = around(two, "x")
    direct = around(three, "x", -1)
    total = own + direct + around(one + passed, "x")

    weight_grad = weight_gradient(turned, grads)
    total, weight_grad = lax.optimization_barrier((total, weight_grad))
    total = lax.all_to_all(total, "yh", 0, 0).sum(0)
    return total.astype(jnp.bfloat16), weight_grad


def solution(mesh):
    fine = Mesh(mesh.devices.reshape(4, 4, 2, 2, 8), AXES)
    return jax.shard_map(
        on_device,
        mesh=fine,
        in_specs=(P(ROW, COL), P(COL, ROW), P(COL, ROW)),
        out_specs=(P(ROW, COL), P(COL, ROW)),
        check_vma=False,
    )
```

time: 265 us -> 133 us (0.50)
  waiting for transfers between devices: 237 us -> 25.1 us
  blocking collectives: 0 us -> 57.4 us
  matrix products: 12.6 us -> 0 us
  starting transfers between devices: 0.11 us -> 11.6 us
  Pallas kernels: 0 us -> 10.6 us
  local copies, waits for them, and re-layouts: 0.01 us -> 8.85 us
    all_gather x2 -> x1, waiting for transfers between devices: 135 us -> 15.4 us  [on_device(): lax.all_gather(pair, 'z', axis=0, tiled=True).reshape(8, 2, 2, 32, 1536)]
    reduce_scatter x1 -> x0, waiting for transfers between devices: 100 us -> none  [on_device(): lax.psum_scatter(inner_hidden(grad_rows, up_weight), 'row', scatter_dimen...]
    all_to_all x0 -> x3, blocking collectives: none -> 48.4 us  [the longest x1 20.1 us: on_device(): total = lax.all_to_all(total, 'yh', 0, 0).sum(0)]
    dot_general x2 -> x0, matrix products: 12.6 us -> none  [the longest x1 6.41 us: outer_tokens(): lax.dot_general(left, right, (((0,), (0,)), ((), ())), preferred_element_...]
    ppermute x0 -> x5, starting transfers between devices: none -> 11.6 us  [the longest x3 7.76 us: around(): return lax.ppermute(value, (axis, 'core'), pairs)]
    pallas_call x0 -> x4, Pallas kernels: none -> 10.6 us  [the longest x2 4.99 us: sums(): pl.pallas_call(sums_kernel, in_specs=[SMEM, VMEM, VMEM], out_specs=[VMEM]...]
    ppermute x0 -> x5, waiting for transfers between devices: none -> 9.61 us  [the longest x3 9.6 us: around(): return lax.ppermute(value, (axis, 'core'), pairs)]
    all_gather x0 -> x1, blocking collectives: none -> 9.06 us  [on_device(): pair = lax.all_gather(upstream, 'yl', axis=0, tiled=True)]
  transfers between devices with their start and end apart: 3 -> 6, of which waited for: 3 -> 3; matrix products, arithmetic and copies ran while one was open for 5% -> 4% of each run, Pallas kernels for 0% -> 6%
where the time goes in v2:
time: 133 us; the launch traced here: 132 us
  blocking collectives  57.4 us (43%)
  waiting for transfers between devices  25.1 us (19%)
  between operations  14.2 us (11%)
  starting transfers between devices  11.6 us (9%)
  Pallas kernels  10.6 us (8%)
  local copies, waits for them, and re-layouts  8.85 us (7%)
  other arithmetic  4.13 us (3%)
    all_to_all x1, blocking collectives, on_device(): total = lax.all_to_all(total, 'yh', 0, 0).sum(0)  20.1 us
    all_to_all x1, blocking collectives, on_device(): act = lax.all_to_all(jnp.tile(activation, (4, 1)), 'yh', 0, 0, tiled=True)  16 us
    all_gather x1, waiting for transfers between devices, on_device(): lax.all_gather(pair, 'z', axis=0, tiled=True).reshape(8, 2, 2, 32, 1536)  15.4 us
    all_to_all x1, blocking collectives, on_device(): act = lax.all_to_all(jnp.tile(act, (4, 1)), 'x', 0, 0, tiled=True)  12.3 us
    ppermute x3, waiting for transfers between devices, around(): return lax.ppermute(value, (axis, 'core'), pairs)  9.6 us
    all_gather x1, blocking collectives, on_device(): pair = lax.all_gather(upstream, 'yl', axis=0, tiled=True)  9.06 us
    unnamed x11, local copies, waits for them, and re-layouts  7.81 us
    ppermute x3, starting transfers between devices, around(): return lax.ppermute(value, (axis, 'core'), pairs)  7.76 us
  transfers between devices with their start and end apart: 6, of which 3 were waited for; matrix products, arithmetic and copies ran while one was open for 4% of the time, Pallas kernels for 6%

profile of v2, /device:TPU:6, one launch (start us, length us, event | category | flops | bytes accessed | tf_op | source)
XLA Modules:
  0.0 131.9 jit_solution(13772608670980686571)
XLA Ops:
  7.2 0.0 all-gather.2.cloned.1.call-start
  7.2 9.1 %all_gather.6 = bf16[128,1536]{1,0:T(8,128)(2,1)} all-gather(bf16[64,1536]{1,0:T(8,128)(2,1)} %param.4), channel_id=1, replica_groups=mesh['x'=4,'yh'=4,'core'=2,'yl'=2,'z'=8] {'yl'}, dimensions={0}, use_global_device_ids=true | all-gather | bytes 589824 | tf_op jit(solution)/shard_map/all_gather | solution.py:105
  16.3 0.0 all-gather.2.cloned.1.call-update
  16.3 0.8 tile.6
  17.1 16.0 %all_to_all.20 = bf16[4,32,768]{2,1,0:T(8,128)(2,1)S(1)} all-to-all(bf16[4,32,768]{2,1,0:T(8,128)(2,1)S(1)} %tile.6), channel_id=1, replica_groups=mesh['x'=4,'yh'=4,'core'=2,'yl'=2,'z'=8] {'yh'}, dimensions={0} | all-to-all | bytes 393216 | tf_op jit(solution)/shard_map/all_to_all | solution.py:109
  33.1 0.1 tile.8
  33.1 12.3 %all_to_all.21 = bf16[4,128,768]{2,1,0:T(8,128)(2,1)S(1)} all-to-all(bf16[4,128,768]{2,1,0:T(8,128)(2,1)S(1)} %tile.8), channel_id=1, replica_groups=mesh['x'=4,'yh'=4,'core'=2,'yl'=2,'z'=8] {'x'}, dimensions={0} | all-to-all | bytes 1572864 | tf_op jit(solution)/shard_map/all_to_all | solution.py:110
  45.5 1.9 %collective-permute-start = (bf16[512,768]{1,0:T(8,128)(2,1)S(1)}, bf16[512,768]{1,0:T(8,128)(2,1)}, u32[]{:S(2)}, u32[]{:S(2)}) collective-permute-start(bf16[512,768]{1,0:T(8,128)(2,1)S(1)} %bitcast.42), channel_id=1, source_target_pairs={{0,16},{16,0},{1,17},{17,1},{2,18},{18,2},{3,19},{19,3},{4,20},{20... | collective-permute-start | bytes 2359304 | tf_op jit(solution)/shard_map/ppermute | solution.py:17
  47.4 2.9 %copy.5 = bf16[768,1536]{0,1:T(8,128)(2,1)S(1)} copy(bf16[768,1536]{1,0:T(8,128)(2,1)} %param.5) | data formatting | bytes 4718592 | tf_op args[2]
  50.3 0.1 stack.44.place
  50.4 0.0 collective-permute-done
  50.4 1.6 %shard_map.50.turned = bf16[2,2,768,256]{3,2,1,0:T(8,128)(2,1)S(1)} custom-call(s32[1]{0:T(128)} %bitcast.place, bf16[2,256,768]{2,1,0:T(8,128)(2,1)S(1)} %bitcast.43, bf16[2,256,768]{2,1,0:T(8,128)(2,1)} %bitcast.10.sibling), custom_call_target="tpu_custom_call" | custom-call | tf_op jit(solution)/shard_map/pallas_call | solution.py:65
  52.0 0.0 copy-start.3
  52.0 1.2 copy-done.3
  53.1 15.4 %all-gather.2.cloned.1.call-done = bf16[1024,1536]{1,0:T(8,128)(2,1)} async-done(((bf16[128,1536]{1,0:T(8,128)(2,1)}), bf16[1024,1536]{1,0:T(8,128)(2,1)}) %all-gather.2.cloned.1.call-update) | async-done | bytes 3145744 | tf_op jit(solution)/shard_map/all_gather | solution.py:106
  68.6 0.0 copy-start
  68.6 1.9 %copy-done = bf16[1024,1536]{1,0:T(8,128)(2,1)S(1)} copy-done((bf16[1024,1536]{1,0:T(8,128)(2,1)S(1)}, bf16[1024,1536]{1,0:T(8,128)(2,1)}, u32[]{:S(2)}) %copy-start) | copy-done | bytes 3145752
  70.4 3.1 %shard_map.52 = f32[4,4,32,768]{3,2,1,0:T(8,128)} custom-call(s32[5]{0:T(128)S(1)} %stack.44.place, bf16[1536,768]{1,0:T(8,128)(2,1)S(1)} %bitcast.37, bf16[8,2,2,32,1536]{4,3,2,1,0:T(8,128)(2,1)S(1)} %bitcast.39), custom_call_target="tpu_custom_call" | custom-call | flops 1207959552 | bytes 6291456 | tf_op jit(solution)/shard_map/pallas_call | solution.py:46
  73.5 1.9 %collective-permute-start.1 = (f32[4,4,32,768]{3,2,1,0:T(8,128)}, f32[4,4,32,768]{3,2,1,0:T(8,128)}, u32[]{:S(2)}, u32[]{:S(2)}) collective-permute-start(f32[4,4,32,768]{3,2,1,0:T(8,128)} %shard_map.52), channel_id=1, source_target_pairs={{0,16},{16,0},{1,17},{17,1},{2,18},{18,2},{3,19},{19,3},{4,20},{20... | collective-permute-start | bytes 4718600 | tf_op jit(solution)/shard_map/ppermute | solution.py:17
  75.4 0.1 stack.39.place
  75.5 0.0 copy-start.1
  75.5 1.9 %copy-done.1 = bf16[1024,1536]{1,0:T(8,128)(2,1)S(1)} copy-done((bf16[1024,1536]{1,0:T(8,128)(2,1)S(1)}, bf16[1024,1536]{1,0:T(8,128)(2,1)}, u32[]{:S(2)}) %copy-start.1) | copy-done | bytes 3145752
  77.4 0.0 copy-start.4
  77.4 1.9 %shard_map.51 = (f32[4,32,768]{2,1,0:T(8,128)S(1)}, f32[4,32,768]{2,1,0:T(8,128)S(1)}, f32[4,32,768]{2,1,0:T(8,128)S(1)}, f32[4,32,768]{2,1,0:T(8,128)S(1)}) custom-call(s32[5]{0:T(128)S(1)} %stack.39.place, bf16[1536,768]{1,0:T(8,128)(2,1)S(1)} %bitcast.38, bf16[8,2,2,32,1536]{4,3,2,1,0:T(8,128)(2,1)S(1)} %bitcast.40), custom_call_target="tpu_custom_call" | custom-call | flops 1207959552 | bytes 6291456 | tf_op jit(solution)/shard_map/pallas_call | solution.py:46
  79.3 0.0 collective-permute-done.1
  79.4 0.0 copy-start.2
  79.4 1.4 %fusion.3 = (f32[4,32,768]{2,1,0:T(8,128)S(1)}, f32[4,32,768]{2,1,0:T(8,128)S(1)}) fusion(f32[4,32,768]{2,1,0:T(8,128)S(1)} %get-tuple-element.14, f32[4,4,32,768]{3,2,1,0:T(8,128)} %collective-permute-done.1, f32[4,32,768]{2,1,0:T(8,128)S(1)} %get-tuple-element.16), kind=kLoop, calls=%fused_computation.6 | loop fusion | flops 196608 | bytes 2359296 | tf_op jit(solution)/shard_map/add | solution.py:124
  80.7 2.5 %collective-permute-start.3 = (f32[4,32,768]{2,1,0:T(8,128)S(1)}, f32[4,32,768]{2,1,0:T(8,128)S(1)}, u32[]{:S(2)}, u32[]{:S(2)}) collective-permute-start(f32[4,32,768]{2,1,0:T(8,128)S(1)} %get-tuple-element.21), channel_id=1, source_target_pairs={{0,128},{16,400},{128,256},{144,16},{256,384},{272,144},{384,0},{4... | collective-permute-start | bytes 1179656 | tf_op jit(solution)/shard_map/ppermute | solution.py:24
  83.2 3.4 %collective-permute-start.2 = (f32[4,32,768]{2,1,0:T(8,128)S(1)}, f32[4,32,768]{2,1,0:T(8,128)S(1)}, u32[]{:S(2)}, u32[]{:S(2)}) collective-permute-start(f32[4,32,768]{2,1,0:T(8,128)S(1)} %get-tuple-element.20), channel_id=1, source_target_pairs={{0,384},{16,144},{128,0},{144,272},{256,128},{272,400},{384,256},{... | collective-permute-start | bytes 1179656 | tf_op jit(solution)/shard_map/ppermute | solution.py:24
  86.6 5.9 %collective-permute-done.3 = f32[4,32,768]{2,1,0:T(8,128)S(1)} collective-permute-done((f32[4,32,768]{2,1,0:T(8,128)S(1)}, f32[4,32,768]{2,1,0:T(8,128)S(1)}, u32[]{:S(2)}, u32[]{:S(2)}) %collective-permute-start.3) | collective-permute-done | bytes 393248 | tf_op jit(solution)/shard_map/ppermute | solution.py:24
  92.5 1.1 fusion.2
  93.6 1.9 %collective-permute-start.4 = (f32[4,32,768]{2,1,0:T(8,128)S(1)}, f32[4,32,768]{2,1,0:T(8,128)S(1)}, u32[]{:S(2)}, u32[]{:S(2)}) collective-permute-start(f32[4,32,768]{2,1,0:T(8,128)S(1)} %fusion.2), channel_id=1, source_target_pairs={{0,128},{16,400},{128,256},{144,16},{256,384},{272,144},{384,0},{4... | collective-permute-start | bytes 1179656 | tf_op jit(solution)/shard_map/ppermute | solution.py:24
  95.5 0.0 copy-done.4
  95.5 0.0 copy-done.2
  95.5 4.1 %shard_map.53 = bf16[768,1536]{1,0:T(8,128)(2,1)} custom-call(bf16[2,2,768,256]{3,2,1,0:T(8,128)(2,1)S(1)} %copy-done.4, bf16[8,2,2,32,1536]{4,3,2,1,0:T(8,128)(2,1)S(1)} %bitcast.41), custom_call_target="tpu_custom_call" | custom-call | flops 2415919104 | bytes 7340032 | tf_op jit(solution)/shard_map/pallas_call | solution.py:85
  99.6 0.0 collective-permute-done.2
  99.6 3.7 %collective-permute-done.4 = f32[4,32,768]{2,1,0:T(8,128)S(1)} collective-permute-done((f32[4,32,768]{2,1,0:T(8,128)S(1)}, f32[4,32,768]{2,1,0:T(8,128)S(1)}, u32[]{:S(2)}, u32[]{:S(2)}) %collective-permute-start.4) | collective-permute-done | bytes 393248 | tf_op jit(solution)/shard_map/ppermute | solution.py:24
  103.3 1.1 fusion.6
  104.3 20.1 %all_to_all.22 = f32[4,32,768]{2,1,0:T(8,128)S(1)} all-to-all(f32[4,32,768]{2,1,0:T(8,128)S(1)} %fusion.6), channel_id=1, replica_groups=mesh['x'=4,'yh'=4,'core'=2,'yl'=2,'z'=8] {'yh'}, dimensions={0} | all-to-all | bytes 786432 | tf_op jit(solution)/shard_map/all_to_all | solution.py:131
  124.4 0.6 reduce_sum.9
Async XLA Ops:
  7.2 61.4 %all-gather.2.cloned.1.call-start = ((), (), s32[]{:S(2)}) async-start(), calls=%async_computation.3 | async-start | bytes 3538944 | tf_op jit(solution)/shard_map/all_gather | solution.py:106
  45.5 4.9 %collective-permute-start = (bf16[512,768]{1,0:T(8,128)(2,1)S(1)}, bf16[512,768]{1,0:T(8,128)(2,1)}, u32[]{:S(2)}, u32[]{:S(2)}) collective-permute-start(bf16[512,768]{1,0:T(8,128)(2,1)S(1)} %bitcast.42), channel_id=1, source_target_pairs={{0,16},{16,0},{1,17},{17,1},{2,18},{18,2},{3,19},{19,3},{4,20},{20... | collective-permute-start | bytes 2359304 | tf_op jit(solution)/shard_map/ppermute | solution.py:17
  52.0 1.2 copy-start.3
  68.6 1.9 %copy-start = (bf16[1024,1536]{1,0:T(8,128)(2,1)S(1)}, bf16[1024,1536]{1,0:T(8,128)(2,1)}, u32[]{:S(2)}) copy-start(bf16[1024,1536]{1,0:T(8,128)(2,1)} %all-gather.2.cloned.1.call-done) | copy-start | bytes 9437188
  73.5 5.8 %collective-permute-start.1 = (f32[4,4,32,768]{3,2,1,0:T(8,128)}, f32[4,4,32,768]{3,2,1,0:T(8,128)}, u32[]{:S(2)}, u32[]{:S(2)}) collective-permute-start(f32[4,4,32,768]{3,2,1,0:T(8,128)} %shard_map.52), channel_id=1, source_target_pairs={{0,16},{16,0},{1,17},{17,1},{2,18},{18,2},{3,19},{19,3},{4,20},{20... | collective-permute-start | bytes 4718600 | tf_op jit(solution)/shard_map/ppermute | solution.py:17
  75.5 1.9 %copy-start.1 = (bf16[1024,1536]{1,0:T(8,128)(2,1)S(1)}, bf16[1024,1536]{1,0:T(8,128)(2,1)}, u32[]{:S(2)}) copy-start(bf16[1024,1536]{1,0:T(8,128)(2,1)} %all-gather.2.cloned.1.call-done) | copy-start | bytes 9437188
  77.4 18.1 %copy-start.4 = (bf16[2,2,768,256]{3,2,1,0:T(8,128)(2,1)S(1)}, bf16[2,2,768,256]{3,2,1,0:T(8,128)(2,1)}, u32[]{:S(2)}) copy-start(bf16[2,2,768,256]{3,2,1,0:T(8,128)(2,1)} %copy-done.3) | copy-start | bytes 4718596
  79.4 16.2 %copy-start.2 = (bf16[1024,1536]{1,0:T(8,128)(2,1)S(1)}, bf16[1024,1536]{1,0:T(8,128)(2,1)}, u32[]{:S(2)}) copy-start(bf16[1024,1536]{1,0:T(8,128)(2,1)} %all-gather.2.cloned.1.call-done) | copy-start | bytes 9437188
  80.7 11.8 %collective-permute-start.3 = (f32[4,32,768]{2,1,0:T(8,128)S(1)}, f32[4,32,768]{2,1,0:T(8,128)S(1)}, u32[]{:S(2)}, u32[]{:S(2)}) collective-permute-start(f32[4,32,768]{2,1,0:T(8,128)S(1)} %get-tuple-element.21), channel_id=1, source_target_pairs={{0,128},{16,400},{128,256},{144,16},{256,384},{272,144},{384,0},{4... | collective-permute-start | bytes 1179656 | tf_op jit(solution)/shard_map/ppermute | solution.py:24
  83.2 16.4 %collective-permute-start.2 = (f32[4,32,768]{2,1,0:T(8,128)S(1)}, f32[4,32,768]{2,1,0:T(8,128)S(1)}, u32[]{:S(2)}, u32[]{:S(2)}) collective-permute-start(f32[4,32,768]{2,1,0:T(8,128)S(1)} %get-tuple-element.20), channel_id=1, source_target_pairs={{0,384},{16,144},{128,0},{144,272},{256,128},{272,400},{384,256},{... | collective-permute-start | bytes 1179656 | tf_op jit(solution)/shard_map/ppermute | solution.py:24
  93.6 9.7 %collective-permute-start.4 = (f32[4,32,768]{2,1,0:T(8,128)S(1)}, f32[4,32,768]{2,1,0:T(8,128)S(1)}, u32[]{:S(2)}, u32[]{:S(2)}) collective-permute-start(f32[4,32,768]{2,1,0:T(8,128)S(1)} %fusion.2), channel_id=1, source_target_pairs={{0,128},{16,400},{128,256},{144,16},{256,384},{272,144},{384,0},{4... | collective-permute-start | bytes 1179656 | tf_op jit(solution)/shard_map/ppermute | solution.py:24
Sparse Core Ops, SparseCore 0:
  16.4 52.1 all-gather.1

commit v3 on v2

v3 whole, which is shorter than its diff:
```python
import functools

import jax
import jax.numpy as jnp
from jax import lax
from jax.experimental import pallas as pl
from jax.experimental.pallas import tpu as pltpu
from jax.sharding import Mesh, PartitionSpec as P

AXES = ("x", "yh", "core", "yl", "z")
ROW = ("x", "yh", "core")
COL = ("yl", "z")
SMEM = pl.BlockSpec(memory_space=pltpu.SMEM)
VMEM = pl.BlockSpec(memory_space=pltpu.VMEM)
MIB = 2**20
HOPS = (0, 1, 2, 3, 4, -1, -2, -3)


def swap(value, axis):
    return lax.ppermute(value, axis, [(0, 1), (1, 0)])


def around(value, axis="z", sign=1):
    n = 8 if axis == "z" else 4
    pairs = []
    for c in range(2):
        for i in range(n):
            j = (i + sign * (1 - 2 * c)) % n
            pairs.append((c * n + i, c * n + j))
    if axis == "z":
        return lax.ppermute(value, ("core", "z"), pairs)
    pairs = [(2 * (i % n) + i // n, 2 * (j % n) + j // n) for i, j in pairs]
    return lax.ppermute(value, (axis, "core"), pairs)


def origin(place, hops):
    return lax.rem(place[1] + (2 * place[0] - 1) * hops + 8, 8)


def sums_kernel(far, place, weight, *refs):
    held, out = refs[:-1], refs[-1]
    half = 1 - place[0] if far else place[0]
    rows = jnp.concatenate([h[:, half].reshape(64, -1) for h in held])
    product = jnp.dot(rows, weight[...], preferred_element_type=jnp.float32)
    for i, hops in enumerate(HOPS):
        z = origin(place, hops)
        for yl in range(2):
            at = 64 * i + 32 * yl
            step = lax.rem((1 - 2 * half) * (2 * yl + z // 4 - place[2]) + 4, 4)
            out[step, lax.rem(z, 4)] = product[at : at + 32]


def sums(far, place, weight, held):
    return pl.pallas_call(
        functools.partial(sums_kernel, far),
        in_specs=[SMEM] + [VMEM] * (1 + len(held)),
        out_specs=VMEM,
        out_shape=jax.ShapeDtypeStruct((4, 4, 32, 768), jnp.float32),
        compiler_params=pltpu.CompilerParams(vmem_limit_bytes=12 * MIB),
        cost_estimate=pl.CostEstimate(
            flops=2 * 512 * 768 * 1536, bytes_accessed=8 * MIB, transcendentals=0
        ),
    )(place, weight, *held)


def flip_kernel(weight, out):
    out[...] = weight[...].T


def flip(weight):
    return pl.pallas_call(
        flip_kernel,
        in_specs=[VMEM],
        out_specs=VMEM,
        out_shape=jax.ShapeDtypeStruct((1536, 768), jnp.bfloat16),
        compiler_params=pltpu.CompilerParams(vmem_limit_bytes=12 * MIB),
        cost_estimate=pl.CostEstimate(flops=0, bytes_accessed=5 * MIB, transcendentals=0),
    )(weight)


def turn_kernel(place, act, sibling, out):
    for yl in range(2):
        out[place[0], yl] = act[yl].T
        out[1 - place[0], yl] = sibling[yl].T


def turn(place, act, sibling):
    return pl.pallas_call(
        turn_kernel,
        in_specs=[SMEM, VMEM, VMEM],
        out_specs=VMEM,
        out_shape=jax.ShapeDtypeStruct((2, 2, 768, 256), jnp.bfloat16),
        compiler_params=pltpu.CompilerParams(vmem_limit_bytes=12 * MIB),
    )(place, act, sibling)


def weight_kernel(place, turned, *refs):
    held, (out, ordered) = refs[: len(HOPS)], refs[len(HOPS) :]
    for block, hops in zip(held, HOPS):
        ordered[origin(place, hops)] = block[...]
    total = jnp.zeros(out.shape, jnp.float32)
    for core in range(2):
        for yl in range(2):
            rows = ordered[:, yl, core].reshape(256, out.shape[1])
            total += jnp.dot(turned[core, yl], rows, preferred_element_type=jnp.float32)
    out[...] = total.astype(out.dtype)


def weight_gradient(place, turned, held):
    wide = 512
    return pl.pallas_call(
        weight_kernel,
        grid=(1536 // wide,),
        in_specs=[SMEM, pl.BlockSpec((2, 2, 768, 256), lambda n: (0, 0, 0, 0))]
        + [pl.BlockSpec((2, 2, 32, wide), lambda n: (0, 0, 0, n))] * len(HOPS),
        out_specs=pl.BlockSpec((768, wide), lambda n: (0, n)),
        out_shape=jax.ShapeDtypeStruct((768, 1536), jnp.bfloat16),
        scratch_shapes=[pltpu.VMEM((8, 2, 2, 32, wide), jnp.bfloat16)],
        compiler_params=pltpu.CompilerParams(vmem_limit_bytes=20 * MIB),
        cost_estimate=pl.CostEstimate(
            flops=2 * 1024 * 768 * 1536, bytes_accessed=7 * MIB, transcendentals=0
        ),
    )(place, turned, *held)


def on_device(activation, upstream, up_weight):
    place = jnp.stack([lax.axis_index(name) for name in ("core", "z", "x")]).astype(jnp.int32)
    upstream, place = lax.optimization_barrier((upstream, place))
    weight = flip(up_weight)

    act = lax.all_to_all(jnp.tile(activation, (16, 1)), ("x", "yh"), 0, 0, tiled=True)
    mine = [lax.all_gather(upstream, "yl", axis=0, tiled=True).reshape(2, 2, 32, 1536)]
    other = [swap(mine[0], "core")]
    for step in range(3):
        mine.append(around(mine[-1]))
        other.append(around(other[-1]))
    mine[2], weight = lax.optimization_barrier((mine[2], weight))
    mine[3] = around(mine[2])
    side = swap(other[1], "core")
    mine[3], side = lax.optimization_barrier((mine[3], side))
    mine.append(around(mine[3]))
    sides = [side, swap(other[2], "core"), swap(other[3], "core")]
    *held, act = lax.optimization_barrier((*mine, *sides, act))

    theirs = swap(sums(True, place, weight, held), "core")
    ours = sums(False, place, weight, held)
    own, one, two, three = (ours[i] + theirs[i] for i in range(4))
    passed = around(two, "x")
    direct = around(three, "x", -1)
    total = own + direct + around(one + passed, "x")

    turned = turn(place, act.reshape(2, 256, 768), swap(act, "core").reshape(2, 256, 768))
    weight_grad = weight_gradient(place, turned, held)
    total, weight_grad = lax.optimization_barrier((total, weight_grad))
    total = lax.all_to_all(total, "yh", 0, 0).sum(0)
    return total.astype(jnp.bfloat16), weight_grad


def solution(mesh):
    fine = Mesh(mesh.devices.reshape(4, 4, 2, 2, 8), AXES)
    return jax.shard_map(
        on_device,
        mesh=fine,
        in_specs=(P(ROW, COL), P(COL, ROW), P(COL, ROW)),
        out_specs=(P(ROW, COL), P(COL, ROW)),
        check_vma=False,
    )
```

time: 133 us -> 118 us (0.89)
  starting transfers between devices: 11.6 us -> 59.1 us
  blocking collectives: 57.4 us -> 27.4 us
  waiting for transfers between devices: 25.1 us -> 8.07 us
  between operations: 14.2 us -> 0.89 us
  other arithmetic: 4.13 us -> 0.95 us
  Pallas kernels: 10.6 us -> 13 us
  local copies, waits for them, and re-layouts: 8.85 us -> 7.01 us
    all_to_all x2 -> x0, blocking collectives: 28.3 us -> none  [the longest x1 16 us: on_device(): act = lax.all_to_all(jnp.tile(activation, (4, 1)), 'yh', 0, 0, tiled=True)]
    ppermute x0 -> x7, starting transfers between devices: none -> 27.2 us  [around(): return lax.ppermute(value, ('core', 'z'), pairs)]
    all_gather x1 -> x0, waiting for transfers between devices: 15.4 us -> none  [on_device(): lax.all_gather(pair, 'z', axis=0, tiled=True).reshape(8, 2, 2, 32, 1536)]
    ppermute x2 -> x6, starting transfers between devices: 3.82 us -> 13.9 us  [swap(): return lax.ppermute(value, axis, [(0, 1), (1, 0)])]
    all_to_all x0 -> x1, starting transfers between devices: none -> 10.1 us  [on_device(): lax.all_to_all(jnp.tile(activation, (16, 1)), ('x', 'yh'), 0, 0, tiled=True)]
    ppermute x3, waiting for transfers between devices: 9.6 us -> 2.51 us  [around(): return lax.ppermute(value, (axis, 'core'), pairs)]
    ppermute x0 -> x7, waiting for transfers between devices: none -> 5.04 us  [around(): return lax.ppermute(value, ('core', 'z'), pairs)]
    pallas_call x3 -> x4, Pallas kernels: 9.05 us -> 12 us  [the longest x2 5.72 us: sums(): pl.pallas_call(functools.partial(sums_kernel, far), in_specs=[SMEM] + [VM...]
  transfers between devices with their start and end apart: 6 -> 17, of which waited for: 3 -> 7; matrix products, arithmetic and copies ran while one was open for 4% -> 2% of each run, Pallas kernels for 6% -> 9%
where the time goes in v3:
time: 118 us; the launch traced here: 116 us
  starting transfers between devices  59.1 us (50%)
  blocking collectives  27.4 us (23%)
  Pallas kernels  13 us (11%)
  waiting for transfers between devices  8.07 us (7%)
  local copies, waits for them, and re-layouts  7.01 us (6%)
    ppermute x7, starting transfers between devices, around(): return lax.ppermute(value, ('core', 'z'), pairs)  27.2 us
    all_to_all x1, blocking collectives, on_device(): total = lax.all_to_all(total, 'yh', 0, 0).sum(0)  19.8 us
    ppermute x6, starting transfers between devices, swap(): return lax.ppermute(value, axis, [(0, 1), (1, 0)])  13.9 us
    all_to_all x1, starting transfers between devices, on_device(): lax.all_to_all(jnp.tile(activation, (16, 1)), ('x', 'yh'), 0, 0, tiled=True)  10.1 us
    ppermute x3, starting transfers between devices, around(): return lax.ppermute(value, (axis, 'core'), pairs)  7.98 us
    all_gather x1, blocking collectives, on_device(): lax.all_gather(upstream, 'yl', axis=0, tiled=True).reshape(2, 2, 32, 1536)  7.52 us
    pallas_call x2, Pallas kernels, sums(): pl.pallas_call(functools.partial(sums_kernel, far), in_specs=[SMEM] + [VM...  5.72 us
    pallas_call x1, Pallas kernels, weight_gradient(): pl.pallas_call(weight_kernel, grid=(1536 // wide,), in_specs=[SMEM, pl.Bl...  5.64 us
  transfers between devices with their start and end apart: 17, of which 7 were waited for; matrix products, arithmetic and copies ran while one was open for 2% of the time, Pallas kernels for 9%

profile of v3, /device:TPU:6, one launch (start us, length us, event | category | flops | bytes accessed | tf_op | source)
XLA Modules:
  0.0 116.4 jit_solution(3307305533956117471)
XLA Ops:
  0.6 0.1 pad_add_fusion.place
  0.7 7.5 %all_gather.3 = bf16[128,1536]{1,0:T(8,128)(2,1)S(1)} all-gather(bf16[64,1536]{1,0:T(8,128)(2,1)} %param.4), channel_id=1, replica_groups=mesh['x'=4,'yh'=4,'core'=2,'yl'=2,'z'=8] {'yl'}, dimensions={0}, use_global_device_ids=true | all-gather | bytes 589824 | tf_op jit(solution)/shard_map/all_gather | solution.py:132
  8.2 1.9 %collective-permute-start.3 = (bf16[2,2,32,1536]{3,2,1,0:T(8,128)(2,1)S(1)}, bf16[2,2,32,1536]{3,2,1,0:T(8,128)(2,1)S(1)}, u32[]{:S(2)}, u32[]{:S(2)}) collective-permute-start(bf16[2,2,32,1536]{3,2,1,0:T(8,128)(2,1)S(1)} %bitcast.21), channel_id=1, source_target_pairs={{0,16},{16,0},{1,17},{17,1},{2,18},{18,2},{3,19},{19,3},{4,20},{20... | collective-permute-start | bytes 1179656 | tf_op jit(solution)/shard_map/ppermute | solution.py:20
  10.1 4.3 %collective-permute-start = (bf16[2,2,32,1536]{3,2,1,0:T(8,128)(2,1)S(1)}, bf16[2,2,32,1536]{3,2,1,0:T(8,128)(2,1)}, u32[]{:S(2)}, u32[]{:S(2)}) collective-permute-start(bf16[2,2,32,1536]{3,2,1,0:T(8,128)(2,1)S(1)} %bitcast.22), channel_id=1, source_target_pairs={{0,1},{1,2},{2,3},{3,4},{4,5},{5,6},{6,7},{7,0},{16,23},{17,16},{1... | collective-permute-start | bytes 1179656 | tf_op jit(solution)/shard_map/ppermute | solution.py:31
  14.4 4.3 %collective-permute-start.4 = (bf16[2,2,32,1536]{3,2,1,0:T(8,128)(2,1)S(1)}, bf16[2,2,32,1536]{3,2,1,0:T(8,128)(2,1)}, u32[]{:S(2)}, u32[]{:S(2)}) collective-permute-start(bf16[2,2,32,1536]{3,2,1,0:T(8,128)(2,1)S(1)} %collective-permute-done.3), channel_id=1, source_target_pairs={{0,1},{1,2},{2,3},{3,4},{4,5},{5,6},{6,7},{7,0},{16,23},{17,16},{1... | collective-permute-start | bytes 1179656 | tf_op jit(solution)/shard_map/ppermute | solution.py:31
  18.7 1.8 %tile.2 = bf16[16,32,768]{2,1,0:T(8,128)(2,1)} broadcast(bf16[32,768]{1,0:T(8,128)(2,1)} %param.3), dimensions={1,2} | broadcast | bytes 835584 | tf_op jit(solution)/shard_map/tile | solution.py:131
  20.5 10.1 %all-to-all-start = ((bf16[16,32,768]{2,1,0:T(8,128)(2,1)}), bf16[16,32,768]{2,1,0:T(8,128)(2,1)S(1)}, u32[]{:S(2)}, u32[]{:S(2)}) async-start(bf16[16,32,768]{2,1,0:T(8,128)(2,1)} %tile.2), calls=%async_computation | async-start | bytes 1572864 | tf_op jit(solution)/shard_map/all_to_all | solution.py:131
  30.6 0.0 collective-permute-done.refs_1_
  30.6 4.3 %collective-permute-start.1 = (bf16[2,2,32,1536]{3,2,1,0:T(8,128)(2,1)}, bf16[2,2,32,1536]{3,2,1,0:T(8,128)(2,1)S(1)}, u32[]{:S(2)}, u32[]{:S(2)}) collective-permute-start(bf16[2,2,32,1536]{3,2,1,0:T(8,128)(2,1)} %collective-permute-done.refs_1_), channel_id=1, source_target_pairs={{0,1},{1,2},{2,3},{3,4},{4,5},{5,6},{6,7},{7,0},{16,23},{17,16},{1... | collective-permute-start | bytes 1179656 | tf_op jit(solution)/shard_map/ppermute | solution.py:31
  34.8 0.0 collective-permute-done.4
  34.9 5.5 %collective-permute-start.7 = (bf16[2,2,32,1536]{3,2,1,0:T(8,128)(2,1)}, bf16[2,2,32,1536]{3,2,1,0:T(8,128)(2,1)}, u32[]{:S(2)}, u32[]{:S(2)}) collective-permute-start(bf16[2,2,32,1536]{3,2,1,0:T(8,128)(2,1)} %collective-permute-done.4), channel_id=1, source_target_pairs={{0,1},{1,2},{2,3},{3,4},{4,5},{5,6},{6,7},{7,0},{16,23},{17,16},{1... | collective-permute-start | bytes 1179656 | tf_op jit(solution)/shard_map/ppermute | solution.py:31
  40.4 0.0 copy-start
  40.4 1.7 %copy-done = bf16[768,1536]{1,0:T(8,128)(2,1)S(1)} copy-done((bf16[768,1536]{1,0:T(8,128)(2,1)S(1)}, bf16[768,1536]{1,0:T(8,128)(2,1)}, u32[]{:S(2)}) %copy-start) | copy-done | bytes 2359320
  42.0 0.7 shard_map.50.weight
  42.7 0.1 collective-permute-done.1.refs_2_
  42.8 3.3 %collective-permute-start.2 = (bf16[2,2,32,1536]{3,2,1,0:T(8,128)(2,1)S(1)}, bf16[2,2,32,1536]{3,2,1,0:T(8,128)(2,1)}, u32[]{:S(2)}, u32[]{:S(2)}) collective-permute-start(bf16[2,2,32,1536]{3,2,1,0:T(8,128)(2,1)S(1)} %collective-permute-done.1.refs_2_), channel_id=1, source_target_pairs={{0,1},{1,2},{2,3},{3,4},{4,5},{5,6},{6,7},{7,0},{16,23},{17,16},{1... | collective-permute-start | bytes 1179656 | tf_op jit(solution)/shard_map/ppermute | solution.py:31
  46.1 0.8 copy-done.1
  46.9 3.0 %collective-permute-start.5 = (bf16[2,2,32,1536]{3,2,1,0:T(8,128)(2,1)}, bf16[2,2,32,1536]{3,2,1,0:T(8,128)(2,1)S(1)}, u32[]{:S(2)}, u32[]{:S(2)}) collective-permute-start(bf16[2,2,32,1536]{3,2,1,0:T(8,128)(2,1)} %collective-permute-done.4), channel_id=1, source_target_pairs={{0,16},{16,0},{1,17},{17,1},{2,18},{18,2},{3,19},{19,3},{4,20},{20... | collective-permute-start | bytes 1179656 | tf_op jit(solution)/shard_map/ppermute | solution.py:20
  49.9 0.0 collective-permute-done.7
  49.9 3.0 %collective-permute-start.9 = (bf16[2,2,32,1536]{3,2,1,0:T(8,128)(2,1)}, bf16[2,2,32,1536]{3,2,1,0:T(8,128)(2,1)}, u32[]{:S(2)}, u32[]{:S(2)}) collective-permute-start(bf16[2,2,32,1536]{3,2,1,0:T(8,128)(2,1)} %collective-permute-done.7), channel_id=1, source_target_pairs={{0,1},{1,2},{2,3},{3,4},{4,5},{5,6},{6,7},{7,0},{16,23},{17,16},{1... | collective-permute-start | bytes 1179656 | tf_op jit(solution)/shard_map/ppermute | solution.py:31
  52.9 0.9 collective-permute-done.2.refs_3_
  53.8 0.0 collective-permute-done.5.refs_5_
  53.8 0.7 copy-done.4
  54.5 2.5 %collective-permute-start.6 = (bf16[2,2,32,1536]{3,2,1,0:T(8,128)(2,1)}, bf16[2,2,32,1536]{3,2,1,0:T(8,128)(2,1)}, u32[]{:S(2)}, u32[]{:S(2)}) collective-permute-start(bf16[2,2,32,1536]{3,2,1,0:T(8,128)(2,1)} %collective-permute-done.2.refs_3_), channel_id=1, source_target_pairs={{0,1},{1,2},{2,3},{3,4},{4,5},{5,6},{6,7},{7,0},{16,23},{17,16},{1... | collective-permute-start | bytes 1179656 | tf_op jit(solution)/shard_map/ppermute | solution.py:31
  57.1 2.7 %collective-permute-start.8 = (bf16[2,2,32,1536]{3,2,1,0:T(8,128)(2,1)}, bf16[2,2,32,1536]{3,2,1,0:T(8,128)(2,1)}, u32[]{:S(2)}, u32[]{:S(2)}) collective-permute-start(bf16[2,2,32,1536]{3,2,1,0:T(8,128)(2,1)} %collective-permute-done.7), channel_id=1, source_target_pairs={{0,16},{16,0},{1,17},{17,1},{2,18},{18,2},{3,19},{19,3},{4,20},{20... | collective-permute-start | bytes 1179656 | tf_op jit(solution)/shard_map/ppermute | solution.py:20
  59.7 1.4 %collective-permute-done.9 = bf16[2,2,32,1536]{3,2,1,0:T(8,128)(2,1)} collective-permute-done((bf16[2,2,32,1536]{3,2,1,0:T(8,128)(2,1)}, bf16[2,2,32,1536]{3,2,1,0:T(8,128)(2,1)}, u32[]{:S(2)}, u32[]{:S(2)}) %collective-permute-start.9) | collective-permute-done | bytes 393248 | tf_op jit(solution)/shard_map/ppermute | solution.py:31
  61.1 1.9 %collective-permute-start.10 = (bf16[2,2,32,1536]{3,2,1,0:T(8,128)(2,1)}, bf16[2,2,32,1536]{3,2,1,0:T(8,128)(2,1)}, u32[]{:S(2)}, u32[]{:S(2)}) collective-permute-start(bf16[2,2,32,1536]{3,2,1,0:T(8,128)(2,1)} %collective-permute-done.9), channel_id=1, source_target_pairs={{0,16},{16,0},{1,17},{17,1},{2,18},{18,2},{3,19},{19,3},{4,20},{20... | collective-permute-start | bytes 1179656 | tf_op jit(solution)/shard_map/ppermute | solution.py:20
  63.0 2.7 %collective-permute-done.6.refs_4_ = bf16[2,2,32,1536]{3,2,1,0:T(8,128)(2,1)} collective-permute-done((bf16[2,2,32,1536]{3,2,1,0:T(8,128)(2,1)}, bf16[2,2,32,1536]{3,2,1,0:T(8,128)(2,1)}, u32[]{:S(2)}, u32[]{:S(2)}) %collective-permute-start.6) | collective-permute-done | bytes 393248 | tf_op jit(solution)/shard_map/ppermute | solution.py:31
  65.7 1.0 copy-done.2
  66.7 1.0 copy-done.5
  67.7 2.9 %shard_map.52 = f32[4,4,32,768]{3,2,1,0:T(8,128)S(1)} custom-call(s32[3]{0:T(128)S(1)} %pad_add_fusion.place, bf16[1536,768]{1,0:T(8,128)(2,1)S(1)} %shard_map.50.weight, bf16[2,2,32,1536]{3,2,1,0:T(8,128)(2,1)S(1)} %bitcast.23, bf16[2,2,32,1536]{3,2,1,0:T(8,128)(2,1)} %collective-permute-done.refs_1_, bf16[2,2,32,1536]{3,2,1,0:T(8,128)(2,1)S(1)} %copy-done.2, ...), custom_call_target="tpu_custom_call" | custom-call | flops 1207959552 | bytes 8388608 | tf_op jit(solution)/shard_map/pallas_call | solution.py:54
  70.6 1.9 %collective-permute-start.11 = (f32[4,4,32,768]{3,2,1,0:T(8,128)S(1)}, f32[4,4,32,768]{3,2,1,0:T(8,128)S(1)}, u32[]{:S(2)}, u32[]{:S(2)}) collective-permute-start(f32[4,4,32,768]{3,2,1,0:T(8,128)S(1)} %shard_map.52), channel_id=1, source_target_pairs={{0,16},{16,0},{1,17},{17,1},{2,18},{18,2},{3,19},{19,3},{4,20},{20... | collective-permute-start | bytes 4718600 | tf_op jit(solution)/shard_map/ppermute | solution.py:20
  72.5 2.9 %shard_map.51 = f32[4,4,32,768]{3,2,1,0:T(8,128)S(1)} custom-call(s32[3]{0:T(128)S(1)} %pad_add_fusion.place, bf16[1536,768]{1,0:T(8,128)(2,1)S(1)} %shard_map.50.weight, bf16[2,2,32,1536]{3,2,1,0:T(8,128)(2,1)S(1)} %bitcast.24, bf16[2,2,32,1536]{3,2,1,0:T(8,128)(2,1)} %collective-permute-done.refs_1_, bf16[2,2,32,1536]{3,2,1,0:T(8,128)(2,1)S(1)} %copy-done.2, ...), custom_call_target="tpu_custom_call" | custom-call | flops 1207959552 | bytes 8388608 | tf_op jit(solution)/shard_map/pallas_call | solution.py:54
  75.4 0.5 collective-permute-done.11
  75.9 0.1 fusion.3
  76.0 2.0 %collective-permute-start.13 = (f32[4,32,768]{2,1,0:T(8,128)S(1)}, f32[4,32,768]{2,1,0:T(8,128)S(1)}, u32[]{:S(2)}, u32[]{:S(2)}) collective-permute-start(f32[4,32,768]{2,1,0:T(8,128)S(1)} %get-tuple-element.37), channel_id=1, source_target_pairs={{0,128},{128,256},{256,384},{384,0},{16,400},{144,16},{272,144},{4... | collective-permute-start | bytes 1179656 | tf_op jit(solution)/shard_map/ppermute | solution.py:33
  78.0 2.5 %collective-permute-start.15 = (bf16[512,768]{1,0:T(8,128)(2,1)S(1)}, bf16[512,768]{1,0:T(8,128)(2,1)S(1)}, u32[]{:S(2)}, u32[]{:S(2)}) collective-permute-start(bf16[512,768]{1,0:T(8,128)(2,1)S(1)} %bitcast.26), channel_id=1, source_target_pairs={{0,16},{16,0},{1,17},{17,1},{2,18},{18,2},{3,19},{19,3},{4,20},{20... | collective-permute-start | bytes 2359304 | tf_op jit(solution)/shard_map/ppermute | solution.py:20
  80.5 3.2 %collective-permute-start.12 = (f32[4,32,768]{2,1,0:T(8,128)S(1)}, f32[4,32,768]{2,1,0:T(8,128)S(1)}, u32[]{:S(2)}, u32[]{:S(2)}) collective-permute-start(f32[4,32,768]{2,1,0:T(8,128)S(1)} %get-tuple-element.36), channel_id=1, source_target_pairs={{0,384},{128,0},{256,128},{384,256},{16,144},{144,272},{272,400},{... | collective-permute-start | bytes 1179656 | tf_op jit(solution)/shard_map/ppermute | solution.py:33
  83.8 2.4 %collective-permute-done.13 = f32[4,32,768]{2,1,0:T(8,128)S(1)} collective-permute-done((f32[4,32,768]{2,1,0:T(8,128)S(1)}, f32[4,32,768]{2,1,0:T(8,128)S(1)}, u32[]{:S(2)}, u32[]{:S(2)}) %collective-permute-start.13) | collective-permute-done | bytes 393248 | tf_op jit(solution)/shard_map/ppermute | solution.py:33
  86.1 0.1 fusion.2
  86.2 2.7 %collective-permute-start.14 = (f32[4,32,768]{2,1,0:T(8,128)S(1)}, f32[4,32,768]{2,1,0:T(8,128)S(1)}, u32[]{:S(2)}, u32[]{:S(2)}) collective-permute-start(f32[4,32,768]{2,1,0:T(8,128)S(1)} %fusion.2), channel_id=1, source_target_pairs={{0,128},{128,256},{256,384},{384,0},{16,400},{144,16},{272,144},{4... | collective-permute-start | bytes 1179656 | tf_op jit(solution)/shard_map/ppermute | solution.py:33
  89.0 1.0 shard_map.53.turned
  90.0 0.1 copy-done.6
  90.1 5.6 %shard_map.54 = bf16[768,1536]{1,0:T(8,128)(2,1)} custom-call(s32[3]{0:T(128)S(1)} %pad_add_fusion.place, bf16[2,2,768,256]{3,2,1,0:T(8,128)(2,1)S(1)} %shard_map.53.turned, bf16[2,2,32,1536]{3,2,1,0:T(8,128)(2,1)S(1)} %bitcast.25, bf16[2,2,32,1536]{3,2,1,0:T(8,128)(2,1)} %collective-permute-done.refs_1_, bf16[2,2,32,1536]{3,2,1,0:T(8,128)(2,1)S(1)} %copy-done.3, ...), custom_call_target="tpu_custom_call" | custom-call | flops 2415919104 | bytes 7340032 | tf_op jit(solution)/shard_map/pallas_call | solution.py:111
  95.7 0.1 collective-permute-done.14
  95.9 0.1 fusion.6
  95.9 19.8 %all_to_all.14 = f32[4,32,768]{2,1,0:T(8,128)S(1)} all-to-all(f32[4,32,768]{2,1,0:T(8,128)S(1)} %fusion.6), channel_id=1, replica_groups=mesh['x'=4,'yh'=4,'core'=2,'yl'=2,'z'=8] {'yh'}, dimensions={0} | all-to-all | bytes 786432 | tf_op jit(solution)/shard_map/all_to_all | solution.py:155
  115.8 0.6 reduce_sum.9
  (13 shorter events, 0.0 us)
Async XLA Ops:
  8.2 6.2 %collective-permute-start.3 = (bf16[2,2,32,1536]{3,2,1,0:T(8,128)(2,1)S(1)}, bf16[2,2,32,1536]{3,2,1,0:T(8,128)(2,1)S(1)}, u32[]{:S(2)}, u32[]{:S(2)}) collective-permute-start(bf16[2,2,32,1536]{3,2,1,0:T(8,128)(2,1)S(1)} %bitcast.21), channel_id=1, source_target_pairs={{0,16},{16,0},{1,17},{17,1},{2,18},{18,2},{3,19},{19,3},{4,20},{20... | collective-permute-start | bytes 1179656 | tf_op jit(solution)/shard_map/ppermute | solution.py:20
  10.1 20.4 %collective-permute-start = (bf16[2,2,32,1536]{3,2,1,0:T(8,128)(2,1)S(1)}, bf16[2,2,32,1536]{3,2,1,0:T(8,128)(2,1)}, u32[]{:S(2)}, u32[]{:S(2)}) collective-permute-start(bf16[2,2,32,1536]{3,2,1,0:T(8,128)(2,1)S(1)} %bitcast.22), channel_id=1, source_target_pairs={{0,1},{1,2},{2,3},{3,4},{4,5},{5,6},{6,7},{7,0},{16,23},{17,16},{1... | collective-permute-start | bytes 1179656 | tf_op jit(solution)/shard_map/ppermute | solution.py:31
  14.4 20.4 %collective-permute-start.4 = (bf16[2,2,32,1536]{3,2,1,0:T(8,128)(2,1)S(1)}, bf16[2,2,32,1536]{3,2,1,0:T(8,128)(2,1)}, u32[]{:S(2)}, u32[]{:S(2)}) collective-permute-start(bf16[2,2,32,1536]{3,2,1,0:T(8,128)(2,1)S(1)} %collective-permute-done.3), channel_id=1, source_target_pairs={{0,1},{1,2},{2,3},{3,4},{4,5},{5,6},{6,7},{7,0},{16,23},{17,16},{1... | collective-permute-start | bytes 1179656 | tf_op jit(solution)/shard_map/ppermute | solution.py:31
  20.5 42.5 %all-to-all-start = ((bf16[16,32,768]{2,1,0:T(8,128)(2,1)}), bf16[16,32,768]{2,1,0:T(8,128)(2,1)S(1)}, u32[]{:S(2)}, u32[]{:S(2)}) async-start(bf16[16,32,768]{2,1,0:T(8,128)(2,1)} %tile.2), calls=%async_computation | async-start | bytes 1572864 | tf_op jit(solution)/shard_map/all_to_all | solution.py:131
  30.6 12.2 %collective-permute-start.1 = (bf16[2,2,32,1536]{3,2,1,0:T(8,128)(2,1)}, bf16[2,2,32,1536]{3,2,1,0:T(8,128)(2,1)S(1)}, u32[]{:S(2)}, u32[]{:S(2)}) collective-permute-start(bf16[2,2,32,1536]{3,2,1,0:T(8,128)(2,1)} %collective-permute-done.refs_1_), channel_id=1, source_target_pairs={{0,1},{1,2},{2,3},{3,4},{4,5},{5,6},{6,7},{7,0},{16,23},{17,16},{1... | collective-permute-start | bytes 1179656 | tf_op jit(solution)/shard_map/ppermute | solution.py:31
  34.9 15.0 %collective-permute-start.7 = (bf16[2,2,32,1536]{3,2,1,0:T(8,128)(2,1)}, bf16[2,2,32,1536]{3,2,1,0:T(8,128)(2,1)}, u32[]{:S(2)}, u32[]{:S(2)}) collective-permute-start(bf16[2,2,32,1536]{3,2,1,0:T(8,128)(2,1)} %collective-permute-done.4), channel_id=1, source_target_pairs={{0,1},{1,2},{2,3},{3,4},{4,5},{5,6},{6,7},{7,0},{16,23},{17,16},{1... | collective-permute-start | bytes 1179656 | tf_op jit(solution)/shard_map/ppermute | solution.py:31
  40.4 1.7 %copy-start = (bf16[768,1536]{1,0:T(8,128)(2,1)S(1)}, bf16[768,1536]{1,0:T(8,128)(2,1)}, u32[]{:S(2)}) copy-start(bf16[768,1536]{1,0:T(8,128)(2,1)} %weight.1) | copy-start | bytes 7077892
  42.8 11.0 %collective-permute-start.2 = (bf16[2,2,32,1536]{3,2,1,0:T(8,128)(2,1)S(1)}, bf16[2,2,32,1536]{3,2,1,0:T(8,128)(2,1)}, u32[]{:S(2)}, u32[]{:S(2)}) collective-permute-start(bf16[2,2,32,1536]{3,2,1,0:T(8,128)(2,1)S(1)} %collective-permute-done.1.refs_2_), channel_id=1, source_target_pairs={{0,1},{1,2},{2,3},{3,4},{4,5},{5,6},{6,7},{7,0},{16,23},{17,16},{1... | collective-permute-start | bytes 1179656 | tf_op jit(solution)/shard_map/ppermute | solution.py:31
  46.1 0.8 copy-start.1
  46.9 6.9 %collective-permute-start.5 = (bf16[2,2,32,1536]{3,2,1,0:T(8,128)(2,1)}, bf16[2,2,32,1536]{3,2,1,0:T(8,128)(2,1)S(1)}, u32[]{:S(2)}, u32[]{:S(2)}) collective-permute-start(bf16[2,2,32,1536]{3,2,1,0:T(8,128)(2,1)} %collective-permute-done.4), channel_id=1, source_target_pairs={{0,16},{16,0},{1,17},{17,1},{2,18},{18,2},{3,19},{19,3},{4,20},{20... | collective-permute-start | bytes 1179656 | tf_op jit(solution)/shard_map/ppermute | solution.py:20
  49.9 11.2 %collective-permute-start.9 = (bf16[2,2,32,1536]{3,2,1,0:T(8,128)(2,1)}, bf16[2,2,32,1536]{3,2,1,0:T(8,128)(2,1)}, u32[]{:S(2)}, u32[]{:S(2)}) collective-permute-start(bf16[2,2,32,1536]{3,2,1,0:T(8,128)(2,1)} %collective-permute-done.7), channel_id=1, source_target_pairs={{0,1},{1,2},{2,3},{3,4},{4,5},{5,6},{6,7},{7,0},{16,23},{17,16},{1... | collective-permute-start | bytes 1179656 | tf_op jit(solution)/shard_map/ppermute | solution.py:31
  53.8 0.7 copy-start.4
  54.5 11.2 %collective-permute-start.6 = (bf16[2,2,32,1536]{3,2,1,0:T(8,128)(2,1)}, bf16[2,2,32,1536]{3,2,1,0:T(8,128)(2,1)}, u32[]{:S(2)}, u32[]{:S(2)}) collective-permute-start(bf16[2,2,32,1536]{3,2,1,0:T(8,128)(2,1)} %collective-permute-done.2.refs_3_), channel_id=1, source_target_pairs={{0,1},{1,2},{2,3},{3,4},{4,5},{5,6},{6,7},{7,0},{16,23},{17,16},{1... | collective-permute-start | bytes 1179656 | tf_op jit(solution)/shard_map/ppermute | solution.py:31
  57.1 8.7 %collective-permute-start.8 = (bf16[2,2,32,1536]{3,2,1,0:T(8,128)(2,1)}, bf16[2,2,32,1536]{3,2,1,0:T(8,128)(2,1)}, u32[]{:S(2)}, u32[]{:S(2)}) collective-permute-start(bf16[2,2,32,1536]{3,2,1,0:T(8,128)(2,1)} %collective-permute-done.7), channel_id=1, source_target_pairs={{0,16},{16,0},{1,17},{17,1},{2,18},{18,2},{3,19},{19,3},{4,20},{20... | collective-permute-start | bytes 1179656 | tf_op jit(solution)/shard_map/ppermute | solution.py:20
  61.1 4.6 %collective-permute-start.10 = (bf16[2,2,32,1536]{3,2,1,0:T(8,128)(2,1)}, bf16[2,2,32,1536]{3,2,1,0:T(8,128)(2,1)}, u32[]{:S(2)}, u32[]{:S(2)}) collective-permute-start(bf16[2,2,32,1536]{3,2,1,0:T(8,128)(2,1)} %collective-permute-done.9), channel_id=1, source_target_pairs={{0,16},{16,0},{1,17},{17,1},{2,18},{18,2},{3,19},{19,3},{4,20},{20... | collective-permute-start | bytes 1179656 | tf_op jit(solution)/shard_map/ppermute | solution.py:20
  65.7 1.0 copy-start.2
  66.7 1.0 copy-start.5
  70.6 5.3 %collective-permute-start.11 = (f32[4,4,32,768]{3,2,1,0:T(8,128)S(1)}, f32[4,4,32,768]{3,2,1,0:T(8,128)S(1)}, u32[]{:S(2)}, u32[]{:S(2)}) collective-permute-start(f32[4,4,32,768]{3,2,1,0:T(8,128)S(1)} %shard_map.52), channel_id=1, source_target_pairs={{0,16},{16,0},{1,17},{17,1},{2,18},{18,2},{3,19},{19,3},{4,20},{20... | collective-permute-start | bytes 4718600 | tf_op jit(solution)/shard_map/ppermute | solution.py:20
  76.0 10.1 %collective-permute-start.13 = (f32[4,32,768]{2,1,0:T(8,128)S(1)}, f32[4,32,768]{2,1,0:T(8,128)S(1)}, u32[]{:S(2)}, u32[]{:S(2)}) collective-permute-start(f32[4,32,768]{2,1,0:T(8,128)S(1)} %get-tuple-element.37), channel_id=1, source_target_pairs={{0,128},{128,256},{256,384},{384,0},{16,400},{144,16},{272,144},{4... | collective-permute-start | bytes 1179656 | tf_op jit(solution)/shard_map/ppermute | solution.py:33
  78.0 10.9 %collective-permute-start.15 = (bf16[512,768]{1,0:T(8,128)(2,1)S(1)}, bf16[512,768]{1,0:T(8,128)(2,1)S(1)}, u32[]{:S(2)}, u32[]{:S(2)}) collective-permute-start(bf16[512,768]{1,0:T(8,128)(2,1)S(1)} %bitcast.26), channel_id=1, source_target_pairs={{0,16},{16,0},{1,17},{17,1},{2,18},{18,2},{3,19},{19,3},{4,20},{20... | collective-permute-start | bytes 2359304 | tf_op jit(solution)/shard_map/ppermute | solution.py:20
  80.5 15.2 %collective-permute-start.12 = (f32[4,32,768]{2,1,0:T(8,128)S(1)}, f32[4,32,768]{2,1,0:T(8,128)S(1)}, u32[]{:S(2)}, u32[]{:S(2)}) collective-permute-start(f32[4,32,768]{2,1,0:T(8,128)S(1)} %get-tuple-element.36), channel_id=1, source_target_pairs={{0,384},{128,0},{256,128},{384,256},{16,144},{144,272},{272,400},{... | collective-permute-start | bytes 1179656 | tf_op jit(solution)/shard_map/ppermute | solution.py:33
  86.2 9.7 %collective-permute-start.14 = (f32[4,32,768]{2,1,0:T(8,128)S(1)}, f32[4,32,768]{2,1,0:T(8,128)S(1)}, u32[]{:S(2)}, u32[]{:S(2)}) collective-permute-start(f32[4,32,768]{2,1,0:T(8,128)S(1)} %fusion.2), channel_id=1, source_target_pairs={{0,128},{128,256},{256,384},{384,0},{16,400},{144,16},{272,144},{4... | collective-permute-start | bytes 1179656 | tf_op jit(solution)/shard_map/ppermute | solution.py:33
  89.0 1.0 copy-start.3
  89.0 1.1 copy-start.6

commit v4 on v3

--- a/solution.py
+++ b/solution.py
@@ -79,9 +79,10 @@
 
 
 def turn_kernel(place, act, sibling, out):
-    for yl in range(2):
-        out[place[0], yl] = act[yl].T
-        out[1 - place[0], yl] = sibling[yl].T
+    for core, rows in ((place[0], act), (1 - place[0], sibling)):
+        for yl in range(2):
+            blocks = [rows[8 * yl + origin(place, hops)] for hops in HOPS]
+            out[core, yl] = jnp.concatenate(blocks).T
 
 
 def turn(place, act, sibling):
@@ -91,36 +92,34 @@
         out_specs=VMEM,
         out_shape=jax.ShapeDtypeStruct((2, 2, 768, 256), jnp.bfloat16),
         compiler_params=pltpu.CompilerParams(vmem_limit_bytes=12 * MIB),
+        cost_estimate=pl.CostEstimate(flops=0, bytes_accessed=5 * MIB, transcendentals=0),
     )(place, act, sibling)
 
 
-def weight_kernel(place, turned, *refs):
-    held, (out, ordered) = refs[: len(HOPS)], refs[len(HOPS) :]
-    for block, hops in zip(held, HOPS):
-        ordered[origin(place, hops)] = block[...]
+def weight_kernel(turned, *refs):
+    held, out = refs[:-1], refs[-1]
     total = jnp.zeros(out.shape, jnp.float32)
     for core in range(2):
         for yl in range(2):
-            rows = ordered[:, yl, core].reshape(256, out.shape[1])
+            rows = jnp.concatenate([block[yl, core] for block in held])
             total += jnp.dot(turned[core, yl], rows, preferred_element_type=jnp.float32)
     out[...] = total.astype(out.dtype)
 
 
-def weight_gradient(place, turned, held):
+def weight_gradient(turned, held):
     wide = 512
     return pl.pallas_call(
         weight_kernel,
         grid=(1536 // wide,),
-        in_specs=[SMEM, pl.BlockSpec((2, 2, 768, 256), lambda n: (0, 0, 0, 0))]
+        in_specs=[pl.BlockSpec((2, 2, 768, 256), lambda n: (0, 0, 0, 0))]
         + [pl.BlockSpec((2, 2, 32, wide), lambda n: (0, 0, 0, n))] * len(HOPS),
         out_specs=pl.BlockSpec((768, wide), lambda n: (0, n)),
         out_shape=jax.ShapeDtypeStruct((768, 1536), jnp.bfloat16),
-        scratch_shapes=[pltpu.VMEM((8, 2, 2, 32, wide), jnp.bfloat16)],
         compiler_params=pltpu.CompilerParams(vmem_limit_bytes=20 * MIB),
         cost_estimate=pl.CostEstimate(
             flops=2 * 1024 * 768 * 1536, bytes_accessed=7 * MIB, transcendentals=0
         ),
-    )(place, turned, *held)
+    )(turned, *held)
 
 
 def on_device(activation, upstream, up_weight):
@@ -141,6 +140,8 @@
     mine.append(around(mine[3]))
     sides = [side, swap(other[2], "core"), swap(other[3], "core")]
     *held, act = lax.optimization_barrier((*mine, *sides, act))
+    held = [pltpu.with_memory_space_constraint(block, pltpu.HBM) for block in held]
+    act = act.reshape(16, 32, 768)
 
     theirs = swap(sums(True, place, weight, held), "core")
     ours = sums(False, place, weight, held)
@@ -149,8 +150,7 @@
     direct = around(three, "x", -1)
     total = own + direct + around(one + passed, "x")
 
-    turned = turn(place, act.reshape(2, 256, 768), swap(act, "core").reshape(2, 256, 768))
-    weight_grad = weight_gradient(place, turned, held)
+    weight_grad = weight_gradient(turn(place, act, swap(act, "core")), held)
     total, weight_grad = lax.optimization_barrier((total, weight_grad))
     total = lax.all_to_all(total, "yh", 0, 0).sum(0)
     return total.astype(jnp.bfloat16), weight_grad

time: 118 us -> 115 us (0.975)
  local copies, waits for them, and re-layouts: 7.01 us -> 3.44 us
    unnamed x14 -> x10, local copies, waits for them, and re-layouts: 5.25 us -> 1.68 us
  transfers between devices with their start and end apart: 17 -> 17, of which waited for: 7 -> 6; matrix products, arithmetic and copies ran while one was open for 2% -> 2% of each run, Pallas kernels for 9% -> 9%
where the time goes in v4:
time: 115 us; the launch traced here: 114 us
  starting transfers between devices  59.5 us (52%)
  blocking collectives  27.6 us (24%)
  Pallas kernels  13.8 us (12%)
  waiting for transfers between devices  7.75 us (7%)
  local copies, waits for them, and re-layouts  3.44 us (3%)
    ppermute x7, starting transfers between devices, around(): return lax.ppermute(value, ('core', 'z'), pairs)  26.7 us
    all_to_all x1, blocking collectives, on_device(): total = lax.all_to_all(total, 'yh', 0, 0).sum(0)  20.1 us
    ppermute x6, starting transfers between devices, swap(): return lax.ppermute(value, axis, [(0, 1), (1, 0)])  14.5 us
    all_to_all x1, starting transfers between devices, on_device(): lax.all_to_all(jnp.tile(activation, (16, 1)), ('x', 'yh'), 0, 0, tiled=True)  10.1 us
    ppermute x3, starting transfers between devices, around(): return lax.ppermute(value, (axis, 'core'), pairs)  8.21 us
    all_gather x1, blocking collectives, on_device(): lax.all_gather(upstream, 'yl', axis=0, tiled=True).reshape(2, 2, 32, 1536)  7.52 us
    pallas_call x2, Pallas kernels, sums(): pl.pallas_call(functools.partial(sums_kernel, far), in_specs=[SMEM] + [VM...  6.44 us
    pallas_call x1, Pallas kernels, weight_gradient(): pl.pallas_call(weight_kernel, grid=(1536 // wide,), in_specs=[pl.BlockSpe...  5.72 us
  transfers between devices with their start and end apart: 17, of which 6 were waited for; matrix products, arithmetic and copies ran while one was open for 2% of the time, Pallas kernels for 9%

profile of v4, /device:TPU:6, one launch (start us, length us, event | category | flops | bytes accessed | tf_op | source)
XLA Modules:
  0.0 114.0 jit_solution(7869032059642123515)
XLA Ops:
  0.6 0.1 pad_add_fusion.place
  0.7 7.5 %all_gather.3 = bf16[128,1536]{1,0:T(8,128)(2,1)S(1)} all-gather(bf16[64,1536]{1,0:T(8,128)(2,1)} %param.4), channel_id=1, replica_groups=mesh['x'=4,'yh'=4,'core'=2,'yl'=2,'z'=8] {'yl'}, dimensions={0}, use_global_device_ids=true | all-gather | bytes 589824 | tf_op jit(solution)/shard_map/all_gather | solution.py:131
  8.2 1.9 %collective-permute-start.3 = (bf16[2,2,32,1536]{3,2,1,0:T(8,128)(2,1)S(1)}, bf16[2,2,32,1536]{3,2,1,0:T(8,128)(2,1)S(1)}, u32[]{:S(2)}, u32[]{:S(2)}) collective-permute-start(bf16[2,2,32,1536]{3,2,1,0:T(8,128)(2,1)S(1)} %bitcast.20), channel_id=1, source_target_pairs={{0,16},{16,0},{1,17},{17,1},{2,18},{18,2},{3,19},{19,3},{4,20},{20... | collective-permute-start | bytes 1179656 | tf_op jit(solution)/shard_map/ppermute | solution.py:20
  10.2 4.3 %collective-permute-start = (bf16[2,2,32,1536]{3,2,1,0:T(8,128)(2,1)S(1)}, bf16[2,2,32,1536]{3,2,1,0:T(8,128)(2,1)}, u32[]{:S(2)}, u32[]{:S(2)}) collective-permute-start(bf16[2,2,32,1536]{3,2,1,0:T(8,128)(2,1)S(1)} %bitcast.21), channel_id=1, source_target_pairs={{0,1},{1,2},{2,3},{3,4},{4,5},{5,6},{6,7},{7,0},{16,23},{17,16},{1... | collective-permute-start | bytes 1179656 | tf_op jit(solution)/shard_map/ppermute | solution.py:31
  14.4 0.0 collective-permute-done.3
  14.4 4.3 %collective-permute-start.4 = (bf16[2,2,32,1536]{3,2,1,0:T(8,128)(2,1)S(1)}, bf16[2,2,32,1536]{3,2,1,0:T(8,128)(2,1)}, u32[]{:S(2)}, u32[]{:S(2)}) collective-permute-start(bf16[2,2,32,1536]{3,2,1,0:T(8,128)(2,1)S(1)} %collective-permute-done.3), channel_id=1, source_target_pairs={{0,1},{1,2},{2,3},{3,4},{4,5},{5,6},{6,7},{7,0},{16,23},{17,16},{1... | collective-permute-start | bytes 1179656 | tf_op jit(solution)/shard_map/ppermute | solution.py:31
  18.7 1.8 %tile.2 = bf16[16,32,768]{2,1,0:T(8,128)(2,1)} broadcast(bf16[32,768]{1,0:T(8,128)(2,1)} %param.3), dimensions={1,2} | broadcast | bytes 835584 | tf_op jit(solution)/shard_map/tile | solution.py:130
  20.5 10.1 %all-to-all-start = ((bf16[16,32,768]{2,1,0:T(8,128)(2,1)}), bf16[16,32,768]{2,1,0:T(8,128)(2,1)S(1)}, u32[]{:S(2)}, u32[]{:S(2)}) async-start(bf16[16,32,768]{2,1,0:T(8,128)(2,1)} %tile.2), calls=%async_computation | async-start | bytes 1572864 | tf_op jit(solution)/shard_map/all_to_all | solution.py:130
  30.6 0.0 collective-permute-done.refs_1_
  30.6 4.3 %collective-permute-start.1 = (bf16[2,2,32,1536]{3,2,1,0:T(8,128)(2,1)}, bf16[2,2,32,1536]{3,2,1,0:T(8,128)(2,1)S(1)}, u32[]{:S(2)}, u32[]{:S(2)}) collective-permute-start(bf16[2,2,32,1536]{3,2,1,0:T(8,128)(2,1)} %collective-permute-done.refs_1_), channel_id=1, source_target_pairs={{0,1},{1,2},{2,3},{3,4},{4,5},{5,6},{6,7},{7,0},{16,23},{17,16},{1... | collective-permute-start | bytes 1179656 | tf_op jit(solution)/shard_map/ppermute | solution.py:31
  34.9 0.0 collective-permute-done.4
  34.9 5.5 %collective-permute-start.7 = (bf16[2,2,32,1536]{3,2,1,0:T(8,128)(2,1)}, bf16[2,2,32,1536]{3,2,1,0:T(8,128)(2,1)}, u32[]{:S(2)}, u32[]{:S(2)}) collective-permute-start(bf16[2,2,32,1536]{3,2,1,0:T(8,128)(2,1)} %collective-permute-done.4), channel_id=1, source_target_pairs={{0,1},{1,2},{2,3},{3,4},{4,5},{5,6},{6,7},{7,0},{16,23},{17,16},{1... | collective-permute-start | bytes 1179656 | tf_op jit(solution)/shard_map/ppermute | solution.py:31
  40.4 0.0 copy-start
  40.4 1.7 %copy-done = bf16[768,1536]{1,0:T(8,128)(2,1)S(1)} copy-done((bf16[768,1536]{1,0:T(8,128)(2,1)S(1)}, bf16[768,1536]{1,0:T(8,128)(2,1)}, u32[]{:S(2)}) %copy-start) | copy-done | bytes 2359320
  42.0 0.7 shard_map.50.weight
  42.7 0.1 collective-permute-done.1.refs_2_
  42.8 3.3 %collective-permute-start.2 = (bf16[2,2,32,1536]{3,2,1,0:T(8,128)(2,1)S(1)}, bf16[2,2,32,1536]{3,2,1,0:T(8,128)(2,1)S(1)}, u32[]{:S(2)}, u32[]{:S(2)}) collective-permute-start(bf16[2,2,32,1536]{3,2,1,0:T(8,128)(2,1)S(1)} %collective-permute-done.1.refs_2_), channel_id=1, source_target_pairs={{0,1},{1,2},{2,3},{3,4},{4,5},{5,6},{6,7},{7,0},{16,23},{17,16},{1... | collective-permute-start | bytes 1179656 | tf_op jit(solution)/shard_map/ppermute | solution.py:31
  46.1 3.0 %collective-permute-start.5 = (bf16[2,2,32,1536]{3,2,1,0:T(8,128)(2,1)}, bf16[2,2,32,1536]{3,2,1,0:T(8,128)(2,1)S(1)}, u32[]{:S(2)}, u32[]{:S(2)}) collective-permute-start(bf16[2,2,32,1536]{3,2,1,0:T(8,128)(2,1)} %collective-permute-done.4), channel_id=1, source_target_pairs={{0,16},{16,0},{1,17},{17,1},{2,18},{18,2},{3,19},{19,3},{4,20},{20... | collective-permute-start | bytes 1179656 | tf_op jit(solution)/shard_map/ppermute | solution.py:20
  49.1 0.0 collective-permute-done.7
  49.1 3.0 %collective-permute-start.9 = (bf16[2,2,32,1536]{3,2,1,0:T(8,128)(2,1)}, bf16[2,2,32,1536]{3,2,1,0:T(8,128)(2,1)}, u32[]{:S(2)}, u32[]{:S(2)}) collective-permute-start(bf16[2,2,32,1536]{3,2,1,0:T(8,128)(2,1)} %collective-permute-done.7), channel_id=1, source_target_pairs={{0,1},{1,2},{2,3},{3,4},{4,5},{5,6},{6,7},{7,0},{16,23},{17,16},{1... | collective-permute-start | bytes 1179656 | tf_op jit(solution)/shard_map/ppermute | solution.py:31
  52.2 1.5 %collective-permute-done.2.refs_3_ = bf16[2,2,32,1536]{3,2,1,0:T(8,128)(2,1)S(1)} collective-permute-done((bf16[2,2,32,1536]{3,2,1,0:T(8,128)(2,1)S(1)}, bf16[2,2,32,1536]{3,2,1,0:T(8,128)(2,1)S(1)}, u32[]{:S(2)}, u32[]{:S(2)}) %collective-permute-start.2) | collective-permute-done | bytes 393248 | tf_op jit(solution)/shard_map/ppermute | solution.py:31
  53.7 0.0 collective-permute-done.5.refs_5_
  53.7 2.1 %collective-permute-start.6 = (bf16[2,2,32,1536]{3,2,1,0:T(8,128)(2,1)S(1)}, bf16[2,2,32,1536]{3,2,1,0:T(8,128)(2,1)}, u32[]{:S(2)}, u32[]{:S(2)}) collective-permute-start(bf16[2,2,32,1536]{3,2,1,0:T(8,128)(2,1)S(1)} %collective-permute-done.2.refs_3_), channel_id=1, source_target_pairs={{0,1},{1,2},{2,3},{3,4},{4,5},{5,6},{6,7},{7,0},{16,23},{17,16},{1... | collective-permute-start | bytes 1179656 | tf_op jit(solution)/shard_map/ppermute | solution.py:31
  55.8 3.2 %collective-permute-start.8 = (bf16[2,2,32,1536]{3,2,1,0:T(8,128)(2,1)}, bf16[2,2,32,1536]{3,2,1,0:T(8,128)(2,1)}, u32[]{:S(2)}, u32[]{:S(2)}) collective-permute-start(bf16[2,2,32,1536]{3,2,1,0:T(8,128)(2,1)} %collective-permute-done.7), channel_id=1, source_target_pairs={{0,16},{16,0},{1,17},{17,1},{2,18},{18,2},{3,19},{19,3},{4,20},{20... | collective-permute-start | bytes 1179656 | tf_op jit(solution)/shard_map/ppermute | solution.py:20
  59.0 1.3 %collective-permute-done.9 = bf16[2,2,32,1536]{3,2,1,0:T(8,128)(2,1)} collective-permute-done((bf16[2,2,32,1536]{3,2,1,0:T(8,128)(2,1)}, bf16[2,2,32,1536]{3,2,1,0:T(8,128)(2,1)}, u32[]{:S(2)}, u32[]{:S(2)}) %collective-permute-start.9) | collective-permute-done | bytes 393248 | tf_op jit(solution)/shard_map/ppermute | solution.py:31
  60.3 1.9 %collective-permute-start.10 = (bf16[2,2,32,1536]{3,2,1,0:T(8,128)(2,1)}, bf16[2,2,32,1536]{3,2,1,0:T(8,128)(2,1)}, u32[]{:S(2)}, u32[]{:S(2)}) collective-permute-start(bf16[2,2,32,1536]{3,2,1,0:T(8,128)(2,1)} %collective-permute-done.9), channel_id=1, source_target_pairs={{0,16},{16,0},{1,17},{17,1},{2,18},{18,2},{3,19},{19,3},{4,20},{20... | collective-permute-start | bytes 1179656 | tf_op jit(solution)/shard_map/ppermute | solution.py:20
  62.3 0.0 all-to-all-done
  62.3 2.4 %collective-permute-done.6.refs_4_ = bf16[2,2,32,1536]{3,2,1,0:T(8,128)(2,1)} collective-permute-done((bf16[2,2,32,1536]{3,2,1,0:T(8,128)(2,1)S(1)}, bf16[2,2,32,1536]{3,2,1,0:T(8,128)(2,1)}, u32[]{:S(2)}, u32[]{:S(2)}) %collective-permute-start.6) | collective-permute-done | bytes 393248 | tf_op jit(solution)/shard_map/ppermute | solution.py:31
  64.7 0.0 collective-permute-done.8.refs_6_
  64.7 0.0 collective-permute-done.10.refs_7_
  64.7 3.2 %shard_map.52 = f32[4,4,32,768]{3,2,1,0:T(8,128)S(1)} custom-call(s32[3]{0:T(128)S(1)} %pad_add_fusion.place, bf16[1536,768]{1,0:T(8,128)(2,1)S(1)} %shard_map.50.weight, bf16[2,2,32,1536]{3,2,1,0:T(8,128)(2,1)} %bitcast.22, bf16[2,2,32,1536]{3,2,1,0:T(8,128)(2,1)} %collective-permute-done.refs_1_, bf16[2,2,32,1536]{3,2,1,0:T(8,128)(2,1)} %copy-done.2, ...), custom_call_target="tpu_custom_call" | custom-call | flops 1207959552 | bytes 8388608 | tf_op jit(solution)/shard_map/pallas_call | solution.py:54
  67.9 1.9 %collective-permute-start.11 = (f32[4,4,32,768]{3,2,1,0:T(8,128)S(1)}, f32[4,4,32,768]{3,2,1,0:T(8,128)S(1)}, u32[]{:S(2)}, u32[]{:S(2)}) collective-permute-start(f32[4,4,32,768]{3,2,1,0:T(8,128)S(1)} %shard_map.52), channel_id=1, source_target_pairs={{0,16},{16,0},{1,17},{17,1},{2,18},{18,2},{3,19},{19,3},{4,20},{20... | collective-permute-start | bytes 4718600 | tf_op jit(solution)/shard_map/ppermute | solution.py:20
  69.8 3.2 %shard_map.51 = f32[4,4,32,768]{3,2,1,0:T(8,128)S(1)} custom-call(s32[3]{0:T(128)S(1)} %pad_add_fusion.place, bf16[1536,768]{1,0:T(8,128)(2,1)S(1)} %shard_map.50.weight, bf16[2,2,32,1536]{3,2,1,0:T(8,128)(2,1)} %bitcast.23, bf16[2,2,32,1536]{3,2,1,0:T(8,128)(2,1)} %collective-permute-done.refs_1_, bf16[2,2,32,1536]{3,2,1,0:T(8,128)(2,1)} %copy-done.2, ...), custom_call_target="tpu_custom_call" | custom-call | flops 1207959552 | bytes 8388608 | tf_op jit(solution)/shard_map/pallas_call | solution.py:54
  73.1 0.1 collective-permute-done.11
  73.2 0.1 fusion.3
  73.3 2.2 %collective-permute-start.13 = (f32[4,32,768]{2,1,0:T(8,128)S(1)}, f32[4,32,768]{2,1,0:T(8,128)S(1)}, u32[]{:S(2)}, u32[]{:S(2)}) collective-permute-start(f32[4,32,768]{2,1,0:T(8,128)S(1)} %get-tuple-element.37), channel_id=1, source_target_pairs={{0,128},{128,256},{256,384},{384,0},{16,400},{144,16},{272,144},{4... | collective-permute-start | bytes 1179656 | tf_op jit(solution)/shard_map/ppermute | solution.py:33
  75.5 2.6 %collective-permute-start.15 = (bf16[16,32,768]{2,1,0:T(8,128)(2,1)S(1)}, bf16[16,32,768]{2,1,0:T(8,128)(2,1)S(1)}, u32[]{:S(2)}, u32[]{:S(2)}) collective-permute-start(bf16[16,32,768]{2,1,0:T(8,128)(2,1)S(1)} %all-to-all-done), channel_id=1, source_target_pairs={{0,16},{16,0},{1,17},{17,1},{2,18},{18,2},{3,19},{19,3},{4,20},{20... | collective-permute-start | bytes 2359304 | tf_op jit(solution)/shard_map/ppermute | solution.py:20
  78.1 3.0 %collective-permute-start.12 = (f32[4,32,768]{2,1,0:T(8,128)S(1)}, f32[4,32,768]{2,1,0:T(8,128)S(1)}, u32[]{:S(2)}, u32[]{:S(2)}) collective-permute-start(f32[4,32,768]{2,1,0:T(8,128)S(1)} %get-tuple-element.36), channel_id=1, source_target_pairs={{0,384},{128,0},{256,128},{384,256},{16,144},{144,272},{272,400},{... | collective-permute-start | bytes 1179656 | tf_op jit(solution)/shard_map/ppermute | solution.py:33
  81.1 2.2 %collective-permute-done.13 = f32[4,32,768]{2,1,0:T(8,128)S(1)} collective-permute-done((f32[4,32,768]{2,1,0:T(8,128)S(1)}, f32[4,32,768]{2,1,0:T(8,128)S(1)}, u32[]{:S(2)}, u32[]{:S(2)}) %collective-permute-start.13) | collective-permute-done | bytes 393248 | tf_op jit(solution)/shard_map/ppermute | solution.py:33
  83.3 0.1 fusion.2
  83.4 3.0 %collective-permute-start.14 = (f32[4,32,768]{2,1,0:T(8,128)S(1)}, f32[4,32,768]{2,1,0:T(8,128)S(1)}, u32[]{:S(2)}, u32[]{:S(2)}) collective-permute-start(f32[4,32,768]{2,1,0:T(8,128)S(1)} %fusion.2), channel_id=1, source_target_pairs={{0,128},{128,256},{256,384},{384,0},{16,400},{144,16},{272,144},{4... | collective-permute-start | bytes 1179656 | tf_op jit(solution)/shard_map/ppermute | solution.py:33
  86.5 1.0 shard_map.53.turned
  87.5 5.7 %shard_map.54 = bf16[768,1536]{1,0:T(8,128)(2,1)} custom-call(bf16[2,2,768,256]{3,2,1,0:T(8,128)(2,1)S(1)} %shard_map.53.turned, bf16[2,2,32,1536]{3,2,1,0:T(8,128)(2,1)} %bitcast.24, bf16[2,2,32,1536]{3,2,1,0:T(8,128)(2,1)} %collective-permute-done.refs_1_, bf16[2,2,32,1536]{3,2,1,0:T(8,128)(2,1)} %copy-done.2, bf16[2,2,32,1536]{3,2,1,0:T(8,128)(2,1)} %copy-done.3, ...), custom_call_target="tpu_custom_call" | custom-call | flops 2415919104 | bytes 7340032 | tf_op jit(solution)/shard_map/pallas_call | solution.py:111
  93.2 0.0 collective-permute-done.12
  93.2 0.0 collective-permute-done.14
  93.2 0.1 fusion.6
  93.3 20.1 %all_to_all.14 = f32[4,32,768]{2,1,0:T(8,128)S(1)} all-to-all(f32[4,32,768]{2,1,0:T(8,128)S(1)} %fusion.6), channel_id=1, replica_groups=mesh['x'=4,'yh'=4,'core'=2,'yl'=2,'z'=8] {'yh'}, dimensions={0} | all-to-all | bytes 786432 | tf_op jit(solution)/shard_map/all_to_all | solution.py:155
  113.4 0.6 reduce_sum.9
  (9 shorter events, 0.0 us)
Async XLA Ops:
  8.2 34.5 %copy-start.1 = (bf16[128,1536]{1,0:T(8,128)(2,1)}, bf16[128,1536]{1,0:T(8,128)(2,1)S(1)}, u32[]{:S(2)}) copy-start(bf16[128,1536]{1,0:T(8,128)(2,1)S(1)} %all_gather.3) | copy-start | bytes 1179652
  8.2 6.2 %collective-permute-start.3 = (bf16[2,2,32,1536]{3,2,1,0:T(8,128)(2,1)S(1)}, bf16[2,2,32,1536]{3,2,1,0:T(8,128)(2,1)S(1)}, u32[]{:S(2)}, u32[]{:S(2)}) collective-permute-start(bf16[2,2,32,1536]{3,2,1,0:T(8,128)(2,1)S(1)} %bitcast.20), channel_id=1, source_target_pairs={{0,16},{16,0},{1,17},{17,1},{2,18},{18,2},{3,19},{19,3},{4,20},{20... | collective-permute-start | bytes 1179656 | tf_op jit(solution)/shard_map/ppermute | solution.py:20
  10.2 20.4 %collective-permute-start = (bf16[2,2,32,1536]{3,2,1,0:T(8,128)(2,1)S(1)}, bf16[2,2,32,1536]{3,2,1,0:T(8,128)(2,1)}, u32[]{:S(2)}, u32[]{:S(2)}) collective-permute-start(bf16[2,2,32,1536]{3,2,1,0:T(8,128)(2,1)S(1)} %bitcast.21), channel_id=1, source_target_pairs={{0,1},{1,2},{2,3},{3,4},{4,5},{5,6},{6,7},{7,0},{16,23},{17,16},{1... | collective-permute-start | bytes 1179656 | tf_op jit(solution)/shard_map/ppermute | solution.py:31
  14.4 20.4 %collective-permute-start.4 = (bf16[2,2,32,1536]{3,2,1,0:T(8,128)(2,1)S(1)}, bf16[2,2,32,1536]{3,2,1,0:T(8,128)(2,1)}, u32[]{:S(2)}, u32[]{:S(2)}) collective-permute-start(bf16[2,2,32,1536]{3,2,1,0:T(8,128)(2,1)S(1)} %collective-permute-done.3), channel_id=1, source_target_pairs={{0,1},{1,2},{2,3},{3,4},{4,5},{5,6},{6,7},{7,0},{16,23},{17,16},{1... | collective-permute-start | bytes 1179656 | tf_op jit(solution)/shard_map/ppermute | solution.py:31
  20.5 41.8 %all-to-all-start = ((bf16[16,32,768]{2,1,0:T(8,128)(2,1)}), bf16[16,32,768]{2,1,0:T(8,128)(2,1)S(1)}, u32[]{:S(2)}, u32[]{:S(2)}) async-start(bf16[16,32,768]{2,1,0:T(8,128)(2,1)} %tile.2), calls=%async_computation | async-start | bytes 1572864 | tf_op jit(solution)/shard_map/all_to_all | solution.py:130
  30.6 12.2 %collective-permute-start.1 = (bf16[2,2,32,1536]{3,2,1,0:T(8,128)(2,1)}, bf16[2,2,32,1536]{3,2,1,0:T(8,128)(2,1)S(1)}, u32[]{:S(2)}, u32[]{:S(2)}) collective-permute-start(bf16[2,2,32,1536]{3,2,1,0:T(8,128)(2,1)} %collective-permute-done.refs_1_), channel_id=1, source_target_pairs={{0,1},{1,2},{2,3},{3,4},{4,5},{5,6},{6,7},{7,0},{16,23},{17,16},{1... | collective-permute-start | bytes 1179656 | tf_op jit(solution)/shard_map/ppermute | solution.py:31
  34.9 14.3 %collective-permute-start.7 = (bf16[2,2,32,1536]{3,2,1,0:T(8,128)(2,1)}, bf16[2,2,32,1536]{3,2,1,0:T(8,128)(2,1)}, u32[]{:S(2)}, u32[]{:S(2)}) collective-permute-start(bf16[2,2,32,1536]{3,2,1,0:T(8,128)(2,1)} %collective-permute-done.4), channel_id=1, source_target_pairs={{0,1},{1,2},{2,3},{3,4},{4,5},{5,6},{6,7},{7,0},{16,23},{17,16},{1... | collective-permute-start | bytes 1179656 | tf_op jit(solution)/shard_map/ppermute | solution.py:31
  40.4 1.7 %copy-start = (bf16[768,1536]{1,0:T(8,128)(2,1)S(1)}, bf16[768,1536]{1,0:T(8,128)(2,1)}, u32[]{:S(2)}) copy-start(bf16[768,1536]{1,0:T(8,128)(2,1)} %weight.1) | copy-start | bytes 7077892
  42.8 17.5 %copy-start.2 = (bf16[2,2,32,1536]{3,2,1,0:T(8,128)(2,1)}, bf16[2,2,32,1536]{3,2,1,0:T(8,128)(2,1)S(1)}, u32[]{:S(2)}) copy-start(bf16[2,2,32,1536]{3,2,1,0:T(8,128)(2,1)S(1)} %collective-permute-done.1.refs_2_) | copy-start | bytes 1179652
  42.8 10.9 %collective-permute-start.2 = (bf16[2,2,32,1536]{3,2,1,0:T(8,128)(2,1)S(1)}, bf16[2,2,32,1536]{3,2,1,0:T(8,128)(2,1)S(1)}, u32[]{:S(2)}, u32[]{:S(2)}) collective-permute-start(bf16[2,2,32,1536]{3,2,1,0:T(8,128)(2,1)S(1)} %collective-permute-done.1.refs_2_), channel_id=1, source_target_pairs={{0,1},{1,2},{2,3},{3,4},{4,5},{5,6},{6,7},{7,0},{16,23},{17,16},{1... | collective-permute-start | bytes 1179656 | tf_op jit(solution)/shard_map/ppermute | solution.py:31
  46.1 7.6 %collective-permute-start.5 = (bf16[2,2,32,1536]{3,2,1,0:T(8,128)(2,1)}, bf16[2,2,32,1536]{3,2,1,0:T(8,128)(2,1)S(1)}, u32[]{:S(2)}, u32[]{:S(2)}) collective-permute-start(bf16[2,2,32,1536]{3,2,1,0:T(8,128)(2,1)} %collective-permute-done.4), channel_id=1, source_target_pairs={{0,16},{16,0},{1,17},{17,1},{2,18},{18,2},{3,19},{19,3},{4,20},{20... | collective-permute-start | bytes 1179656 | tf_op jit(solution)/shard_map/ppermute | solution.py:20
  49.1 11.2 %collective-permute-start.9 = (bf16[2,2,32,1536]{3,2,1,0:T(8,128)(2,1)}, bf16[2,2,32,1536]{3,2,1,0:T(8,128)(2,1)}, u32[]{:S(2)}, u32[]{:S(2)}) collective-permute-start(bf16[2,2,32,1536]{3,2,1,0:T(8,128)(2,1)} %collective-permute-done.7), channel_id=1, source_target_pairs={{0,1},{1,2},{2,3},{3,4},{4,5},{5,6},{6,7},{7,0},{16,23},{17,16},{1... | collective-permute-start | bytes 1179656 | tf_op jit(solution)/shard_map/ppermute | solution.py:31
  53.7 11.0 %copy-start.3 = (bf16[2,2,32,1536]{3,2,1,0:T(8,128)(2,1)}, bf16[2,2,32,1536]{3,2,1,0:T(8,128)(2,1)S(1)}, u32[]{:S(2)}) copy-start(bf16[2,2,32,1536]{3,2,1,0:T(8,128)(2,1)S(1)} %collective-permute-done.2.refs_3_) | copy-start | bytes 1179652
  53.7 6.7 %copy-start.4 = (bf16[2,2,32,1536]{3,2,1,0:T(8,128)(2,1)}, bf16[2,2,32,1536]{3,2,1,0:T(8,128)(2,1)S(1)}, u32[]{:S(2)}) copy-start(bf16[2,2,32,1536]{3,2,1,0:T(8,128)(2,1)S(1)} %collective-permute-done.5.refs_5_) | copy-start | bytes 1179652
  53.7 11.0 %collective-permute-start.6 = (bf16[2,2,32,1536]{3,2,1,0:T(8,128)(2,1)S(1)}, bf16[2,2,32,1536]{3,2,1,0:T(8,128)(2,1)}, u32[]{:S(2)}, u32[]{:S(2)}) collective-permute-start(bf16[2,2,32,1536]{3,2,1,0:T(8,128)(2,1)S(1)} %collective-permute-done.2.refs_3_), channel_id=1, source_target_pairs={{0,1},{1,2},{2,3},{3,4},{4,5},{5,6},{6,7},{7,0},{16,23},{17,16},{1... | collective-permute-start | bytes 1179656 | tf_op jit(solution)/shard_map/ppermute | solution.py:31
  55.8 8.9 %collective-permute-start.8 = (bf16[2,2,32,1536]{3,2,1,0:T(8,128)(2,1)}, bf16[2,2,32,1536]{3,2,1,0:T(8,128)(2,1)}, u32[]{:S(2)}, u32[]{:S(2)}) collective-permute-start(bf16[2,2,32,1536]{3,2,1,0:T(8,128)(2,1)} %collective-permute-done.7), channel_id=1, source_target_pairs={{0,16},{16,0},{1,17},{17,1},{2,18},{18,2},{3,19},{19,3},{4,20},{20... | collective-permute-start | bytes 1179656 | tf_op jit(solution)/shard_map/ppermute | solution.py:20
  60.3 4.3 %collective-permute-start.10 = (bf16[2,2,32,1536]{3,2,1,0:T(8,128)(2,1)}, bf16[2,2,32,1536]{3,2,1,0:T(8,128)(2,1)}, u32[]{:S(2)}, u32[]{:S(2)}) collective-permute-start(bf16[2,2,32,1536]{3,2,1,0:T(8,128)(2,1)} %collective-permute-done.9), channel_id=1, source_target_pairs={{0,16},{16,0},{1,17},{17,1},{2,18},{18,2},{3,19},{19,3},{4,20},{20... | collective-permute-start | bytes 1179656 | tf_op jit(solution)/shard_map/ppermute | solution.py:20
  67.9 5.3 %collective-permute-start.11 = (f32[4,4,32,768]{3,2,1,0:T(8,128)S(1)}, f32[4,4,32,768]{3,2,1,0:T(8,128)S(1)}, u32[]{:S(2)}, u32[]{:S(2)}) collective-permute-start(f32[4,4,32,768]{3,2,1,0:T(8,128)S(1)} %shard_map.52), channel_id=1, source_target_pairs={{0,16},{16,0},{1,17},{17,1},{2,18},{18,2},{3,19},{19,3},{4,20},{20... | collective-permute-start | bytes 4718600 | tf_op jit(solution)/shard_map/ppermute | solution.py:20
  73.3 10.0 %collective-permute-start.13 = (f32[4,32,768]{2,1,0:T(8,128)S(1)}, f32[4,32,768]{2,1,0:T(8,128)S(1)}, u32[]{:S(2)}, u32[]{:S(2)}) collective-permute-start(f32[4,32,768]{2,1,0:T(8,128)S(1)} %get-tuple-element.37), channel_id=1, source_target_pairs={{0,128},{128,256},{256,384},{384,0},{16,400},{144,16},{272,144},{4... | collective-permute-start | bytes 1179656 | tf_op jit(solution)/shard_map/ppermute | solution.py:33
  75.5 11.0 %collective-permute-start.15 = (bf16[16,32,768]{2,1,0:T(8,128)(2,1)S(1)}, bf16[16,32,768]{2,1,0:T(8,128)(2,1)S(1)}, u32[]{:S(2)}, u32[]{:S(2)}) collective-permute-start(bf16[16,32,768]{2,1,0:T(8,128)(2,1)S(1)} %all-to-all-done), channel_id=1, source_target_pairs={{0,16},{16,0},{1,17},{17,1},{2,18},{18,2},{3,19},{19,3},{4,20},{20... | collective-permute-start | bytes 2359304 | tf_op jit(solution)/shard_map/ppermute | solution.py:20
  78.1 15.1 %collective-permute-start.12 = (f32[4,32,768]{2,1,0:T(8,128)S(1)}, f32[4,32,768]{2,1,0:T(8,128)S(1)}, u32[]{:S(2)}, u32[]{:S(2)}) collective-permute-start(f32[4,32,768]{2,1,0:T(8,128)S(1)} %get-tuple-element.36), channel_id=1, source_target_pairs={{0,384},{128,0},{256,128},{384,256},{16,144},{144,272},{272,400},{... | collective-permute-start | bytes 1179656 | tf_op jit(solution)/shard_map/ppermute | solution.py:33
  83.4 9.8 %collective-permute-start.14 = (f32[4,32,768]{2,1,0:T(8,128)S(1)}, f32[4,32,768]{2,1,0:T(8,128)S(1)}, u32[]{:S(2)}, u32[]{:S(2)}) collective-permute-start(f32[4,32,768]{2,1,0:T(8,128)S(1)} %fusion.2), channel_id=1, source_target_pairs={{0,128},{128,256},{256,384},{384,0},{16,400},{144,16},{272,144},{4... | collective-permute-start | bytes 1179656 | tf_op jit(solution)/shard_map/ppermute | solution.py:33

commit v5 on v4

--- a/solution.py
+++ b/solution.py
@@ -14,6 +14,7 @@
 VMEM = pl.BlockSpec(memory_space=pltpu.VMEM)
 MIB = 2**20
 HOPS = (0, 1, 2, 3, 4, -1, -2, -3)
+EARLY, LATE = (0, 1, 2, 3, -1, -2), (4, -3)
 
 
 def swap(value, axis):
@@ -37,12 +38,14 @@
     return lax.rem(place[1] + (2 * place[0] - 1) * hops + 8, 8)
 
 
-def sums_kernel(far, place, weight, *refs):
-    held, out = refs[:-1], refs[-1]
+def sums_kernel(far, arrived, place, weight, *refs):
+    held, before, out = refs[: len(arrived)], refs[len(arrived) : -1], refs[-1]
     half = 1 - place[0] if far else place[0]
     rows = jnp.concatenate([h[:, half].reshape(64, -1) for h in held])
     product = jnp.dot(rows, weight[...], preferred_element_type=jnp.float32)
-    for i, hops in enumerate(HOPS):
+    if before:
+        out[...] = before[0][...]
+    for i, hops in enumerate(arrived):
         z = origin(place, hops)
         for yl in range(2):
             at = 64 * i + 32 * yl
@@ -50,17 +53,17 @@
             out[step, lax.rem(z, 4)] = product[at : at + 32]
 
 
-def sums(far, place, weight, held):
+def sums(far, arrived, place, weight, held, *before):
     return pl.pallas_call(
-        functools.partial(sums_kernel, far),
-        in_specs=[SMEM] + [VMEM] * (1 + len(held)),
+        functools.partial(sums_kernel, far, arrived),
+        in_specs=[SMEM] + [VMEM] * (1 + len(held) + len(before)),
         out_specs=VMEM,
         out_shape=jax.ShapeDtypeStruct((4, 4, 32, 768), jnp.float32),
         compiler_params=pltpu.CompilerParams(vmem_limit_bytes=12 * MIB),
         cost_estimate=pl.CostEstimate(
-            flops=2 * 512 * 768 * 1536, bytes_accessed=8 * MIB, transcendentals=0
+            flops=128 * len(held) * 768 * 1536, bytes_accessed=8 * MIB, transcendentals=0
         ),
-    )(place, weight, *held)
+    )(place, weight, *held, *before)
 
 
 def flip_kernel(weight, out):
@@ -139,12 +142,15 @@
     mine[3], side = lax.optimization_barrier((mine[3], side))
     mine.append(around(mine[3]))
     sides = [side, swap(other[2], "core"), swap(other[3], "core")]
-    *held, act = lax.optimization_barrier((*mine, *sides, act))
-    held = [pltpu.with_memory_space_constraint(block, pltpu.HBM) for block in held]
+    fixed = lambda blocks: [pltpu.with_memory_space_constraint(b, pltpu.HBM) for b in blocks]
+    sides[1], act = lax.optimization_barrier((sides[1], act))
+    start = sums(True, EARLY, place, weight, fixed([*mine[:4], *sides[:2]]))
+    *held, start = lax.optimization_barrier((*mine, *sides, start))
+    held = fixed(held)
     act = act.reshape(16, 32, 768)
 
-    theirs = swap(sums(True, place, weight, held), "core")
-    ours = sums(False, place, weight, held)
+    theirs = swap(sums(True, LATE, place, weight, [held[4], held[7]], start), "core")
+    ours = sums(False, HOPS, place, weight, held)
     own, one, two, three = (ours[i] + theirs[i] for i in range(4))
     passed = around(two, "x")
     direct = around(three, "x", -1)

time: 115 us -> 114 us (level)
  waiting for transfers between devices: 7.75 us -> 5.38 us
  Pallas kernels: 13.8 us -> 15 us
    ppermute x7, waiting for transfers between devices: 5.37 us -> 3.07 us  [around(): return lax.ppermute(value, ('core', 'z'), pairs)]
    ppermute x7, starting transfers between devices: 26.7 us -> 28 us  [around(): return lax.ppermute(value, ('core', 'z'), pairs)]
    ppermute x6, starting transfers between devices: 14.5 us -> 13.3 us  [swap(): return lax.ppermute(value, axis, [(0, 1), (1, 0)])]
    pallas_call x2 -> x3, Pallas kernels: 6.44 us -> 7.61 us  [sums(): pl.pallas_call(functools.partial(sums_kernel, far, arrived), in_specs=[SM...]
  transfers between devices with their start and end apart: 17 -> 17, of which waited for: 6 -> 4; matrix products, arithmetic and copies ran while one was open for 2% -> 2% of each run, Pallas kernels for 9% -> 12%
where the time goes in v5:
time: 114 us; the launch traced here: 113 us
  starting transfers between devices  60 us (53%)
  blocking collectives  27.3 us (24%)
  Pallas kernels  15 us (13%)
  waiting for transfers between devices  5.38 us (5%)
  local copies, waits for them, and re-layouts  3.44 us (3%)
    ppermute x7, starting transfers between devices, around(): return lax.ppermute(value, ('core', 'z'), pairs)  28 us
    all_to_all x1, blocking collectives, on_device(): total = lax.all_to_all(total, 'yh', 0, 0).sum(0)  19.8 us
    ppermute x6, starting transfers between devices, swap(): return lax.ppermute(value, axis, [(0, 1), (1, 0)])  13.3 us
    all_to_all x1, starting transfers between devices, on_device(): lax.all_to_all(jnp.tile(activation, (16, 1)), ('x', 'yh'), 0, 0, tiled=True)  10.1 us
    ppermute x3, starting transfers between devices, around(): return lax.ppermute(value, (axis, 'core'), pairs)  8.6 us
    pallas_call x3, Pallas kernels, sums(): pl.pallas_call(functools.partial(sums_kernel, far, arrived), in_specs=[SM...  7.61 us
    all_gather x1, blocking collectives, on_device(): lax.all_gather(upstream, 'yl', axis=0, tiled=True).reshape(2, 2, 32, 1536)  7.52 us
    pallas_call x1, Pallas kernels, weight_gradient(): pl.pallas_call(weight_kernel, grid=(1536 // wide,), in_specs=[pl.BlockSpe...  5.72 us
  transfers between devices with their start and end apart: 17, of which 4 were waited for; matrix products, arithmetic and copies ran while one was open for 2% of the time, Pallas kernels for 12%

profile of v5, /device:TPU:6, one launch (start us, length us, event | category | flops | bytes accessed | tf_op | source)
XLA Modules:
  0.0 113.0 jit_solution(11152475842859319746)
XLA Ops:
  0.6 0.1 pad_add_fusion.place
  0.7 7.5 %all_gather.3 = bf16[128,1536]{1,0:T(8,128)(2,1)S(1)} all-gather(bf16[64,1536]{1,0:T(8,128)(2,1)} %param.4), channel_id=1, replica_groups=mesh['x'=4,'yh'=4,'core'=2,'yl'=2,'z'=8] {'yl'}, dimensions={0}, use_global_device_ids=true | all-gather | bytes 589824 | tf_op jit(solution)/shard_map/all_gather | solution.py:134
  8.2 1.9 %collective-permute-start.3 = (bf16[2,2,32,1536]{3,2,1,0:T(8,128)(2,1)S(1)}, bf16[2,2,32,1536]{3,2,1,0:T(8,128)(2,1)S(1)}, u32[]{:S(2)}, u32[]{:S(2)}) collective-permute-start(bf16[2,2,32,1536]{3,2,1,0:T(8,128)(2,1)S(1)} %bitcast.20), channel_id=1, source_target_pairs={{0,16},{16,0},{1,17},{17,1},{2,18},{18,2},{3,19},{19,3},{4,20},{20... | collective-permute-start | bytes 1179656 | tf_op jit(solution)/shard_map/ppermute | solution.py:21
  10.2 4.3 %collective-permute-start = (bf16[2,2,32,1536]{3,2,1,0:T(8,128)(2,1)S(1)}, bf16[2,2,32,1536]{3,2,1,0:T(8,128)(2,1)}, u32[]{:S(2)}, u32[]{:S(2)}) collective-permute-start(bf16[2,2,32,1536]{3,2,1,0:T(8,128)(2,1)S(1)} %bitcast.21), channel_id=1, source_target_pairs={{0,1},{1,2},{2,3},{3,4},{4,5},{5,6},{6,7},{7,0},{16,23},{17,16},{1... | collective-permute-start | bytes 1179656 | tf_op jit(solution)/shard_map/ppermute | solution.py:32
  14.4 0.0 collective-permute-done.3
  14.4 4.3 %collective-permute-start.4 = (bf16[2,2,32,1536]{3,2,1,0:T(8,128)(2,1)S(1)}, bf16[2,2,32,1536]{3,2,1,0:T(8,128)(2,1)}, u32[]{:S(2)}, u32[]{:S(2)}) collective-permute-start(bf16[2,2,32,1536]{3,2,1,0:T(8,128)(2,1)S(1)} %collective-permute-done.3), channel_id=1, source_target_pairs={{0,1},{1,2},{2,3},{3,4},{4,5},{5,6},{6,7},{7,0},{16,23},{17,16},{1... | collective-permute-start | bytes 1179656 | tf_op jit(solution)/shard_map/ppermute | solution.py:32
  18.7 1.8 %tile.2 = bf16[16,32,768]{2,1,0:T(8,128)(2,1)} broadcast(bf16[32,768]{1,0:T(8,128)(2,1)} %param.3), dimensions={1,2} | broadcast | bytes 835584 | tf_op jit(solution)/shard_map/tile | solution.py:133
  20.5 10.1 %all-to-all-start = ((bf16[16,32,768]{2,1,0:T(8,128)(2,1)}), bf16[16,32,768]{2,1,0:T(8,128)(2,1)S(1)}, u32[]{:S(2)}, u32[]{:S(2)}) async-start(bf16[16,32,768]{2,1,0:T(8,128)(2,1)} %tile.2), calls=%async_computation | async-start | bytes 1572864 | tf_op jit(solution)/shard_map/all_to_all | solution.py:133
  30.6 0.0 collective-permute-done.refs_1_
  30.6 4.3 %collective-permute-start.1 = (bf16[2,2,32,1536]{3,2,1,0:T(8,128)(2,1)}, bf16[2,2,32,1536]{3,2,1,0:T(8,128)(2,1)S(1)}, u32[]{:S(2)}, u32[]{:S(2)}) collective-permute-start(bf16[2,2,32,1536]{3,2,1,0:T(8,128)(2,1)} %collective-permute-done.refs_1_), channel_id=1, source_target_pairs={{0,1},{1,2},{2,3},{3,4},{4,5},{5,6},{6,7},{7,0},{16,23},{17,16},{1... | collective-permute-start | bytes 1179656 | tf_op jit(solution)/shard_map/ppermute | solution.py:32
  34.9 0.0 collective-permute-done.4
  34.9 5.5 %collective-permute-start.7 = (bf16[2,2,32,1536]{3,2,1,0:T(8,128)(2,1)}, bf16[2,2,32,1536]{3,2,1,0:T(8,128)(2,1)}, u32[]{:S(2)}, u32[]{:S(2)}) collective-permute-start(bf16[2,2,32,1536]{3,2,1,0:T(8,128)(2,1)} %collective-permute-done.4), channel_id=1, source_target_pairs={{0,1},{1,2},{2,3},{3,4},{4,5},{5,6},{6,7},{7,0},{16,23},{17,16},{1... | collective-permute-start | bytes 1179656 | tf_op jit(solution)/shard_map/ppermute | solution.py:32
  40.4 0.0 copy-start
  40.4 1.7 %copy-done = bf16[768,1536]{1,0:T(8,128)(2,1)S(1)} copy-done((bf16[768,1536]{1,0:T(8,128)(2,1)S(1)}, bf16[768,1536]{1,0:T(8,128)(2,1)}, u32[]{:S(2)}) %copy-start) | copy-done | bytes 2359320
  42.0 0.7 shard_map.50.weight
  42.7 0.1 collective-permute-done.1.refs_2_
  42.8 3.3 %collective-permute-start.2 = (bf16[2,2,32,1536]{3,2,1,0:T(8,128)(2,1)S(1)}, bf16[2,2,32,1536]{3,2,1,0:T(8,128)(2,1)S(1)}, u32[]{:S(2)}, u32[]{:S(2)}) collective-permute-start(bf16[2,2,32,1536]{3,2,1,0:T(8,128)(2,1)S(1)} %collective-permute-done.1.refs_2_), channel_id=1, source_target_pairs={{0,1},{1,2},{2,3},{3,4},{4,5},{5,6},{6,7},{7,0},{16,23},{17,16},{1... | collective-permute-start | bytes 1179656 | tf_op jit(solution)/shard_map/ppermute | solution.py:32
  46.1 3.0 %collective-permute-start.5 = (bf16[2,2,32,1536]{3,2,1,0:T(8,128)(2,1)}, bf16[2,2,32,1536]{3,2,1,0:T(8,128)(2,1)S(1)}, u32[]{:S(2)}, u32[]{:S(2)}) collective-permute-start(bf16[2,2,32,1536]{3,2,1,0:T(8,128)(2,1)} %collective-permute-done.4), channel_id=1, source_target_pairs={{0,16},{16,0},{1,17},{17,1},{2,18},{18,2},{3,19},{19,3},{4,20},{20... | collective-permute-start | bytes 1179656 | tf_op jit(solution)/shard_map/ppermute | solution.py:21
  49.1 0.0 collective-permute-done.7
  49.1 3.0 %collective-permute-start.9 = (bf16[2,2,32,1536]{3,2,1,0:T(8,128)(2,1)}, bf16[2,2,32,1536]{3,2,1,0:T(8,128)(2,1)}, u32[]{:S(2)}, u32[]{:S(2)}) collective-permute-start(bf16[2,2,32,1536]{3,2,1,0:T(8,128)(2,1)} %collective-permute-done.7), channel_id=1, source_target_pairs={{0,1},{1,2},{2,3},{3,4},{4,5},{5,6},{6,7},{7,0},{16,23},{17,16},{1... | collective-permute-start | bytes 1179656 | tf_op jit(solution)/shard_map/ppermute | solution.py:32
  52.2 1.9 %collective-permute-start.8 = (bf16[2,2,32,1536]{3,2,1,0:T(8,128)(2,1)}, bf16[2,2,32,1536]{3,2,1,0:T(8,128)(2,1)}, u32[]{:S(2)}, u32[]{:S(2)}) collective-permute-start(bf16[2,2,32,1536]{3,2,1,0:T(8,128)(2,1)} %collective-permute-done.7), channel_id=1, source_target_pairs={{0,16},{16,0},{1,17},{17,1},{2,18},{18,2},{3,19},{19,3},{4,20},{20... | collective-permute-start | bytes 1179656 | tf_op jit(solution)/shard_map/ppermute | solution.py:21
  54.1 0.0 collective-permute-done.2.refs_3_
  54.1 0.0 collective-permute-done.5.refs_4_.refs_5_
  54.1 3.4 %collective-permute-start.6 = (bf16[2,2,32,1536]{3,2,1,0:T(8,128)(2,1)S(1)}, bf16[2,2,32,1536]{3,2,1,0:T(8,128)(2,1)}, u32[]{:S(2)}, u32[]{:S(2)}) collective-permute-start(bf16[2,2,32,1536]{3,2,1,0:T(8,128)(2,1)S(1)} %collective-permute-done.2.refs_3_), channel_id=1, source_target_pairs={{0,1},{1,2},{2,3},{3,4},{4,5},{5,6},{6,7},{7,0},{16,23},{17,16},{1... | collective-permute-start | bytes 1179656 | tf_op jit(solution)/shard_map/ppermute | solution.py:32
  57.5 2.8 %collective-permute-done.9 = bf16[2,2,32,1536]{3,2,1,0:T(8,128)(2,1)} collective-permute-done((bf16[2,2,32,1536]{3,2,1,0:T(8,128)(2,1)}, bf16[2,2,32,1536]{3,2,1,0:T(8,128)(2,1)}, u32[]{:S(2)}, u32[]{:S(2)}) %collective-permute-start.9) | collective-permute-done | bytes 393248 | tf_op jit(solution)/shard_map/ppermute | solution.py:32
  60.3 1.9 %collective-permute-start.10 = (bf16[2,2,32,1536]{3,2,1,0:T(8,128)(2,1)}, bf16[2,2,32,1536]{3,2,1,0:T(8,128)(2,1)}, u32[]{:S(2)}, u32[]{:S(2)}) collective-permute-start(bf16[2,2,32,1536]{3,2,1,0:T(8,128)(2,1)} %collective-permute-done.9), channel_id=1, source_target_pairs={{0,16},{16,0},{1,17},{17,1},{2,18},{18,2},{3,19},{19,3},{4,20},{20... | collective-permute-start | bytes 1179656 | tf_op jit(solution)/shard_map/ppermute | solution.py:21
  62.3 0.0 all-to-all-done
  62.3 0.0 collective-permute-done.8.refs_5_.refs_6_
  62.3 2.7 %shard_map.51.refs_2_ = f32[4,4,32,768]{3,2,1,0:T(8,128)S(1)} custom-call(s32[3]{0:T(128)S(1)} %pad_add_fusion.place, bf16[1536,768]{1,0:T(8,128)(2,1)S(1)} %shard_map.50.weight, bf16[2,2,32,1536]{3,2,1,0:T(8,128)(2,1)} %bitcast.22, bf16[2,2,32,1536]{3,2,1,0:T(8,128)(2,1)} %collective-permute-done.refs_1_, bf16[2,2,32,1536]{3,2,1,0:T(8,128)(2,1)} %copy-done.2, ...), custom_call_target="tpu_custom_call" | custom-call | flops 905969664 | bytes 8388608 | tf_op jit(solution)/shard_map/pallas_call | solution.py:57
  65.0 0.2 collective-permute-done.6.refs_4_.refs_0_
  65.1 0.0 collective-permute-done.10.refs_7_.refs_1_
  65.1 1.7 %shard_map.53 = f32[4,4,32,768]{3,2,1,0:T(8,128)S(1)} custom-call(s32[3]{0:T(128)S(1)} %pad_add_fusion.place, bf16[1536,768]{1,0:T(8,128)(2,1)S(1)} %shard_map.50.weight, bf16[2,2,32,1536]{3,2,1,0:T(8,128)(2,1)} %collective-permute-done.6.refs_4_.refs_0_, bf16[2,2,32,1536]{3,2,1,0:T(8,128)(2,1)} %collective-permute-done.10.refs_7_.refs_1_, ...), custom_call_target="tpu_custom_call" | custom-call | flops 301989888 | bytes 8388608 | tf_op jit(solution)/shard_map/pallas_call | solution.py:57
  66.8 2.3 %collective-permute-start.11 = (f32[4,4,32,768]{3,2,1,0:T(8,128)S(1)}, f32[4,4,32,768]{3,2,1,0:T(8,128)S(1)}, u32[]{:S(2)}, u32[]{:S(2)}) collective-permute-start(f32[4,4,32,768]{3,2,1,0:T(8,128)S(1)} %shard_map.53), channel_id=1, source_target_pairs={{0,16},{16,0},{1,17},{17,1},{2,18},{18,2},{3,19},{19,3},{4,20},{20... | collective-permute-start | bytes 4718600 | tf_op jit(solution)/shard_map/ppermute | solution.py:21
  69.1 3.2 %shard_map.52 = f32[4,4,32,768]{3,2,1,0:T(8,128)S(1)} custom-call(s32[3]{0:T(128)S(1)} %pad_add_fusion.place, bf16[1536,768]{1,0:T(8,128)(2,1)S(1)} %shard_map.50.weight, bf16[2,2,32,1536]{3,2,1,0:T(8,128)(2,1)} %bitcast.23, bf16[2,2,32,1536]{3,2,1,0:T(8,128)(2,1)} %collective-permute-done.refs_1_, bf16[2,2,32,1536]{3,2,1,0:T(8,128)(2,1)} %copy-done.2, ...), custom_call_target="tpu_custom_call" | custom-call | flops 1207959552 | bytes 8388608 | tf_op jit(solution)/shard_map/pallas_call | solution.py:57
  72.4 0.1 fusion.3
  72.5 2.3 %collective-permute-start.13 = (f32[4,32,768]{2,1,0:T(8,128)S(1)}, f32[4,32,768]{2,1,0:T(8,128)S(1)}, u32[]{:S(2)}, u32[]{:S(2)}) collective-permute-start(f32[4,32,768]{2,1,0:T(8,128)S(1)} %get-tuple-element.41), channel_id=1, source_target_pairs={{0,128},{128,256},{256,384},{384,0},{16,400},{144,16},{272,144},{4... | collective-permute-start | bytes 1179656 | tf_op jit(solution)/shard_map/ppermute | solution.py:34
  74.8 2.3 %collective-permute-start.15 = (bf16[16,32,768]{2,1,0:T(8,128)(2,1)S(1)}, bf16[16,32,768]{2,1,0:T(8,128)(2,1)S(1)}, u32[]{:S(2)}, u32[]{:S(2)}) collective-permute-start(bf16[16,32,768]{2,1,0:T(8,128)(2,1)S(1)} %all-to-all-done), channel_id=1, source_target_pairs={{0,16},{16,0},{1,17},{17,1},{2,18},{18,2},{3,19},{19,3},{4,20},{20... | collective-permute-start | bytes 2359304 | tf_op jit(solution)/shard_map/ppermute | solution.py:21
  77.0 3.2 %collective-permute-start.12 = (f32[4,32,768]{2,1,0:T(8,128)S(1)}, f32[4,32,768]{2,1,0:T(8,128)S(1)}, u32[]{:S(2)}, u32[]{:S(2)}) collective-permute-start(f32[4,32,768]{2,1,0:T(8,128)S(1)} %get-tuple-element.40), channel_id=1, source_target_pairs={{0,384},{128,0},{256,128},{384,256},{16,144},{144,272},{272,400},{... | collective-permute-start | bytes 1179656 | tf_op jit(solution)/shard_map/ppermute | solution.py:34
  80.2 2.3 %collective-permute-done.13 = f32[4,32,768]{2,1,0:T(8,128)S(1)} collective-permute-done((f32[4,32,768]{2,1,0:T(8,128)S(1)}, f32[4,32,768]{2,1,0:T(8,128)S(1)}, u32[]{:S(2)}, u32[]{:S(2)}) %collective-permute-start.13) | collective-permute-done | bytes 393248 | tf_op jit(solution)/shard_map/ppermute | solution.py:34
  82.5 0.1 fusion.2
  82.6 3.1 %collective-permute-start.14 = (f32[4,32,768]{2,1,0:T(8,128)S(1)}, f32[4,32,768]{2,1,0:T(8,128)S(1)}, u32[]{:S(2)}, u32[]{:S(2)}) collective-permute-start(f32[4,32,768]{2,1,0:T(8,128)S(1)} %fusion.2), channel_id=1, source_target_pairs={{0,128},{128,256},{256,384},{384,0},{16,400},{144,16},{272,144},{4... | collective-permute-start | bytes 1179656 | tf_op jit(solution)/shard_map/ppermute | solution.py:34
  85.7 0.0 collective-permute-done.15.sibling
  85.7 1.0 shard_map.54.turned
  86.7 5.7 %shard_map.55 = bf16[768,1536]{1,0:T(8,128)(2,1)} custom-call(bf16[2,2,768,256]{3,2,1,0:T(8,128)(2,1)S(1)} %shard_map.54.turned, bf16[2,2,32,1536]{3,2,1,0:T(8,128)(2,1)} %bitcast.24, bf16[2,2,32,1536]{3,2,1,0:T(8,128)(2,1)} %collective-permute-done.refs_1_, bf16[2,2,32,1536]{3,2,1,0:T(8,128)(2,1)} %copy-done.2, bf16[2,2,32,1536]{3,2,1,0:T(8,128)(2,1)} %copy-done.3, ...), custom_call_target="tpu_custom_call" | custom-call | flops 2415919104 | bytes 7340032 | tf_op jit(solution)/shard_map/pallas_call | solution.py:114
  92.5 0.0 collective-permute-done.14
  92.5 0.1 fusion.6
  92.6 19.8 %all_to_all.14 = f32[4,32,768]{2,1,0:T(8,128)S(1)} all-to-all(f32[4,32,768]{2,1,0:T(8,128)S(1)} %fusion.6), channel_id=1, replica_groups=mesh['x'=4,'yh'=4,'core'=2,'yl'=2,'z'=8] {'yh'}, dimensions={0} | all-to-all | bytes 786432 | tf_op jit(solution)/shard_map/all_to_all | solution.py:161
  112.3 0.6 reduce_sum.9
  (10 shorter events, 0.0 us)
Async XLA Ops:
  8.2 34.5 %copy-start.1 = (bf16[128,1536]{1,0:T(8,128)(2,1)}, bf16[128,1536]{1,0:T(8,128)(2,1)S(1)}, u32[]{:S(2)}) copy-start(bf16[128,1536]{1,0:T(8,128)(2,1)S(1)} %all_gather.3) | copy-start | bytes 1179652
  8.2 6.2 %collective-permute-start.3 = (bf16[2,2,32,1536]{3,2,1,0:T(8,128)(2,1)S(1)}, bf16[2,2,32,1536]{3,2,1,0:T(8,128)(2,1)S(1)}, u32[]{:S(2)}, u32[]{:S(2)}) collective-permute-start(bf16[2,2,32,1536]{3,2,1,0:T(8,128)(2,1)S(1)} %bitcast.20), channel_id=1, source_target_pairs={{0,16},{16,0},{1,17},{17,1},{2,18},{18,2},{3,19},{19,3},{4,20},{20... | collective-permute-start | bytes 1179656 | tf_op jit(solution)/shard_map/ppermute | solution.py:21
  10.2 20.4 %collective-permute-start = (bf16[2,2,32,1536]{3,2,1,0:T(8,128)(2,1)S(1)}, bf16[2,2,32,1536]{3,2,1,0:T(8,128)(2,1)}, u32[]{:S(2)}, u32[]{:S(2)}) collective-permute-start(bf16[2,2,32,1536]{3,2,1,0:T(8,128)(2,1)S(1)} %bitcast.21), channel_id=1, source_target_pairs={{0,1},{1,2},{2,3},{3,4},{4,5},{5,6},{6,7},{7,0},{16,23},{17,16},{1... | collective-permute-start | bytes 1179656 | tf_op jit(solution)/shard_map/ppermute | solution.py:32
  14.4 20.4 %collective-permute-start.4 = (bf16[2,2,32,1536]{3,2,1,0:T(8,128)(2,1)S(1)}, bf16[2,2,32,1536]{3,2,1,0:T(8,128)(2,1)}, u32[]{:S(2)}, u32[]{:S(2)}) collective-permute-start(bf16[2,2,32,1536]{3,2,1,0:T(8,128)(2,1)S(1)} %collective-permute-done.3), channel_id=1, source_target_pairs={{0,1},{1,2},{2,3},{3,4},{4,5},{5,6},{6,7},{7,0},{16,23},{17,16},{1... | collective-permute-start | bytes 1179656 | tf_op jit(solution)/shard_map/ppermute | solution.py:32
  20.5 41.8 %all-to-all-start = ((bf16[16,32,768]{2,1,0:T(8,128)(2,1)}), bf16[16,32,768]{2,1,0:T(8,128)(2,1)S(1)}, u32[]{:S(2)}, u32[]{:S(2)}) async-start(bf16[16,32,768]{2,1,0:T(8,128)(2,1)} %tile.2), calls=%async_computation | async-start | bytes 1572864 | tf_op jit(solution)/shard_map/all_to_all | solution.py:133
  30.6 12.2 %collective-permute-start.1 = (bf16[2,2,32,1536]{3,2,1,0:T(8,128)(2,1)}, bf16[2,2,32,1536]{3,2,1,0:T(8,128)(2,1)S(1)}, u32[]{:S(2)}, u32[]{:S(2)}) collective-permute-start(bf16[2,2,32,1536]{3,2,1,0:T(8,128)(2,1)} %collective-permute-done.refs_1_), channel_id=1, source_target_pairs={{0,1},{1,2},{2,3},{3,4},{4,5},{5,6},{6,7},{7,0},{16,23},{17,16},{1... | collective-permute-start | bytes 1179656 | tf_op jit(solution)/shard_map/ppermute | solution.py:32
  34.9 14.3 %collective-permute-start.7 = (bf16[2,2,32,1536]{3,2,1,0:T(8,128)(2,1)}, bf16[2,2,32,1536]{3,2,1,0:T(8,128)(2,1)}, u32[]{:S(2)}, u32[]{:S(2)}) collective-permute-start(bf16[2,2,32,1536]{3,2,1,0:T(8,128)(2,1)} %collective-permute-done.4), channel_id=1, source_target_pairs={{0,1},{1,2},{2,3},{3,4},{4,5},{5,6},{6,7},{7,0},{16,23},{17,16},{1... | collective-permute-start | bytes 1179656 | tf_op jit(solution)/shard_map/ppermute | solution.py:32
  40.4 1.7 %copy-start = (bf16[768,1536]{1,0:T(8,128)(2,1)S(1)}, bf16[768,1536]{1,0:T(8,128)(2,1)}, u32[]{:S(2)}) copy-start(bf16[768,1536]{1,0:T(8,128)(2,1)} %weight.1) | copy-start | bytes 7077892
  42.8 17.5 %copy-start.2 = (bf16[2,2,32,1536]{3,2,1,0:T(8,128)(2,1)}, bf16[2,2,32,1536]{3,2,1,0:T(8,128)(2,1)S(1)}, u32[]{:S(2)}) copy-start(bf16[2,2,32,1536]{3,2,1,0:T(8,128)(2,1)S(1)} %collective-permute-done.1.refs_2_) | copy-start | bytes 1179652
  42.8 11.3 %collective-permute-start.2 = (bf16[2,2,32,1536]{3,2,1,0:T(8,128)(2,1)S(1)}, bf16[2,2,32,1536]{3,2,1,0:T(8,128)(2,1)S(1)}, u32[]{:S(2)}, u32[]{:S(2)}) collective-permute-start(bf16[2,2,32,1536]{3,2,1,0:T(8,128)(2,1)S(1)} %collective-permute-done.1.refs_2_), channel_id=1, source_target_pairs={{0,1},{1,2},{2,3},{3,4},{4,5},{5,6},{6,7},{7,0},{16,23},{17,16},{1... | collective-permute-start | bytes 1179656 | tf_op jit(solution)/shard_map/ppermute | solution.py:32
  46.1 8.0 %collective-permute-start.5 = (bf16[2,2,32,1536]{3,2,1,0:T(8,128)(2,1)}, bf16[2,2,32,1536]{3,2,1,0:T(8,128)(2,1)S(1)}, u32[]{:S(2)}, u32[]{:S(2)}) collective-permute-start(bf16[2,2,32,1536]{3,2,1,0:T(8,128)(2,1)} %collective-permute-done.4), channel_id=1, source_target_pairs={{0,16},{16,0},{1,17},{17,1},{2,18},{18,2},{3,19},{19,3},{4,20},{20... | collective-permute-start | bytes 1179656 | tf_op jit(solution)/shard_map/ppermute | solution.py:21
  49.1 11.2 %collective-permute-start.9 = (bf16[2,2,32,1536]{3,2,1,0:T(8,128)(2,1)}, bf16[2,2,32,1536]{3,2,1,0:T(8,128)(2,1)}, u32[]{:S(2)}, u32[]{:S(2)}) collective-permute-start(bf16[2,2,32,1536]{3,2,1,0:T(8,128)(2,1)} %collective-permute-done.7), channel_id=1, source_target_pairs={{0,1},{1,2},{2,3},{3,4},{4,5},{5,6},{6,7},{7,0},{16,23},{17,16},{1... | collective-permute-start | bytes 1179656 | tf_op jit(solution)/shard_map/ppermute | solution.py:32
  52.2 10.1 %collective-permute-start.8 = (bf16[2,2,32,1536]{3,2,1,0:T(8,128)(2,1)}, bf16[2,2,32,1536]{3,2,1,0:T(8,128)(2,1)}, u32[]{:S(2)}, u32[]{:S(2)}) collective-permute-start(bf16[2,2,32,1536]{3,2,1,0:T(8,128)(2,1)} %collective-permute-done.7), channel_id=1, source_target_pairs={{0,16},{16,0},{1,17},{17,1},{2,18},{18,2},{3,19},{19,3},{4,20},{20... | collective-permute-start | bytes 1179656 | tf_op jit(solution)/shard_map/ppermute | solution.py:21
  54.1 8.2 %copy-start.3 = (bf16[2,2,32,1536]{3,2,1,0:T(8,128)(2,1)}, bf16[2,2,32,1536]{3,2,1,0:T(8,128)(2,1)S(1)}, u32[]{:S(2)}) copy-start(bf16[2,2,32,1536]{3,2,1,0:T(8,128)(2,1)S(1)} %collective-permute-done.2.refs_3_) | copy-start | bytes 1179652
  54.1 6.2 %copy-start.4 = (bf16[2,2,32,1536]{3,2,1,0:T(8,128)(2,1)}, bf16[2,2,32,1536]{3,2,1,0:T(8,128)(2,1)S(1)}, u32[]{:S(2)}) copy-start(bf16[2,2,32,1536]{3,2,1,0:T(8,128)(2,1)S(1)} %collective-permute-done.5.refs_4_.refs_5_) | copy-start | bytes 1179652
  54.1 11.0 %collective-permute-start.6 = (bf16[2,2,32,1536]{3,2,1,0:T(8,128)(2,1)S(1)}, bf16[2,2,32,1536]{3,2,1,0:T(8,128)(2,1)}, u32[]{:S(2)}, u32[]{:S(2)}) collective-permute-start(bf16[2,2,32,1536]{3,2,1,0:T(8,128)(2,1)S(1)} %collective-permute-done.2.refs_3_), channel_id=1, source_target_pairs={{0,1},{1,2},{2,3},{3,4},{4,5},{5,6},{6,7},{7,0},{16,23},{17,16},{1... | collective-permute-start | bytes 1179656 | tf_op jit(solution)/shard_map/ppermute | solution.py:32
  60.3 4.8 %collective-permute-start.10 = (bf16[2,2,32,1536]{3,2,1,0:T(8,128)(2,1)}, bf16[2,2,32,1536]{3,2,1,0:T(8,128)(2,1)}, u32[]{:S(2)}, u32[]{:S(2)}) collective-permute-start(bf16[2,2,32,1536]{3,2,1,0:T(8,128)(2,1)} %collective-permute-done.9), channel_id=1, source_target_pairs={{0,16},{16,0},{1,17},{17,1},{2,18},{18,2},{3,19},{19,3},{4,20},{20... | collective-permute-start | bytes 1179656 | tf_op jit(solution)/shard_map/ppermute | solution.py:21
  66.8 5.5 %collective-permute-start.11 = (f32[4,4,32,768]{3,2,1,0:T(8,128)S(1)}, f32[4,4,32,768]{3,2,1,0:T(8,128)S(1)}, u32[]{:S(2)}, u32[]{:S(2)}) collective-permute-start(f32[4,4,32,768]{3,2,1,0:T(8,128)S(1)} %shard_map.53), channel_id=1, source_target_pairs={{0,16},{16,0},{1,17},{17,1},{2,18},{18,2},{3,19},{19,3},{4,20},{20... | collective-permute-start | bytes 4718600 | tf_op jit(solution)/shard_map/ppermute | solution.py:21
  72.5 10.1 %collective-permute-start.13 = (f32[4,32,768]{2,1,0:T(8,128)S(1)}, f32[4,32,768]{2,1,0:T(8,128)S(1)}, u32[]{:S(2)}, u32[]{:S(2)}) collective-permute-start(f32[4,32,768]{2,1,0:T(8,128)S(1)} %get-tuple-element.41), channel_id=1, source_target_pairs={{0,128},{128,256},{256,384},{384,0},{16,400},{144,16},{272,144},{4... | collective-permute-start | bytes 1179656 | tf_op jit(solution)/shard_map/ppermute | solution.py:34
  74.8 11.0 %collective-permute-start.15 = (bf16[16,32,768]{2,1,0:T(8,128)(2,1)S(1)}, bf16[16,32,768]{2,1,0:T(8,128)(2,1)S(1)}, u32[]{:S(2)}, u32[]{:S(2)}) collective-permute-start(bf16[16,32,768]{2,1,0:T(8,128)(2,1)S(1)} %all-to-all-done), channel_id=1, source_target_pairs={{0,16},{16,0},{1,17},{17,1},{2,18},{18,2},{3,19},{19,3},{4,20},{20... | collective-permute-start | bytes 2359304 | tf_op jit(solution)/shard_map/ppermute | solution.py:21
  77.0 15.4 %collective-permute-start.12 = (f32[4,32,768]{2,1,0:T(8,128)S(1)}, f32[4,32,768]{2,1,0:T(8,128)S(1)}, u32[]{:S(2)}, u32[]{:S(2)}) collective-permute-start(f32[4,32,768]{2,1,0:T(8,128)S(1)} %get-tuple-element.40), channel_id=1, source_target_pairs={{0,384},{128,0},{256,128},{384,256},{16,144},{144,272},{272,400},{... | collective-permute-start | bytes 1179656 | tf_op jit(solution)/shard_map/ppermute | solution.py:34
  82.6 9.9 %collective-permute-start.14 = (f32[4,32,768]{2,1,0:T(8,128)S(1)}, f32[4,32,768]{2,1,0:T(8,128)S(1)}, u32[]{:S(2)}, u32[]{:S(2)}) collective-permute-start(f32[4,32,768]{2,1,0:T(8,128)S(1)} %fusion.2), channel_id=1, source_target_pairs={{0,128},{128,256},{256,384},{384,0},{16,400},{144,16},{272,144},{4... | collective-permute-start | bytes 1179656 | tf_op jit(solution)/shard_map/ppermute | solution.py:34

commit v6 on v5

--- a/solution.py
+++ b/solution.py
@@ -81,6 +81,22 @@
     )(weight)
 
 
+def copies_kernel(act, out):
+    for i in range(16):
+        out[i] = act[...]
+
+
+def copies(act):
+    return pl.pallas_call(
+        copies_kernel,
+        in_specs=[VMEM],
+        out_specs=VMEM,
+        out_shape=jax.ShapeDtypeStruct((16, 32, 768), jnp.bfloat16),
+        compiler_params=pltpu.CompilerParams(vmem_limit_bytes=8 * MIB),
+        cost_estimate=pl.CostEstimate(flops=0, bytes_accessed=MIB, transcendentals=0),
+    )(pltpu.with_memory_space_constraint(act, pltpu.HBM))
+
+
 def turn_kernel(place, act, sibling, out):
     for core, rows in ((place[0], act), (1 - place[0], sibling)):
         for yl in range(2):
@@ -130,7 +146,7 @@
     upstream, place = lax.optimization_barrier((upstream, place))
     weight = flip(up_weight)
 
-    act = lax.all_to_all(jnp.tile(activation, (16, 1)), ("x", "yh"), 0, 0, tiled=True)
+    act = lax.all_to_all(copies(activation), ("x", "yh"), 0, 0, tiled=True)
     mine = [lax.all_gather(upstream, "yl", axis=0, tiled=True).reshape(2, 2, 32, 1536)]
     other = [swap(mine[0], "core")]
     for step in range(3):
@@ -147,7 +163,6 @@
     start = sums(True, EARLY, place, weight, fixed([*mine[:4], *sides[:2]]))
     *held, start = lax.optimization_barrier((*mine, *sides, start))
     held = fixed(held)
-    act = act.reshape(16, 32, 768)
 
     theirs = swap(sums(True, LATE, place, weight, [held[4], held[7]], start), "core")
     ours = sums(False, HOPS, place, weight, held)

time: 114 us -> 114 us (level)
  local copies, waits for them, and re-layouts: 3.44 us -> 1.68 us
  Pallas kernels: 15 us -> 16.7 us
    another operation x1 -> x0, local copies, waits for them, and re-layouts: 1.76 us -> none  [on_device(): jnp.tile(activation, (16, 1))]
    pallas_call x0 -> x1, Pallas kernels: none -> 1.73 us  [copies(): pl.pallas_call(copies_kernel, in_specs=[VMEM], out_specs=VMEM, out_shape=...]
  transfers between devices with their start and end apart: 17 -> 17, of which waited for: 4 -> 4; matrix products, arithmetic and copies ran while one was open for 2% -> 0% of each run, Pallas kernels for 12% -> 13%
where the time goes in v6:
time: 114 us; the launch traced here: 113 us
  starting transfers between devices  60 us (53%)
  blocking collectives  27.3 us (24%)
  Pallas kernels  16.7 us (15%)
  waiting for transfers between devices  5.36 us (5%)
  local copies, waits for them, and re-layouts  1.68 us (1%)
    ppermute x7, starting transfers between devices, around(): return lax.ppermute(value, ('core', 'z'), pairs)  28 us
    all_to_all x1, blocking collectives, on_device(): total = lax.all_to_all(total, 'yh', 0, 0).sum(0)  19.8 us
    ppermute x6, starting transfers between devices, swap(): return lax.ppermute(value, axis, [(0, 1), (1, 0)])  13.3 us
    all_to_all x1, starting transfers between devices, on_device(): act = lax.all_to_all(copies(activation), ('x', 'yh'), 0, 0, tiled=True)  10.1 us
    ppermute x3, starting transfers between devices, around(): return lax.ppermute(value, (axis, 'core'), pairs)  8.63 us
    pallas_call x3, Pallas kernels, sums(): pl.pallas_call(functools.partial(sums_kernel, far, arrived), in_specs=[SM...  7.61 us
    all_gather x1, blocking collectives, on_device(): lax.all_gather(upstream, 'yl', axis=0, tiled=True).reshape(2, 2, 32, 1536)  7.52 us
    pallas_call x1, Pallas kernels, weight_gradient(): pl.pallas_call(weight_kernel, grid=(1536 // wide,), in_specs=[pl.BlockSpe...  5.72 us
  transfers between devices with their start and end apart: 17, of which 4 were waited for; matrix products, arithmetic and copies ran while one was open for 0% of the time, Pallas kernels for 13%

profile of v6, /device:TPU:6, one launch (start us, length us, event | category | flops | bytes accessed | tf_op | source)
XLA Modules:
  0.0 113.0 jit_solution(11761267956714710995)
XLA Ops:
  0.6 0.1 pad_add_fusion.place
  0.7 7.5 %all_gather.3 = bf16[128,1536]{1,0:T(8,128)(2,1)S(1)} all-gather(bf16[64,1536]{1,0:T(8,128)(2,1)} %param.4), channel_id=1, replica_groups=mesh['x'=4,'yh'=4,'core'=2,'yl'=2,'z'=8] {'yl'}, dimensions={0}, use_global_device_ids=true | all-gather | bytes 589824 | tf_op jit(solution)/shard_map/all_gather | solution.py:150
  8.2 1.9 %collective-permute-start.3 = (bf16[2,2,32,1536]{3,2,1,0:T(8,128)(2,1)S(1)}, bf16[2,2,32,1536]{3,2,1,0:T(8,128)(2,1)S(1)}, u32[]{:S(2)}, u32[]{:S(2)}) collective-permute-start(bf16[2,2,32,1536]{3,2,1,0:T(8,128)(2,1)S(1)} %bitcast.18), channel_id=1, source_target_pairs={{0,16},{16,0},{1,17},{17,1},{2,18},{18,2},{3,19},{19,3},{4,20},{20... | collective-permute-start | bytes 1179656 | tf_op jit(solution)/shard_map/ppermute | solution.py:21
  10.2 4.3 %collective-permute-start = (bf16[2,2,32,1536]{3,2,1,0:T(8,128)(2,1)S(1)}, bf16[2,2,32,1536]{3,2,1,0:T(8,128)(2,1)}, u32[]{:S(2)}, u32[]{:S(2)}) collective-permute-start(bf16[2,2,32,1536]{3,2,1,0:T(8,128)(2,1)S(1)} %bitcast.19), channel_id=1, source_target_pairs={{0,1},{1,2},{2,3},{3,4},{4,5},{5,6},{6,7},{7,0},{16,23},{17,16},{1... | collective-permute-start | bytes 1179656 | tf_op jit(solution)/shard_map/ppermute | solution.py:32
  14.4 0.0 collective-permute-done.3
  14.4 4.3 %collective-permute-start.4 = (bf16[2,2,32,1536]{3,2,1,0:T(8,128)(2,1)S(1)}, bf16[2,2,32,1536]{3,2,1,0:T(8,128)(2,1)}, u32[]{:S(2)}, u32[]{:S(2)}) collective-permute-start(bf16[2,2,32,1536]{3,2,1,0:T(8,128)(2,1)S(1)} %collective-permute-done.3), channel_id=1, source_target_pairs={{0,1},{1,2},{2,3},{3,4},{4,5},{5,6},{6,7},{7,0},{16,23},{17,16},{1... | collective-permute-start | bytes 1179656 | tf_op jit(solution)/shard_map/ppermute | solution.py:32
  18.7 1.7 %shard_map.51 = bf16[16,32,768]{2,1,0:T(8,128)(2,1)} custom-call(bf16[32,768]{1,0:T(8,128)(2,1)} %act.1), custom_call_target="tpu_custom_call" | custom-call | bytes 1048576 | tf_op jit(solution)/shard_map/pallas_call | solution.py:90
  20.5 10.1 %all-to-all-start = ((bf16[16,32,768]{2,1,0:T(8,128)(2,1)}), bf16[16,32,768]{2,1,0:T(8,128)(2,1)S(1)}, u32[]{:S(2)}, u32[]{:S(2)}) async-start(bf16[16,32,768]{2,1,0:T(8,128)(2,1)} %shard_map.51), calls=%async_computation | async-start | bytes 1572864 | tf_op jit(solution)/shard_map/all_to_all | solution.py:149
  30.5 0.0 collective-permute-done.refs_1_
  30.5 4.3 %collective-permute-start.1 = (bf16[2,2,32,1536]{3,2,1,0:T(8,128)(2,1)}, bf16[2,2,32,1536]{3,2,1,0:T(8,128)(2,1)S(1)}, u32[]{:S(2)}, u32[]{:S(2)}) collective-permute-start(bf16[2,2,32,1536]{3,2,1,0:T(8,128)(2,1)} %collective-permute-done.refs_1_), channel_id=1, source_target_pairs={{0,1},{1,2},{2,3},{3,4},{4,5},{5,6},{6,7},{7,0},{16,23},{17,16},{1... | collective-permute-start | bytes 1179656 | tf_op jit(solution)/shard_map/ppermute | solution.py:32
  34.8 0.0 collective-permute-done.4
  34.8 5.5 %collective-permute-start.7 = (bf16[2,2,32,1536]{3,2,1,0:T(8,128)(2,1)}, bf16[2,2,32,1536]{3,2,1,0:T(8,128)(2,1)}, u32[]{:S(2)}, u32[]{:S(2)}) collective-permute-start(bf16[2,2,32,1536]{3,2,1,0:T(8,128)(2,1)} %collective-permute-done.4), channel_id=1, source_target_pairs={{0,1},{1,2},{2,3},{3,4},{4,5},{5,6},{6,7},{7,0},{16,23},{17,16},{1... | collective-permute-start | bytes 1179656 | tf_op jit(solution)/shard_map/ppermute | solution.py:32
  40.3 0.0 copy-start
  40.3 1.7 %copy-done = bf16[768,1536]{1,0:T(8,128)(2,1)S(1)} copy-done((bf16[768,1536]{1,0:T(8,128)(2,1)S(1)}, bf16[768,1536]{1,0:T(8,128)(2,1)}, u32[]{:S(2)}) %copy-start) | copy-done | bytes 2359320
  42.0 0.7 shard_map.50.weight
  42.7 0.1 collective-permute-done.1.refs_2_
  42.8 3.3 %collective-permute-start.2 = (bf16[2,2,32,1536]{3,2,1,0:T(8,128)(2,1)S(1)}, bf16[2,2,32,1536]{3,2,1,0:T(8,128)(2,1)S(1)}, u32[]{:S(2)}, u32[]{:S(2)}) collective-permute-start(bf16[2,2,32,1536]{3,2,1,0:T(8,128)(2,1)S(1)} %collective-permute-done.1.refs_2_), channel_id=1, source_target_pairs={{0,1},{1,2},{2,3},{3,4},{4,5},{5,6},{6,7},{7,0},{16,23},{17,16},{1... | collective-permute-start | bytes 1179656 | tf_op jit(solution)/shard_map/ppermute | solution.py:32
  46.1 3.0 %collective-permute-start.5 = (bf16[2,2,32,1536]{3,2,1,0:T(8,128)(2,1)}, bf16[2,2,32,1536]{3,2,1,0:T(8,128)(2,1)S(1)}, u32[]{:S(2)}, u32[]{:S(2)}) collective-permute-start(bf16[2,2,32,1536]{3,2,1,0:T(8,128)(2,1)} %collective-permute-done.4), channel_id=1, source_target_pairs={{0,16},{16,0},{1,17},{17,1},{2,18},{18,2},{3,19},{19,3},{4,20},{20... | collective-permute-start | bytes 1179656 | tf_op jit(solution)/shard_map/ppermute | solution.py:21
  49.1 0.0 collective-permute-done.7
  49.1 3.0 %collective-permute-start.9 = (bf16[2,2,32,1536]{3,2,1,0:T(8,128)(2,1)}, bf16[2,2,32,1536]{3,2,1,0:T(8,128)(2,1)}, u32[]{:S(2)}, u32[]{:S(2)}) collective-permute-start(bf16[2,2,32,1536]{3,2,1,0:T(8,128)(2,1)} %collective-permute-done.7), channel_id=1, source_target_pairs={{0,1},{1,2},{2,3},{3,4},{4,5},{5,6},{6,7},{7,0},{16,23},{17,16},{1... | collective-permute-start | bytes 1179656 | tf_op jit(solution)/shard_map/ppermute | solution.py:32
  52.1 1.9 %collective-permute-start.8 = (bf16[2,2,32,1536]{3,2,1,0:T(8,128)(2,1)}, bf16[2,2,32,1536]{3,2,1,0:T(8,128)(2,1)}, u32[]{:S(2)}, u32[]{:S(2)}) collective-permute-start(bf16[2,2,32,1536]{3,2,1,0:T(8,128)(2,1)} %collective-permute-done.7), channel_id=1, source_target_pairs={{0,16},{16,0},{1,17},{17,1},{2,18},{18,2},{3,19},{19,3},{4,20},{20... | collective-permute-start | bytes 1179656 | tf_op jit(solution)/shard_map/ppermute | solution.py:21
  54.1 0.0 collective-permute-done.2.refs_3_
  54.1 0.0 collective-permute-done.5.refs_4_.refs_5_
  54.1 3.4 %collective-permute-start.6 = (bf16[2,2,32,1536]{3,2,1,0:T(8,128)(2,1)S(1)}, bf16[2,2,32,1536]{3,2,1,0:T(8,128)(2,1)}, u32[]{:S(2)}, u32[]{:S(2)}) collective-permute-start(bf16[2,2,32,1536]{3,2,1,0:T(8,128)(2,1)S(1)} %collective-permute-done.2.refs_3_), channel_id=1, source_target_pairs={{0,1},{1,2},{2,3},{3,4},{4,5},{5,6},{6,7},{7,0},{16,23},{17,16},{1... | collective-permute-start | bytes 1179656 | tf_op jit(solution)/shard_map/ppermute | solution.py:32
  57.5 2.8 %collective-permute-done.9 = bf16[2,2,32,1536]{3,2,1,0:T(8,128)(2,1)} collective-permute-done((bf16[2,2,32,1536]{3,2,1,0:T(8,128)(2,1)}, bf16[2,2,32,1536]{3,2,1,0:T(8,128)(2,1)}, u32[]{:S(2)}, u32[]{:S(2)}) %collective-permute-start.9) | collective-permute-done | bytes 393248 | tf_op jit(solution)/shard_map/ppermute | solution.py:32
  60.3 1.9 %collective-permute-start.10 = (bf16[2,2,32,1536]{3,2,1,0:T(8,128)(2,1)}, bf16[2,2,32,1536]{3,2,1,0:T(8,128)(2,1)}, u32[]{:S(2)}, u32[]{:S(2)}) collective-permute-start(bf16[2,2,32,1536]{3,2,1,0:T(8,128)(2,1)} %collective-permute-done.9), channel_id=1, source_target_pairs={{0,16},{16,0},{1,17},{17,1},{2,18},{18,2},{3,19},{19,3},{4,20},{20... | collective-permute-start | bytes 1179656 | tf_op jit(solution)/shard_map/ppermute | solution.py:21
  62.2 0.0 collective-permute-done.8.refs_5_.refs_6_
  62.3 2.7 %shard_map.52.refs_2_ = f32[4,4,32,768]{3,2,1,0:T(8,128)S(1)} custom-call(s32[3]{0:T(128)S(1)} %pad_add_fusion.place, bf16[1536,768]{1,0:T(8,128)(2,1)S(1)} %shard_map.50.weight, bf16[2,2,32,1536]{3,2,1,0:T(8,128)(2,1)} %bitcast.20, bf16[2,2,32,1536]{3,2,1,0:T(8,128)(2,1)} %collective-permute-done.refs_1_, bf16[2,2,32,1536]{3,2,1,0:T(8,128)(2,1)} %copy-done.2, ...), custom_call_target="tpu_custom_call" | custom-call | flops 905969664 | bytes 8388608 | tf_op jit(solution)/shard_map/pallas_call | solution.py:57
  64.9 0.2 collective-permute-done.6.refs_4_.refs_0_
  65.1 0.0 collective-permute-done.10.refs_7_.refs_1_
  65.1 1.7 %shard_map.54 = f32[4,4,32,768]{3,2,1,0:T(8,128)S(1)} custom-call(s32[3]{0:T(128)S(1)} %pad_add_fusion.place, bf16[1536,768]{1,0:T(8,128)(2,1)S(1)} %shard_map.50.weight, bf16[2,2,32,1536]{3,2,1,0:T(8,128)(2,1)} %collective-permute-done.6.refs_4_.refs_0_, bf16[2,2,32,1536]{3,2,1,0:T(8,128)(2,1)} %collective-permute-done.10.refs_7_.refs_1_, ...), custom_call_target="tpu_custom_call" | custom-call | flops 301989888 | bytes 8388608 | tf_op jit(solution)/shard_map/pallas_call | solution.py:57
  66.8 2.3 %collective-permute-start.11 = (f32[4,4,32,768]{3,2,1,0:T(8,128)S(1)}, f32[4,4,32,768]{3,2,1,0:T(8,128)S(1)}, u32[]{:S(2)}, u32[]{:S(2)}) collective-permute-start(f32[4,4,32,768]{3,2,1,0:T(8,128)S(1)} %shard_map.54), channel_id=1, source_target_pairs={{0,16},{16,0},{1,17},{17,1},{2,18},{18,2},{3,19},{19,3},{4,20},{20... | collective-permute-start | bytes 4718600 | tf_op jit(solution)/shard_map/ppermute | solution.py:21
  69.1 3.2 %shard_map.53 = f32[4,4,32,768]{3,2,1,0:T(8,128)S(1)} custom-call(s32[3]{0:T(128)S(1)} %pad_add_fusion.place, bf16[1536,768]{1,0:T(8,128)(2,1)S(1)} %shard_map.50.weight, bf16[2,2,32,1536]{3,2,1,0:T(8,128)(2,1)} %bitcast.21, bf16[2,2,32,1536]{3,2,1,0:T(8,128)(2,1)} %collective-permute-done.refs_1_, bf16[2,2,32,1536]{3,2,1,0:T(8,128)(2,1)} %copy-done.2, ...), custom_call_target="tpu_custom_call" | custom-call | flops 1207959552 | bytes 8388608 | tf_op jit(solution)/shard_map/pallas_call | solution.py:57
  72.3 0.0 collective-permute-done.11
  72.3 0.1 fusion.3
  72.4 2.3 %collective-permute-start.13 = (f32[4,32,768]{2,1,0:T(8,128)S(1)}, f32[4,32,768]{2,1,0:T(8,128)S(1)}, u32[]{:S(2)}, u32[]{:S(2)}) collective-permute-start(f32[4,32,768]{2,1,0:T(8,128)S(1)} %get-tuple-element.41), channel_id=1, source_target_pairs={{0,128},{128,256},{256,384},{384,0},{16,400},{144,16},{272,144},{4... | collective-permute-start | bytes 1179656 | tf_op jit(solution)/shard_map/ppermute | solution.py:34
  74.7 2.3 %collective-permute-start.15 = (bf16[16,32,768]{2,1,0:T(8,128)(2,1)S(1)}, bf16[16,32,768]{2,1,0:T(8,128)(2,1)S(1)}, u32[]{:S(2)}, u32[]{:S(2)}) collective-permute-start(bf16[16,32,768]{2,1,0:T(8,128)(2,1)S(1)} %all-to-all-done.act), channel_id=1, source_target_pairs={{0,16},{16,0},{1,17},{17,1},{2,18},{18,2},{3,19},{19,3},{4,20},{20... | collective-permute-start | bytes 2359304 | tf_op jit(solution)/shard_map/ppermute | solution.py:21
  77.0 3.2 %collective-permute-start.12 = (f32[4,32,768]{2,1,0:T(8,128)S(1)}, f32[4,32,768]{2,1,0:T(8,128)S(1)}, u32[]{:S(2)}, u32[]{:S(2)}) collective-permute-start(f32[4,32,768]{2,1,0:T(8,128)S(1)} %get-tuple-element.40), channel_id=1, source_target_pairs={{0,384},{128,0},{256,128},{384,256},{16,144},{144,272},{272,400},{... | collective-permute-start | bytes 1179656 | tf_op jit(solution)/shard_map/ppermute | solution.py:34
  80.2 2.3 %collective-permute-done.13 = f32[4,32,768]{2,1,0:T(8,128)S(1)} collective-permute-done((f32[4,32,768]{2,1,0:T(8,128)S(1)}, f32[4,32,768]{2,1,0:T(8,128)S(1)}, u32[]{:S(2)}, u32[]{:S(2)}) %collective-permute-start.13) | collective-permute-done | bytes 393248 | tf_op jit(solution)/shard_map/ppermute | solution.py:34
  82.5 0.1 fusion.2
  82.6 3.1 %collective-permute-start.14 = (f32[4,32,768]{2,1,0:T(8,128)S(1)}, f32[4,32,768]{2,1,0:T(8,128)S(1)}, u32[]{:S(2)}, u32[]{:S(2)}) collective-permute-start(f32[4,32,768]{2,1,0:T(8,128)S(1)} %fusion.2), channel_id=1, source_target_pairs={{0,128},{128,256},{256,384},{384,0},{16,400},{144,16},{272,144},{4... | collective-permute-start | bytes 1179656 | tf_op jit(solution)/shard_map/ppermute | solution.py:34
  85.7 0.0 collective-permute-done.15.sibling
  85.7 1.0 shard_map.55.turned
  86.7 5.7 %shard_map.56 = bf16[768,1536]{1,0:T(8,128)(2,1)} custom-call(bf16[2,2,768,256]{3,2,1,0:T(8,128)(2,1)S(1)} %shard_map.55.turned, bf16[2,2,32,1536]{3,2,1,0:T(8,128)(2,1)} %bitcast.22, bf16[2,2,32,1536]{3,2,1,0:T(8,128)(2,1)} %collective-permute-done.refs_1_, bf16[2,2,32,1536]{3,2,1,0:T(8,128)(2,1)} %copy-done.2, bf16[2,2,32,1536]{3,2,1,0:T(8,128)(2,1)} %copy-done.3, ...), custom_call_target="tpu_custom_call" | custom-call | flops 2415919104 | bytes 7340032 | tf_op jit(solution)/shard_map/pallas_call | solution.py:130
  92.4 0.0 collective-permute-done.14
  92.5 0.1 fusion.6
  92.5 19.8 %all_to_all.10 = f32[4,32,768]{2,1,0:T(8,128)S(1)} all-to-all(f32[4,32,768]{2,1,0:T(8,128)S(1)} %fusion.6), channel_id=1, replica_groups=mesh['x'=4,'yh'=4,'core'=2,'yl'=2,'z'=8] {'yh'}, dimensions={0} | all-to-all | bytes 786432 | tf_op jit(solution)/shard_map/all_to_all | solution.py:176
  112.3 0.6 reduce_sum.9
  (10 shorter events, 0.0 us)
Async XLA Ops:
  8.2 34.4 %copy-start.1 = (bf16[128,1536]{1,0:T(8,128)(2,1)}, bf16[128,1536]{1,0:T(8,128)(2,1)S(1)}, u32[]{:S(2)}) copy-start(bf16[128,1536]{1,0:T(8,128)(2,1)S(1)} %all_gather.3) | copy-start | bytes 1179652
  8.2 6.2 %collective-permute-start.3 = (bf16[2,2,32,1536]{3,2,1,0:T(8,128)(2,1)S(1)}, bf16[2,2,32,1536]{3,2,1,0:T(8,128)(2,1)S(1)}, u32[]{:S(2)}, u32[]{:S(2)}) collective-permute-start(bf16[2,2,32,1536]{3,2,1,0:T(8,128)(2,1)S(1)} %bitcast.18), channel_id=1, source_target_pairs={{0,16},{16,0},{1,17},{17,1},{2,18},{18,2},{3,19},{19,3},{4,20},{20... | collective-permute-start | bytes 1179656 | tf_op jit(solution)/shard_map/ppermute | solution.py:21
  10.2 20.4 %collective-permute-start = (bf16[2,2,32,1536]{3,2,1,0:T(8,128)(2,1)S(1)}, bf16[2,2,32,1536]{3,2,1,0:T(8,128)(2,1)}, u32[]{:S(2)}, u32[]{:S(2)}) collective-permute-start(bf16[2,2,32,1536]{3,2,1,0:T(8,128)(2,1)S(1)} %bitcast.19), channel_id=1, source_target_pairs={{0,1},{1,2},{2,3},{3,4},{4,5},{5,6},{6,7},{7,0},{16,23},{17,16},{1... | collective-permute-start | bytes 1179656 | tf_op jit(solution)/shard_map/ppermute | solution.py:32
  14.4 20.4 %collective-permute-start.4 = (bf16[2,2,32,1536]{3,2,1,0:T(8,128)(2,1)S(1)}, bf16[2,2,32,1536]{3,2,1,0:T(8,128)(2,1)}, u32[]{:S(2)}, u32[]{:S(2)}) collective-permute-start(bf16[2,2,32,1536]{3,2,1,0:T(8,128)(2,1)S(1)} %collective-permute-done.3), channel_id=1, source_target_pairs={{0,1},{1,2},{2,3},{3,4},{4,5},{5,6},{6,7},{7,0},{16,23},{17,16},{1... | collective-permute-start | bytes 1179656 | tf_op jit(solution)/shard_map/ppermute | solution.py:32
  20.5 41.8 %all-to-all-start = ((bf16[16,32,768]{2,1,0:T(8,128)(2,1)}), bf16[16,32,768]{2,1,0:T(8,128)(2,1)S(1)}, u32[]{:S(2)}, u32[]{:S(2)}) async-start(bf16[16,32,768]{2,1,0:T(8,128)(2,1)} %shard_map.51), calls=%async_computation | async-start | bytes 1572864 | tf_op jit(solution)/shard_map/all_to_all | solution.py:149
  30.5 12.2 %collective-permute-start.1 = (bf16[2,2,32,1536]{3,2,1,0:T(8,128)(2,1)}, bf16[2,2,32,1536]{3,2,1,0:T(8,128)(2,1)S(1)}, u32[]{:S(2)}, u32[]{:S(2)}) collective-permute-start(bf16[2,2,32,1536]{3,2,1,0:T(8,128)(2,1)} %collective-permute-done.refs_1_), channel_id=1, source_target_pairs={{0,1},{1,2},{2,3},{3,4},{4,5},{5,6},{6,7},{7,0},{16,23},{17,16},{1... | collective-permute-start | bytes 1179656 | tf_op jit(solution)/shard_map/ppermute | solution.py:32
  34.8 14.3 %collective-permute-start.7 = (bf16[2,2,32,1536]{3,2,1,0:T(8,128)(2,1)}, bf16[2,2,32,1536]{3,2,1,0:T(8,128)(2,1)}, u32[]{:S(2)}, u32[]{:S(2)}) collective-permute-start(bf16[2,2,32,1536]{3,2,1,0:T(8,128)(2,1)} %collective-permute-done.4), channel_id=1, source_target_pairs={{0,1},{1,2},{2,3},{3,4},{4,5},{5,6},{6,7},{7,0},{16,23},{17,16},{1... | collective-permute-start | bytes 1179656 | tf_op jit(solution)/shard_map/ppermute | solution.py:32
  40.3 1.7 %copy-start = (bf16[768,1536]{1,0:T(8,128)(2,1)S(1)}, bf16[768,1536]{1,0:T(8,128)(2,1)}, u32[]{:S(2)}) copy-start(bf16[768,1536]{1,0:T(8,128)(2,1)} %weight.1) | copy-start | bytes 7077892
  42.8 17.5 %copy-start.2 = (bf16[2,2,32,1536]{3,2,1,0:T(8,128)(2,1)}, bf16[2,2,32,1536]{3,2,1,0:T(8,128)(2,1)S(1)}, u32[]{:S(2)}) copy-start(bf16[2,2,32,1536]{3,2,1,0:T(8,128)(2,1)S(1)} %collective-permute-done.1.refs_2_) | copy-start | bytes 1179652
  42.8 11.3 %collective-permute-start.2 = (bf16[2,2,32,1536]{3,2,1,0:T(8,128)(2,1)S(1)}, bf16[2,2,32,1536]{3,2,1,0:T(8,128)(2,1)S(1)}, u32[]{:S(2)}, u32[]{:S(2)}) collective-permute-start(bf16[2,2,32,1536]{3,2,1,0:T(8,128)(2,1)S(1)} %collective-permute-done.1.refs_2_), channel_id=1, source_target_pairs={{0,1},{1,2},{2,3},{3,4},{4,5},{5,6},{6,7},{7,0},{16,23},{17,16},{1... | collective-permute-start | bytes 1179656 | tf_op jit(solution)/shard_map/ppermute | solution.py:32
  46.1 8.0 %collective-permute-start.5 = (bf16[2,2,32,1536]{3,2,1,0:T(8,128)(2,1)}, bf16[2,2,32,1536]{3,2,1,0:T(8,128)(2,1)S(1)}, u32[]{:S(2)}, u32[]{:S(2)}) collective-permute-start(bf16[2,2,32,1536]{3,2,1,0:T(8,128)(2,1)} %collective-permute-done.4), channel_id=1, source_target_pairs={{0,16},{16,0},{1,17},{17,1},{2,18},{18,2},{3,19},{19,3},{4,20},{20... | collective-permute-start | bytes 1179656 | tf_op jit(solution)/shard_map/ppermute | solution.py:21
  49.1 11.2 %collective-permute-start.9 = (bf16[2,2,32,1536]{3,2,1,0:T(8,128)(2,1)}, bf16[2,2,32,1536]{3,2,1,0:T(8,128)(2,1)}, u32[]{:S(2)}, u32[]{:S(2)}) collective-permute-start(bf16[2,2,32,1536]{3,2,1,0:T(8,128)(2,1)} %collective-permute-done.7), channel_id=1, source_target_pairs={{0,1},{1,2},{2,3},{3,4},{4,5},{5,6},{6,7},{7,0},{16,23},{17,16},{1... | collective-permute-start | bytes 1179656 | tf_op jit(solution)/shard_map/ppermute | solution.py:32
  52.1 10.1 %collective-permute-start.8 = (bf16[2,2,32,1536]{3,2,1,0:T(8,128)(2,1)}, bf16[2,2,32,1536]{3,2,1,0:T(8,128)(2,1)}, u32[]{:S(2)}, u32[]{:S(2)}) collective-permute-start(bf16[2,2,32,1536]{3,2,1,0:T(8,128)(2,1)} %collective-permute-done.7), channel_id=1, source_target_pairs={{0,16},{16,0},{1,17},{17,1},{2,18},{18,2},{3,19},{19,3},{4,20},{20... | collective-permute-start | bytes 1179656 | tf_op jit(solution)/shard_map/ppermute | solution.py:21
  54.1 8.2 %copy-start.3 = (bf16[2,2,32,1536]{3,2,1,0:T(8,128)(2,1)}, bf16[2,2,32,1536]{3,2,1,0:T(8,128)(2,1)S(1)}, u32[]{:S(2)}) copy-start(bf16[2,2,32,1536]{3,2,1,0:T(8,128)(2,1)S(1)} %collective-permute-done.2.refs_3_) | copy-start | bytes 1179652
  54.1 6.2 %copy-start.4 = (bf16[2,2,32,1536]{3,2,1,0:T(8,128)(2,1)}, bf16[2,2,32,1536]{3,2,1,0:T(8,128)(2,1)S(1)}, u32[]{:S(2)}) copy-start(bf16[2,2,32,1536]{3,2,1,0:T(8,128)(2,1)S(1)} %collective-permute-done.5.refs_4_.refs_5_) | copy-start | bytes 1179652
  54.1 11.0 %collective-permute-start.6 = (bf16[2,2,32,1536]{3,2,1,0:T(8,128)(2,1)S(1)}, bf16[2,2,32,1536]{3,2,1,0:T(8,128)(2,1)}, u32[]{:S(2)}, u32[]{:S(2)}) collective-permute-start(bf16[2,2,32,1536]{3,2,1,0:T(8,128)(2,1)S(1)} %collective-permute-done.2.refs_3_), channel_id=1, source_target_pairs={{0,1},{1,2},{2,3},{3,4},{4,5},{5,6},{6,7},{7,0},{16,23},{17,16},{1... | collective-permute-start | bytes 1179656 | tf_op jit(solution)/shard_map/ppermute | solution.py:32
  60.3 4.8 %collective-permute-start.10 = (bf16[2,2,32,1536]{3,2,1,0:T(8,128)(2,1)}, bf16[2,2,32,1536]{3,2,1,0:T(8,128)(2,1)}, u32[]{:S(2)}, u32[]{:S(2)}) collective-permute-start(bf16[2,2,32,1536]{3,2,1,0:T(8,128)(2,1)} %collective-permute-done.9), channel_id=1, source_target_pairs={{0,16},{16,0},{1,17},{17,1},{2,18},{18,2},{3,19},{19,3},{4,20},{20... | collective-permute-start | bytes 1179656 | tf_op jit(solution)/shard_map/ppermute | solution.py:21
  66.8 5.5 %collective-permute-start.11 = (f32[4,4,32,768]{3,2,1,0:T(8,128)S(1)}, f32[4,4,32,768]{3,2,1,0:T(8,128)S(1)}, u32[]{:S(2)}, u32[]{:S(2)}) collective-permute-start(f32[4,4,32,768]{3,2,1,0:T(8,128)S(1)} %shard_map.54), channel_id=1, source_target_pairs={{0,16},{16,0},{1,17},{17,1},{2,18},{18,2},{3,19},{19,3},{4,20},{20... | collective-permute-start | bytes 4718600 | tf_op jit(solution)/shard_map/ppermute | solution.py:21
  72.4 10.1 %collective-permute-start.13 = (f32[4,32,768]{2,1,0:T(8,128)S(1)}, f32[4,32,768]{2,1,0:T(8,128)S(1)}, u32[]{:S(2)}, u32[]{:S(2)}) collective-permute-start(f32[4,32,768]{2,1,0:T(8,128)S(1)} %get-tuple-element.41), channel_id=1, source_target_pairs={{0,128},{128,256},{256,384},{384,0},{16,400},{144,16},{272,144},{4... | collective-permute-start | bytes 1179656 | tf_op jit(solution)/shard_map/ppermute | solution.py:34
  74.7 11.0 %collective-permute-start.15 = (bf16[16,32,768]{2,1,0:T(8,128)(2,1)S(1)}, bf16[16,32,768]{2,1,0:T(8,128)(2,1)S(1)}, u32[]{:S(2)}, u32[]{:S(2)}) collective-permute-start(bf16[16,32,768]{2,1,0:T(8,128)(2,1)S(1)} %all-to-all-done.act), channel_id=1, source_target_pairs={{0,16},{16,0},{1,17},{17,1},{2,18},{18,2},{3,19},{19,3},{4,20},{20... | collective-permute-start | bytes 2359304 | tf_op jit(solution)/shard_map/ppermute | solution.py:21
  77.0 15.5 %collective-permute-start.12 = (f32[4,32,768]{2,1,0:T(8,128)S(1)}, f32[4,32,768]{2,1,0:T(8,128)S(1)}, u32[]{:S(2)}, u32[]{:S(2)}) collective-permute-start(f32[4,32,768]{2,1,0:T(8,128)S(1)} %get-tuple-element.40), channel_id=1, source_target_pairs={{0,384},{128,0},{256,128},{384,256},{16,144},{144,272},{272,400},{... | collective-permute-start | bytes 1179656 | tf_op jit(solution)/shard_map/ppermute | solution.py:34
  82.6 9.9 %collective-permute-start.14 = (f32[4,32,768]{2,1,0:T(8,128)S(1)}, f32[4,32,768]{2,1,0:T(8,128)S(1)}, u32[]{:S(2)}, u32[]{:S(2)}) collective-permute-start(f32[4,32,768]{2,1,0:T(8,128)S(1)} %fusion.2), channel_id=1, source_target_pairs={{0,128},{128,256},{256,384},{384,0},{16,400},{144,16},{272,144},{4... | collective-permute-start | bytes 1179656 | tf_op jit(solution)/shard_map/ppermute | solution.py:34

commit v7 on v6

--- a/solution.py
+++ b/solution.py
@@ -126,7 +126,7 @@
 
 
 def weight_gradient(turned, held):
-    wide = 512
+    wide = 768
     return pl.pallas_call(
         weight_kernel,
         grid=(1536 // wide,),

time: 114 us -> 114 us (level)
  transfers between devices with their start and end apart: 17 -> 17, of which waited for: 4 -> 5; matrix products, arithmetic and copies ran while one was open for 0% -> 0% of each run, Pallas kernels for 13% -> 13%
where the time goes in v7:
time: 114 us; the launch traced here: 113 us
  starting transfers between devices  60 us (53%)
  blocking collectives  27.5 us (24%)
  Pallas kernels  16.3 us (14%)
  waiting for transfers between devices  5.55 us (5%)
  local copies, waits for them, and re-layouts  1.68 us (1%)
    ppermute x7, starting transfers between devices, around(): return lax.ppermute(value, ('core', 'z'), pairs)  28 us
    all_to_all x1, blocking collectives, on_device(): total = lax.all_to_all(total, 'yh', 0, 0).sum(0)  20 us
    ppermute x6, starting transfers between devices, swap(): return lax.ppermute(value, axis, [(0, 1), (1, 0)])  13.3 us
    all_to_all x1, starting transfers between devices, on_device(): act = lax.all_to_all(copies(activation), ('x', 'yh'), 0, 0, tiled=True)  10.1 us
    ppermute x3, starting transfers between devices, around(): return lax.ppermute(value, (axis, 'core'), pairs)  8.63 us
    pallas_call x3, Pallas kernels, sums(): pl.pallas_call(functools.partial(sums_kernel, far, arrived), in_specs=[SM...  7.61 us
    all_gather x1, blocking collectives, on_device(): lax.all_gather(upstream, 'yl', axis=0, tiled=True).reshape(2, 2, 32, 1536)  7.52 us
    pallas_call x1, Pallas kernels, weight_gradient(): pl.pallas_call(weight_kernel, grid=(1536 // wide,), in_specs=[pl.BlockSpe...  5.33 us
  transfers between devices with their start and end apart: 17, of which 5 were waited for; matrix products, arithmetic and copies ran while one was open for 0% of the time, Pallas kernels for 13%

profile of v7, /device:TPU:6, one launch (start us, length us, event | category | flops | bytes accessed | tf_op | source)
XLA Modules:
  0.0 113.0 jit_solution(3722686576712454912)
XLA Ops:
  0.6 0.1 pad_add_fusion.place
  0.7 7.5 %all_gather.3 = bf16[128,1536]{1,0:T(8,128)(2,1)S(1)} all-gather(bf16[64,1536]{1,0:T(8,128)(2,1)} %param.4), channel_id=1, replica_groups=mesh['x'=4,'yh'=4,'core'=2,'yl'=2,'z'=8] {'yl'}, dimensions={0}, use_global_device_ids=true | all-gather | bytes 589824 | tf_op jit(solution)/shard_map/all_gather | solution.py:150
  8.2 1.9 %collective-permute-start.3 = (bf16[2,2,32,1536]{3,2,1,0:T(8,128)(2,1)S(1)}, bf16[2,2,32,1536]{3,2,1,0:T(8,128)(2,1)S(1)}, u32[]{:S(2)}, u32[]{:S(2)}) collective-permute-start(bf16[2,2,32,1536]{3,2,1,0:T(8,128)(2,1)S(1)} %bitcast.18), channel_id=1, source_target_pairs={{0,16},{16,0},{1,17},{17,1},{2,18},{18,2},{3,19},{19,3},{4,20},{20... | collective-permute-start | bytes 1179656 | tf_op jit(solution)/shard_map/ppermute | solution.py:21
  10.2 4.3 %collective-permute-start = (bf16[2,2,32,1536]{3,2,1,0:T(8,128)(2,1)S(1)}, bf16[2,2,32,1536]{3,2,1,0:T(8,128)(2,1)}, u32[]{:S(2)}, u32[]{:S(2)}) collective-permute-start(bf16[2,2,32,1536]{3,2,1,0:T(8,128)(2,1)S(1)} %bitcast.19), channel_id=1, source_target_pairs={{0,1},{1,2},{2,3},{3,4},{4,5},{5,6},{6,7},{7,0},{16,23},{17,16},{1... | collective-permute-start | bytes 1179656 | tf_op jit(solution)/shard_map/ppermute | solution.py:32
  14.4 0.0 collective-permute-done.3
  14.4 4.3 %collective-permute-start.4 = (bf16[2,2,32,1536]{3,2,1,0:T(8,128)(2,1)S(1)}, bf16[2,2,32,1536]{3,2,1,0:T(8,128)(2,1)}, u32[]{:S(2)}, u32[]{:S(2)}) collective-permute-start(bf16[2,2,32,1536]{3,2,1,0:T(8,128)(2,1)S(1)} %collective-permute-done.3), channel_id=1, source_target_pairs={{0,1},{1,2},{2,3},{3,4},{4,5},{5,6},{6,7},{7,0},{16,23},{17,16},{1... | collective-permute-start | bytes 1179656 | tf_op jit(solution)/shard_map/ppermute | solution.py:32
  18.7 1.7 %shard_map.51 = bf16[16,32,768]{2,1,0:T(8,128)(2,1)} custom-call(bf16[32,768]{1,0:T(8,128)(2,1)} %act.1), custom_call_target="tpu_custom_call" | custom-call | bytes 1048576 | tf_op jit(solution)/shard_map/pallas_call | solution.py:90
  20.5 10.1 %all-to-all-start = ((bf16[16,32,768]{2,1,0:T(8,128)(2,1)}), bf16[16,32,768]{2,1,0:T(8,128)(2,1)S(1)}, u32[]{:S(2)}, u32[]{:S(2)}) async-start(bf16[16,32,768]{2,1,0:T(8,128)(2,1)} %shard_map.51), calls=%async_computation | async-start | bytes 1572864 | tf_op jit(solution)/shard_map/all_to_all | solution.py:149
  30.5 0.0 collective-permute-done.refs_1_
  30.5 4.3 %collective-permute-start.1 = (bf16[2,2,32,1536]{3,2,1,0:T(8,128)(2,1)}, bf16[2,2,32,1536]{3,2,1,0:T(8,128)(2,1)S(1)}, u32[]{:S(2)}, u32[]{:S(2)}) collective-permute-start(bf16[2,2,32,1536]{3,2,1,0:T(8,128)(2,1)} %collective-permute-done.refs_1_), channel_id=1, source_target_pairs={{0,1},{1,2},{2,3},{3,4},{4,5},{5,6},{6,7},{7,0},{16,23},{17,16},{1... | collective-permute-start | bytes 1179656 | tf_op jit(solution)/shard_map/ppermute | solution.py:32
  34.8 0.0 collective-permute-done.4
  34.8 5.5 %collective-permute-start.7 = (bf16[2,2,32,1536]{3,2,1,0:T(8,128)(2,1)}, bf16[2,2,32,1536]{3,2,1,0:T(8,128)(2,1)}, u32[]{:S(2)}, u32[]{:S(2)}) collective-permute-start(bf16[2,2,32,1536]{3,2,1,0:T(8,128)(2,1)} %collective-permute-done.4), channel_id=1, source_target_pairs={{0,1},{1,2},{2,3},{3,4},{4,5},{5,6},{6,7},{7,0},{16,23},{17,16},{1... | collective-permute-start | bytes 1179656 | tf_op jit(solution)/shard_map/ppermute | solution.py:32
  40.3 0.0 copy-start
  40.3 1.7 %copy-done = bf16[768,1536]{1,0:T(8,128)(2,1)S(1)} copy-done((bf16[768,1536]{1,0:T(8,128)(2,1)S(1)}, bf16[768,1536]{1,0:T(8,128)(2,1)}, u32[]{:S(2)}) %copy-start) | copy-done | bytes 2359320
  42.0 0.7 shard_map.50.weight
  42.7 0.1 collective-permute-done.1.refs_2_
  42.8 3.3 %collective-permute-start.2 = (bf16[2,2,32,1536]{3,2,1,0:T(8,128)(2,1)S(1)}, bf16[2,2,32,1536]{3,2,1,0:T(8,128)(2,1)S(1)}, u32[]{:S(2)}, u32[]{:S(2)}) collective-permute-start(bf16[2,2,32,1536]{3,2,1,0:T(8,128)(2,1)S(1)} %collective-permute-done.1.refs_2_), channel_id=1, source_target_pairs={{0,1},{1,2},{2,3},{3,4},{4,5},{5,6},{6,7},{7,0},{16,23},{17,16},{1... | collective-permute-start | bytes 1179656 | tf_op jit(solution)/shard_map/ppermute | solution.py:32
  46.1 3.0 %collective-permute-start.5 = (bf16[2,2,32,1536]{3,2,1,0:T(8,128)(2,1)}, bf16[2,2,32,1536]{3,2,1,0:T(8,128)(2,1)S(1)}, u32[]{:S(2)}, u32[]{:S(2)}) collective-permute-start(bf16[2,2,32,1536]{3,2,1,0:T(8,128)(2,1)} %collective-permute-done.4), channel_id=1, source_target_pairs={{0,16},{16,0},{1,17},{17,1},{2,18},{18,2},{3,19},{19,3},{4,20},{20... | collective-permute-start | bytes 1179656 | tf_op jit(solution)/shard_map/ppermute | solution.py:21
  49.1 0.0 collective-permute-done.7
  49.1 3.0 %collective-permute-start.9 = (bf16[2,2,32,1536]{3,2,1,0:T(8,128)(2,1)}, bf16[2,2,32,1536]{3,2,1,0:T(8,128)(2,1)}, u32[]{:S(2)}, u32[]{:S(2)}) collective-permute-start(bf16[2,2,32,1536]{3,2,1,0:T(8,128)(2,1)} %collective-permute-done.7), channel_id=1, source_target_pairs={{0,1},{1,2},{2,3},{3,4},{4,5},{5,6},{6,7},{7,0},{16,23},{17,16},{1... | collective-permute-start | bytes 1179656 | tf_op jit(solution)/shard_map/ppermute | solution.py:32
  52.1 1.9 %collective-permute-start.8 = (bf16[2,2,32,1536]{3,2,1,0:T(8,128)(2,1)}, bf16[2,2,32,1536]{3,2,1,0:T(8,128)(2,1)}, u32[]{:S(2)}, u32[]{:S(2)}) collective-permute-start(bf16[2,2,32,1536]{3,2,1,0:T(8,128)(2,1)} %collective-permute-done.7), channel_id=1, source_target_pairs={{0,16},{16,0},{1,17},{17,1},{2,18},{18,2},{3,19},{19,3},{4,20},{20... | collective-permute-start | bytes 1179656 | tf_op jit(solution)/shard_map/ppermute | solution.py:21
  54.1 0.0 collective-permute-done.2.refs_3_
  54.1 0.0 collective-permute-done.5.refs_4_.refs_5_
  54.1 3.4 %collective-permute-start.6 = (bf16[2,2,32,1536]{3,2,1,0:T(8,128)(2,1)S(1)}, bf16[2,2,32,1536]{3,2,1,0:T(8,128)(2,1)}, u32[]{:S(2)}, u32[]{:S(2)}) collective-permute-start(bf16[2,2,32,1536]{3,2,1,0:T(8,128)(2,1)S(1)} %collective-permute-done.2.refs_3_), channel_id=1, source_target_pairs={{0,1},{1,2},{2,3},{3,4},{4,5},{5,6},{6,7},{7,0},{16,23},{17,16},{1... | collective-permute-start | bytes 1179656 | tf_op jit(solution)/shard_map/ppermute | solution.py:32
  57.5 2.8 %collective-permute-done.9 = bf16[2,2,32,1536]{3,2,1,0:T(8,128)(2,1)} collective-permute-done((bf16[2,2,32,1536]{3,2,1,0:T(8,128)(2,1)}, bf16[2,2,32,1536]{3,2,1,0:T(8,128)(2,1)}, u32[]{:S(2)}, u32[]{:S(2)}) %collective-permute-start.9) | collective-permute-done | bytes 393248 | tf_op jit(solution)/shard_map/ppermute | solution.py:32
  60.3 1.9 %collective-permute-start.10 = (bf16[2,2,32,1536]{3,2,1,0:T(8,128)(2,1)}, bf16[2,2,32,1536]{3,2,1,0:T(8,128)(2,1)}, u32[]{:S(2)}, u32[]{:S(2)}) collective-permute-start(bf16[2,2,32,1536]{3,2,1,0:T(8,128)(2,1)} %collective-permute-done.9), channel_id=1, source_target_pairs={{0,16},{16,0},{1,17},{17,1},{2,18},{18,2},{3,19},{19,3},{4,20},{20... | collective-permute-start | bytes 1179656 | tf_op jit(solution)/shard_map/ppermute | solution.py:21
  62.2 0.0 collective-permute-done.8.refs_5_.refs_6_
  62.3 2.7 %shard_map.52.refs_2_ = f32[4,4,32,768]{3,2,1,0:T(8,128)S(1)} custom-call(s32[3]{0:T(128)S(1)} %pad_add_fusion.place, bf16[1536,768]{1,0:T(8,128)(2,1)S(1)} %shard_map.50.weight, bf16[2,2,32,1536]{3,2,1,0:T(8,128)(2,1)} %bitcast.20, bf16[2,2,32,1536]{3,2,1,0:T(8,128)(2,1)} %collective-permute-done.refs_1_, bf16[2,2,32,1536]{3,2,1,0:T(8,128)(2,1)} %copy-done.2, ...), custom_call_target="tpu_custom_call" | custom-call | flops 905969664 | bytes 8388608 | tf_op jit(solution)/shard_map/pallas_call | solution.py:57
  64.9 0.2 collective-permute-done.6.refs_4_.refs_0_
  65.1 0.0 collective-permute-done.10.refs_7_.refs_1_
  65.1 1.7 %shard_map.54 = f32[4,4,32,768]{3,2,1,0:T(8,128)S(1)} custom-call(s32[3]{0:T(128)S(1)} %pad_add_fusion.place, bf16[1536,768]{1,0:T(8,128)(2,1)S(1)} %shard_map.50.weight, bf16[2,2,32,1536]{3,2,1,0:T(8,128)(2,1)} %collective-permute-done.6.refs_4_.refs_0_, bf16[2,2,32,1536]{3,2,1,0:T(8,128)(2,1)} %collective-permute-done.10.refs_7_.refs_1_, ...), custom_call_target="tpu_custom_call" | custom-call | flops 301989888 | bytes 8388608 | tf_op jit(solution)/shard_map/pallas_call | solution.py:57
  66.8 2.3 %collective-permute-start.11 = (f32[4,4,32,768]{3,2,1,0:T(8,128)S(1)}, f32[4,4,32,768]{3,2,1,0:T(8,128)S(1)}, u32[]{:S(2)}, u32[]{:S(2)}) collective-permute-start(f32[4,4,32,768]{3,2,1,0:T(8,128)S(1)} %shard_map.54), channel_id=1, source_target_pairs={{0,16},{16,0},{1,17},{17,1},{2,18},{18,2},{3,19},{19,3},{4,20},{20... | collective-permute-start | bytes 4718600 | tf_op jit(solution)/shard_map/ppermute | solution.py:21
  69.1 3.2 %shard_map.53 = f32[4,4,32,768]{3,2,1,0:T(8,128)S(1)} custom-call(s32[3]{0:T(128)S(1)} %pad_add_fusion.place, bf16[1536,768]{1,0:T(8,128)(2,1)S(1)} %shard_map.50.weight, bf16[2,2,32,1536]{3,2,1,0:T(8,128)(2,1)} %bitcast.21, bf16[2,2,32,1536]{3,2,1,0:T(8,128)(2,1)} %collective-permute-done.refs_1_, bf16[2,2,32,1536]{3,2,1,0:T(8,128)(2,1)} %copy-done.2, ...), custom_call_target="tpu_custom_call" | custom-call | flops 1207959552 | bytes 8388608 | tf_op jit(solution)/shard_map/pallas_call | solution.py:57
  72.3 0.0 collective-permute-done.11
  72.3 0.1 fusion.3
  72.4 2.3 %collective-permute-start.13 = (f32[4,32,768]{2,1,0:T(8,128)S(1)}, f32[4,32,768]{2,1,0:T(8,128)S(1)}, u32[]{:S(2)}, u32[]{:S(2)}) collective-permute-start(f32[4,32,768]{2,1,0:T(8,128)S(1)} %get-tuple-element.41), channel_id=1, source_target_pairs={{0,128},{128,256},{256,384},{384,0},{16,400},{144,16},{272,144},{4... | collective-permute-start | bytes 1179656 | tf_op jit(solution)/shard_map/ppermute | solution.py:34
  74.7 2.3 %collective-permute-start.15 = (bf16[16,32,768]{2,1,0:T(8,128)(2,1)S(1)}, bf16[16,32,768]{2,1,0:T(8,128)(2,1)S(1)}, u32[]{:S(2)}, u32[]{:S(2)}) collective-permute-start(bf16[16,32,768]{2,1,0:T(8,128)(2,1)S(1)} %all-to-all-done.act), channel_id=1, source_target_pairs={{0,16},{16,0},{1,17},{17,1},{2,18},{18,2},{3,19},{19,3},{4,20},{20... | collective-permute-start | bytes 2359304 | tf_op jit(solution)/shard_map/ppermute | solution.py:21
  77.0 3.2 %collective-permute-start.12 = (f32[4,32,768]{2,1,0:T(8,128)S(1)}, f32[4,32,768]{2,1,0:T(8,128)S(1)}, u32[]{:S(2)}, u32[]{:S(2)}) collective-permute-start(f32[4,32,768]{2,1,0:T(8,128)S(1)} %get-tuple-element.40), channel_id=1, source_target_pairs={{0,384},{128,0},{256,128},{384,256},{16,144},{144,272},{272,400},{... | collective-permute-start | bytes 1179656 | tf_op jit(solution)/shard_map/ppermute | solution.py:34
  80.2 2.3 %collective-permute-done.13 = f32[4,32,768]{2,1,0:T(8,128)S(1)} collective-permute-done((f32[4,32,768]{2,1,0:T(8,128)S(1)}, f32[4,32,768]{2,1,0:T(8,128)S(1)}, u32[]{:S(2)}, u32[]{:S(2)}) %collective-permute-start.13) | collective-permute-done | bytes 393248 | tf_op jit(solution)/shard_map/ppermute | solution.py:34
  82.5 0.1 fusion.2
  82.6 3.1 %collective-permute-start.14 = (f32[4,32,768]{2,1,0:T(8,128)S(1)}, f32[4,32,768]{2,1,0:T(8,128)S(1)}, u32[]{:S(2)}, u32[]{:S(2)}) collective-permute-start(f32[4,32,768]{2,1,0:T(8,128)S(1)} %fusion.2), channel_id=1, source_target_pairs={{0,128},{128,256},{256,384},{384,0},{16,400},{144,16},{272,144},{4... | collective-permute-start | bytes 1179656 | tf_op jit(solution)/shard_map/ppermute | solution.py:34
  85.7 0.0 collective-permute-done.15.sibling
  85.7 1.0 shard_map.55.turned
  86.7 5.3 %shard_map.56 = bf16[768,1536]{1,0:T(8,128)(2,1)} custom-call(bf16[2,2,768,256]{3,2,1,0:T(8,128)(2,1)S(1)} %shard_map.55.turned, bf16[2,2,32,1536]{3,2,1,0:T(8,128)(2,1)} %bitcast.22, bf16[2,2,32,1536]{3,2,1,0:T(8,128)(2,1)} %collective-permute-done.refs_1_, bf16[2,2,32,1536]{3,2,1,0:T(8,128)(2,1)} %copy-done.2, bf16[2,2,32,1536]{3,2,1,0:T(8,128)(2,1)} %copy-done.3, ...), custom_call_target="tpu_custom_call" | custom-call | flops 2415919104 | bytes 7340032 | tf_op jit(solution)/shard_map/pallas_call | solution.py:130
  92.0 0.2 collective-permute-done.14
  92.2 0.1 fusion.6
  92.3 20.0 %all_to_all.10 = f32[4,32,768]{2,1,0:T(8,128)S(1)} all-to-all(f32[4,32,768]{2,1,0:T(8,128)S(1)} %fusion.6), channel_id=1, replica_groups=mesh['x'=4,'yh'=4,'core'=2,'yl'=2,'z'=8] {'yh'}, dimensions={0} | all-to-all | bytes 786432 | tf_op jit(solution)/shard_map/all_to_all | solution.py:176
  112.3 0.6 reduce_sum.9
  (10 shorter events, 0.0 us)
Async XLA Ops:
  8.2 34.4 %copy-start.1 = (bf16[128,1536]{1,0:T(8,128)(2,1)}, bf16[128,1536]{1,0:T(8,128)(2,1)S(1)}, u32[]{:S(2)}) copy-start(bf16[128,1536]{1,0:T(8,128)(2,1)S(1)} %all_gather.3) | copy-start | bytes 1179652
  8.2 6.2 %collective-permute-start.3 = (bf16[2,2,32,1536]{3,2,1,0:T(8,128)(2,1)S(1)}, bf16[2,2,32,1536]{3,2,1,0:T(8,128)(2,1)S(1)}, u32[]{:S(2)}, u32[]{:S(2)}) collective-permute-start(bf16[2,2,32,1536]{3,2,1,0:T(8,128)(2,1)S(1)} %bitcast.18), channel_id=1, source_target_pairs={{0,16},{16,0},{1,17},{17,1},{2,18},{18,2},{3,19},{19,3},{4,20},{20... | collective-permute-start | bytes 1179656 | tf_op jit(solution)/shard_map/ppermute | solution.py:21
  10.2 20.4 %collective-permute-start = (bf16[2,2,32,1536]{3,2,1,0:T(8,128)(2,1)S(1)}, bf16[2,2,32,1536]{3,2,1,0:T(8,128)(2,1)}, u32[]{:S(2)}, u32[]{:S(2)}) collective-permute-start(bf16[2,2,32,1536]{3,2,1,0:T(8,128)(2,1)S(1)} %bitcast.19), channel_id=1, source_target_pairs={{0,1},{1,2},{2,3},{3,4},{4,5},{5,6},{6,7},{7,0},{16,23},{17,16},{1... | collective-permute-start | bytes 1179656 | tf_op jit(solution)/shard_map/ppermute | solution.py:32
  14.4 20.4 %collective-permute-start.4 = (bf16[2,2,32,1536]{3,2,1,0:T(8,128)(2,1)S(1)}, bf16[2,2,32,1536]{3,2,1,0:T(8,128)(2,1)}, u32[]{:S(2)}, u32[]{:S(2)}) collective-permute-start(bf16[2,2,32,1536]{3,2,1,0:T(8,128)(2,1)S(1)} %collective-permute-done.3), channel_id=1, source_target_pairs={{0,1},{1,2},{2,3},{3,4},{4,5},{5,6},{6,7},{7,0},{16,23},{17,16},{1... | collective-permute-start | bytes 1179656 | tf_op jit(solution)/shard_map/ppermute | solution.py:32
  20.5 41.8 %all-to-all-start = ((bf16[16,32,768]{2,1,0:T(8,128)(2,1)}), bf16[16,32,768]{2,1,0:T(8,128)(2,1)S(1)}, u32[]{:S(2)}, u32[]{:S(2)}) async-start(bf16[16,32,768]{2,1,0:T(8,128)(2,1)} %shard_map.51), calls=%async_computation | async-start | bytes 1572864 | tf_op jit(solution)/shard_map/all_to_all | solution.py:149
  30.5 12.2 %collective-permute-start.1 = (bf16[2,2,32,1536]{3,2,1,0:T(8,128)(2,1)}, bf16[2,2,32,1536]{3,2,1,0:T(8,128)(2,1)S(1)}, u32[]{:S(2)}, u32[]{:S(2)}) collective-permute-start(bf16[2,2,32,1536]{3,2,1,0:T(8,128)(2,1)} %collective-permute-done.refs_1_), channel_id=1, source_target_pairs={{0,1},{1,2},{2,3},{3,4},{4,5},{5,6},{6,7},{7,0},{16,23},{17,16},{1... | collective-permute-start | bytes 1179656 | tf_op jit(solution)/shard_map/ppermute | solution.py:32
  34.8 14.3 %collective-permute-start.7 = (bf16[2,2,32,1536]{3,2,1,0:T(8,128)(2,1)}, bf16[2,2,32,1536]{3,2,1,0:T(8,128)(2,1)}, u32[]{:S(2)}, u32[]{:S(2)}) collective-permute-start(bf16[2,2,32,1536]{3,2,1,0:T(8,128)(2,1)} %collective-permute-done.4), channel_id=1, source_target_pairs={{0,1},{1,2},{2,3},{3,4},{4,5},{5,6},{6,7},{7,0},{16,23},{17,16},{1... | collective-permute-start | bytes 1179656 | tf_op jit(solution)/shard_map/ppermute | solution.py:32
  40.3 1.7 %copy-start = (bf16[768,1536]{1,0:T(8,128)(2,1)S(1)}, bf16[768,1536]{1,0:T(8,128)(2,1)}, u32[]{:S(2)}) copy-start(bf16[768,1536]{1,0:T(8,128)(2,1)} %weight.1) | copy-start | bytes 7077892
  42.8 17.5 %copy-start.2 = (bf16[2,2,32,1536]{3,2,1,0:T(8,128)(2,1)}, bf16[2,2,32,1536]{3,2,1,0:T(8,128)(2,1)S(1)}, u32[]{:S(2)}) copy-start(bf16[2,2,32,1536]{3,2,1,0:T(8,128)(2,1)S(1)} %collective-permute-done.1.refs_2_) | copy-start | bytes 1179652
  42.8 11.3 %collective-permute-start.2 = (bf16[2,2,32,1536]{3,2,1,0:T(8,128)(2,1)S(1)}, bf16[2,2,32,1536]{3,2,1,0:T(8,128)(2,1)S(1)}, u32[]{:S(2)}, u32[]{:S(2)}) collective-permute-start(bf16[2,2,32,1536]{3,2,1,0:T(8,128)(2,1)S(1)} %collective-permute-done.1.refs_2_), channel_id=1, source_target_pairs={{0,1},{1,2},{2,3},{3,4},{4,5},{5,6},{6,7},{7,0},{16,23},{17,16},{1... | collective-permute-start | bytes 1179656 | tf_op jit(solution)/shard_map/ppermute | solution.py:32
  46.1 8.0 %collective-permute-start.5 = (bf16[2,2,32,1536]{3,2,1,0:T(8,128)(2,1)}, bf16[2,2,32,1536]{3,2,1,0:T(8,128)(2,1)S(1)}, u32[]{:S(2)}, u32[]{:S(2)}) collective-permute-start(bf16[2,2,32,1536]{3,2,1,0:T(8,128)(2,1)} %collective-permute-done.4), channel_id=1, source_target_pairs={{0,16},{16,0},{1,17},{17,1},{2,18},{18,2},{3,19},{19,3},{4,20},{20... | collective-permute-start | bytes 1179656 | tf_op jit(solution)/shard_map/ppermute | solution.py:21
  49.1 11.2 %collective-permute-start.9 = (bf16[2,2,32,1536]{3,2,1,0:T(8,128)(2,1)}, bf16[2,2,32,1536]{3,2,1,0:T(8,128)(2,1)}, u32[]{:S(2)}, u32[]{:S(2)}) collective-permute-start(bf16[2,2,32,1536]{3,2,1,0:T(8,128)(2,1)} %collective-permute-done.7), channel_id=1, source_target_pairs={{0,1},{1,2},{2,3},{3,4},{4,5},{5,6},{6,7},{7,0},{16,23},{17,16},{1... | collective-permute-start | bytes 1179656 | tf_op jit(solution)/shard_map/ppermute | solution.py:32
  52.1 10.1 %collective-permute-start.8 = (bf16[2,2,32,1536]{3,2,1,0:T(8,128)(2,1)}, bf16[2,2,32,1536]{3,2,1,0:T(8,128)(2,1)}, u32[]{:S(2)}, u32[]{:S(2)}) collective-permute-start(bf16[2,2,32,1536]{3,2,1,0:T(8,128)(2,1)} %collective-permute-done.7), channel_id=1, source_target_pairs={{0,16},{16,0},{1,17},{17,1},{2,18},{18,2},{3,19},{19,3},{4,20},{20... | collective-permute-start | bytes 1179656 | tf_op jit(solution)/shard_map/ppermute | solution.py:21
  54.1 8.2 %copy-start.3 = (bf16[2,2,32,1536]{3,2,1,0:T(8,128)(2,1)}, bf16[2,2,32,1536]{3,2,1,0:T(8,128)(2,1)S(1)}, u32[]{:S(2)}) copy-start(bf16[2,2,32,1536]{3,2,1,0:T(8,128)(2,1)S(1)} %collective-permute-done.2.refs_3_) | copy-start | bytes 1179652
  54.1 6.2 %copy-start.4 = (bf16[2,2,32,1536]{3,2,1,0:T(8,128)(2,1)}, bf16[2,2,32,1536]{3,2,1,0:T(8,128)(2,1)S(1)}, u32[]{:S(2)}) copy-start(bf16[2,2,32,1536]{3,2,1,0:T(8,128)(2,1)S(1)} %collective-permute-done.5.refs_4_.refs_5_) | copy-start | bytes 1179652
  54.1 11.0 %collective-permute-start.6 = (bf16[2,2,32,1536]{3,2,1,0:T(8,128)(2,1)S(1)}, bf16[2,2,32,1536]{3,2,1,0:T(8,128)(2,1)}, u32[]{:S(2)}, u32[]{:S(2)}) collective-permute-start(bf16[2,2,32,1536]{3,2,1,0:T(8,128)(2,1)S(1)} %collective-permute-done.2.refs_3_), channel_id=1, source_target_pairs={{0,1},{1,2},{2,3},{3,4},{4,5},{5,6},{6,7},{7,0},{16,23},{17,16},{1... | collective-permute-start | bytes 1179656 | tf_op jit(solution)/shard_map/ppermute | solution.py:32
  60.3 4.8 %collective-permute-start.10 = (bf16[2,2,32,1536]{3,2,1,0:T(8,128)(2,1)}, bf16[2,2,32,1536]{3,2,1,0:T(8,128)(2,1)}, u32[]{:S(2)}, u32[]{:S(2)}) collective-permute-start(bf16[2,2,32,1536]{3,2,1,0:T(8,128)(2,1)} %collective-permute-done.9), channel_id=1, source_target_pairs={{0,16},{16,0},{1,17},{17,1},{2,18},{18,2},{3,19},{19,3},{4,20},{20... | collective-permute-start | bytes 1179656 | tf_op jit(solution)/shard_map/ppermute | solution.py:21
  66.8 5.5 %collective-permute-start.11 = (f32[4,4,32,768]{3,2,1,0:T(8,128)S(1)}, f32[4,4,32,768]{3,2,1,0:T(8,128)S(1)}, u32[]{:S(2)}, u32[]{:S(2)}) collective-permute-start(f32[4,4,32,768]{3,2,1,0:T(8,128)S(1)} %shard_map.54), channel_id=1, source_target_pairs={{0,16},{16,0},{1,17},{17,1},{2,18},{18,2},{3,19},{19,3},{4,20},{20... | collective-permute-start | bytes 4718600 | tf_op jit(solution)/shard_map/ppermute | solution.py:21
  72.4 10.1 %collective-permute-start.13 = (f32[4,32,768]{2,1,0:T(8,128)S(1)}, f32[4,32,768]{2,1,0:T(8,128)S(1)}, u32[]{:S(2)}, u32[]{:S(2)}) collective-permute-start(f32[4,32,768]{2,1,0:T(8,128)S(1)} %get-tuple-element.41), channel_id=1, source_target_pairs={{0,128},{128,256},{256,384},{384,0},{16,400},{144,16},{272,144},{4... | collective-permute-start | bytes 1179656 | tf_op jit(solution)/shard_map/ppermute | solution.py:34
  74.7 11.0 %collective-permute-start.15 = (bf16[16,32,768]{2,1,0:T(8,128)(2,1)S(1)}, bf16[16,32,768]{2,1,0:T(8,128)(2,1)S(1)}, u32[]{:S(2)}, u32[]{:S(2)}) collective-permute-start(bf16[16,32,768]{2,1,0:T(8,128)(2,1)S(1)} %all-to-all-done.act), channel_id=1, source_target_pairs={{0,16},{16,0},{1,17},{17,1},{2,18},{18,2},{3,19},{19,3},{4,20},{20... | collective-permute-start | bytes 2359304 | tf_op jit(solution)/shard_map/ppermute | solution.py:21
  77.0 15.1 %collective-permute-start.12 = (f32[4,32,768]{2,1,0:T(8,128)S(1)}, f32[4,32,768]{2,1,0:T(8,128)S(1)}, u32[]{:S(2)}, u32[]{:S(2)}) collective-permute-start(f32[4,32,768]{2,1,0:T(8,128)S(1)} %get-tuple-element.40), channel_id=1, source_target_pairs={{0,384},{128,0},{256,128},{384,256},{16,144},{144,272},{272,400},{... | collective-permute-start | bytes 1179656 | tf_op jit(solution)/shard_map/ppermute | solution.py:34
  82.6 9.7 %collective-permute-start.14 = (f32[4,32,768]{2,1,0:T(8,128)S(1)}, f32[4,32,768]{2,1,0:T(8,128)S(1)}, u32[]{:S(2)}, u32[]{:S(2)}) collective-permute-start(f32[4,32,768]{2,1,0:T(8,128)S(1)} %fusion.2), channel_id=1, source_target_pairs={{0,128},{128,256},{256,384},{384,0},{16,400},{144,16},{272,144},{4... | collective-permute-start | bytes 1179656 | tf_op jit(solution)/shard_map/ppermute | solution.py:34
